TPU v7x, 32 devices: a whole 2x2x4 slice. The times are simulated.
32 devices in a mesh: dp: 8 (over z, y), pass: 2 (over x), vocab: 2 (over core).
Axes of the slice: x: 2, y: 2, z: 4, core: 2. Of those that a mesh axis runs over, the one named last changes fastest.
Arguments:
- inputs: bfloat16 [4096, 512], P('dp'), may hold values from -6 to 6
- memory: bfloat16 [8192, 512], P('dp'), may hold values from -6 to 6
- expert_ids: int32 [2, 4096, 1], P('pass', 'dp'), may hold values from 0 to 3; in each aligned block of 512 rows (0 to 511, 512 to 1023, ..., all dimensions but the last counted through in order) at most 256 rows name the same one
- targets: int32 [4096], P('dp'), may hold values from 0 to 31999
- lengths: int32 [8], replicated, may hold values from 128 to 512, as said below
- memory_mask: int32 [8, 1024], P('dp'), may hold values from 0 to 1, as said below
- norm_gain: bfloat16 [4, 512], P(None, ('dp', 'pass')), may hold values from 0.5 to 1.5
- norm_bias: bfloat16 [4, 512], P(None, ('dp', 'pass')), may hold values from -3 to 3
- self_project: bfloat16 [512, 1536], P(None, ('dp', 'pass')), may hold values from -0.25 to 0.25
- self_output: bfloat16 [512, 512], P(None, ('dp', 'pass')), may hold values from -1 to 1
- cross_query: bfloat16 [512, 512], P(None, ('dp', 'pass')), may hold values from -0.25 to 0.25
- memory_project: bfloat16 [512, 1024], P(None, ('dp', 'pass')), may hold values from -0.25 to 0.25
- cross_output: bfloat16 [512, 512], P(None, ('dp', 'pass')), may hold values from -1 to 1
- expert_in: bfloat16 [4, 512, 2048], P(None, None, ('dp', 'pass')), may hold values from -0.25 to 0.25
- expert_out: bfloat16 [4, 512, 2048], P(None, None, ('dp', 'pass')), may hold values from -0.125 to 0.125
- embedding: bfloat16 [32000, 512], P(('dp', 'pass', 'vocab')), may hold values from -0.5 to 0.5
Outputs:
- block_out: float32 [2, 4096, 512], P('pass', 'dp')
- mean_loss: float32 [], replicated
- inputs_gradient: float32 [4096, 512], P('dp')
- memory_gradient: float32 [8192, 512], P('dp')
- norm_gain_gradient: float32 [4, 512], P(None, ('dp', 'pass'))
- norm_bias_gradient: float32 [4, 512], P(None, ('dp', 'pass'))
- self_project_gradient: float32 [512, 1536], P(None, ('dp', 'pass'))
- self_output_gradient: float32 [512, 512], P(None, ('dp', 'pass'))
- cross_query_gradient: float32 [512, 512], P(None, ('dp', 'pass'))
- memory_project_gradient: float32 [512, 1024], P(None, ('dp', 'pass'))
- cross_output_gradient: float32 [512, 512], P(None, ('dp', 'pass'))
- expert_in_gradient: float32 [4, 512, 2048], P(None, None, ('dp', 'pass'))
- expert_out_gradient: float32 [4, 512, 2048], P(None, None, ('dp', 'pass'))
- embedding_gradient: float32 [32000, 512], P(('dp', 'pass', 'vocab'))
Inputs may be any that keep to these rules, and one draw needn't show every extreme that they name: `expert_ids`: in each pass no expert is named by more than 256 tokens of one row, and some row reaches 256. `lengths`: some row has all 512 slots valid. `memory_mask`: the first memory position of every row is 1.
All inputs are finite; a program needn't handle non-finite values.
Results may differ from a plain program's by a relative error of at most 0.017.
Values may be sent and summed in bfloat16 or wider, within the bound.
No kernel may reach another device: no remote copies, remote signals or barrier semaphores. Data moves between devices by JAX's collectives and lax.ppermute only.
A program may use at most 192 MiB of HBM per device.

v0:
```python
import jax
import jax.numpy as jnp
from jax import lax
from jax.sharding import PartitionSpec as P

HEADS = 8
VOCAB = 32000


epsilon = 1e-05
smoothing = 0.1
consistency = 1.0
vocab_blocks = 16


def swapped(block, axis, distance):
    count = lax.axis_size(axis)
    route = []
    for low in range(count):
        high = low | 1 << distance
        if high != low and high < count:
            route += [(low, high), (high, low)]
    return lax.ppermute(block, axis, route)


def joined_2(part, axis, combine):
    gathered = jax.tree.map(lambda a: lax.all_gather(a, axis), part)

    def take(source):
        return jax.tree.map(lambda a: lax.dynamic_index_in_dim(a, source, 0, False), gathered)

    return lax.fori_loop(
        1, lax.axis_size(axis), lambda source, state: combine(state, take(source)), take(0)
    )


def normalize(values, norm_gain, norm_bias):
    average = jnp.mean(values, axis=-1, keepdims=True)
    centered = values - average
    variance = jnp.mean(centered * centered, axis=-1, keepdims=True)
    return centered * lax.rsqrt(variance + epsilon) * norm_gain + norm_bias


def norm_back(values, norm_gain, norm_bias, upstream):
    unused, pullback = jax.vjp(normalize, values, norm_gain, norm_bias)
    return pullback(upstream)


def split_heads(matrix):
    return matrix.reshape(matrix.shape[0], HEADS, -1).transpose(1, 0, 2)


def merge_heads(stacked):
    return stacked.transpose(1, 0, 2).reshape(stacked.shape[1], -1)


def attend_forward(queries, keys, values, allowed):
    scaling = queries.shape[-1] ** (-0.5)

    def one_head(parts):
        query_head, key_head, value_head = parts
        scores = (
            jnp.einsum("qd,kd->qk", query_head, key_head, preferred_element_type=jnp.float32)
            * scaling
        )
        scores = jnp.where(allowed, scores, -1e30)
        row_max = jnp.max(scores, axis=-1, keepdims=True)
        numerator = jnp.exp(scores - row_max)
        row_sum = jnp.sum(numerator, axis=-1, keepdims=True)
        prob_low = (numerator / row_sum).astype(jnp.bfloat16)
        mixed = jnp.dot(prob_low, value_head, preferred_element_type=jnp.float32).astype(
            jnp.bfloat16
        )
        return (mixed, (row_max + jnp.log(row_sum))[:, 0])

    return lax.map(one_head, (queries, keys, values))


def attend_backward(queries, keys, values, allowed, log_sums, upstream):
    scaling = queries.shape[-1] ** (-0.5)

    def one_head(parts):
        query_head, key_head, value_head, log_sum, grad_head = parts
        scores = (
            jnp.einsum("qd,kd->qk", query_head, key_head, preferred_element_type=jnp.float32)
            * scaling
        )
        weights = jnp.where(allowed, jnp.exp(scores - log_sum[:, None]), 0.0)
        weight_grad = jnp.einsum(
            "qd,kd->qk", grad_head, value_head, preferred_element_type=jnp.float32
        )
        score_grad = (
            weights * (weight_grad - jnp.sum(weights * weight_grad, axis=-1, keepdims=True))
        ).astype(jnp.bfloat16)
        query_grad = (
            jnp.dot(score_grad, key_head, preferred_element_type=jnp.float32) * scaling
        ).astype(jnp.bfloat16)
        key_grad = (
            jnp.einsum("qk,qd->kd", score_grad, query_head, preferred_element_type=jnp.float32)
            * scaling
        ).astype(jnp.bfloat16)
        value_grad = jnp.einsum(
            "qk,qd->kd", weights.astype(jnp.bfloat16), grad_head, preferred_element_type=jnp.float32
        ).astype(jnp.bfloat16)
        return (query_grad, key_grad, value_grad)

    return lax.map(one_head, (queries, keys, values, log_sums, upstream))


def expert_forward(dispatched, weight_in, weight_out):
    pre_act = jnp.einsum("ecd,edf->ecf", dispatched, weight_in, preferred_element_type=jnp.float32)
    activation = jax.nn.gelu(pre_act).astype(jnp.bfloat16)
    return jnp.einsum("ecf,edf->ecd", activation, weight_out, preferred_element_type=jnp.float32)


def online_stats(mine, theirs):
    mine_max = jnp.max(mine, axis=1)
    mine_exp = jnp.exp(mine - mine_max[:, None])
    their_max = jnp.max(theirs, axis=1)
    their_exp = jnp.exp(theirs - their_max[:, None])
    return (
        mine_max,
        jnp.sum(mine_exp, axis=1),
        jnp.sum(mine_exp * mine, axis=1),
        jnp.sum(mine_exp * theirs, axis=1),
        their_max,
        jnp.sum(their_exp, axis=1),
        jnp.sum(their_exp * theirs, axis=1),
        jnp.sum(their_exp * mine, axis=1),
    )


def rescale(left, right):
    joined = jnp.maximum(left[0], right[0])
    left_factor = jnp.exp(left[0] - joined)
    right_factor = jnp.exp(right[0] - joined)
    return (joined,) + tuple(
        (left[entry] * left_factor + right[entry] * right_factor for entry in range(1, 4))
    )


def combine_stats(left, right):
    totals = tuple((left[entry] + right[entry] for entry in range(8, len(left))))
    return rescale(left[0:4], right[0:4]) + rescale(left[4:8], right[4:8]) + totals


def logit_gradient(mine, theirs, lse_mine, lse_theirs, drift_mine, target_hit, weight_rows):
    prob_mine = jnp.exp(mine - lse_mine[:, None])
    prob_theirs = jnp.exp(theirs - lse_theirs[:, None])
    raw = (
        prob_mine * (1.0 + consistency * (1.0 + mine - theirs - drift_mine[:, None]))
        - consistency * prob_theirs
        - (1.0 - smoothing) * target_hit
        - smoothing / VOCAB
    )
    return (raw * weight_rows[:, None]).astype(jnp.bfloat16)


def local(
    inputs,
    memory,
    expert_ids,
    targets,
    lengths,
    memory_mask,
    norm_gain,
    norm_bias,
    self_project,
    self_output,
    cross_query,
    memory_project,
    cross_output,
    expert_in,
    expert_out,
    embedding,
):
    seq_len, model_width = inputs.shape
    tokens = inputs.astype(jnp.float32)
    routes = expert_ids[0, :, 0]
    positions = jnp.arange(seq_len)
    valid_mask = (positions < lengths[lax.axis_index("dp")]).astype(jnp.float32)
    token_count = jnp.sum(lengths).astype(jnp.float32)
    causal = positions[None, :] <= positions[:, None]
    visible = jnp.broadcast_to(memory_mask[0][None, :] == 1, (seq_len, memory.shape[0]))
    gathered = (
        lax.all_gather(norm_gain, ("dp", "pass"), axis=1, tiled=True),
        lax.all_gather(norm_bias, ("dp", "pass"), axis=1, tiled=True),
        lax.all_gather(self_project, ("dp", "pass"), axis=1, tiled=True),
        lax.all_gather(self_output, ("dp", "pass"), axis=1, tiled=True),
        lax.all_gather(cross_query, ("dp", "pass"), axis=1, tiled=True),
        lax.all_gather(memory_project, ("dp", "pass"), axis=1, tiled=True),
        lax.all_gather(cross_output, ("dp", "pass"), axis=1, tiled=True),
    )
    norm_gains = gathered[0].astype(jnp.float32)
    biases = gathered[1].astype(jnp.float32)
    normed_one = normalize(tokens, norm_gains[0], biases[0]).astype(jnp.bfloat16)
    projected = jnp.dot(normed_one, gathered[2], preferred_element_type=jnp.float32).astype(
        jnp.bfloat16
    )
    self_heads = (
        split_heads(projected[:, :model_width]),
        split_heads(projected[:, model_width : 2 * model_width]),
        split_heads(projected[:, 2 * model_width :]),
    )
    self_mixed, self_sums = attend_forward(self_heads[0], self_heads[1], self_heads[2], causal)
    self_attended = merge_heads(self_mixed)
    hidden_one = tokens + jnp.dot(self_attended, gathered[3], preferred_element_type=jnp.float32)
    normed_two = normalize(hidden_one, norm_gains[1], biases[1]).astype(jnp.bfloat16)
    cross_heads = split_heads(
        jnp.dot(normed_two, gathered[4], preferred_element_type=jnp.float32).astype(jnp.bfloat16)
    )
    keyval = jnp.dot(memory, gathered[5], preferred_element_type=jnp.float32).astype(jnp.bfloat16)
    memory_heads = (split_heads(keyval[:, :model_width]), split_heads(keyval[:, model_width:]))
    cross_mixed, cross_sums = attend_forward(cross_heads, memory_heads[0], memory_heads[1], visible)
    cross_attended = merge_heads(cross_mixed)
    hidden_two = hidden_one + jnp.dot(
        cross_attended, gathered[6], preferred_element_type=jnp.float32
    )
    normed_three = normalize(hidden_two, norm_gains[2], biases[2]).astype(jnp.bfloat16)
    expert_count = expert_in.shape[0]
    capacity = 2 * seq_len // expert_count
    onehot = (routes[:, None] == jnp.arange(expert_count)[None, :]).astype(jnp.int32)
    slot_rank = jnp.sum((jnp.cumsum(onehot, axis=0) - 1) * onehot, axis=1)
    slot_index = routes * capacity + slot_rank
    dispatched = (
        jnp.zeros((expert_count * capacity, model_width), jnp.bfloat16)
        .at[slot_index]
        .set(normed_three)
        .reshape(expert_count, capacity, model_width)
    )
    expert_result = expert_forward(
        dispatched,
        lax.all_gather(expert_in, ("dp", "pass"), axis=2, tiled=True),
        lax.all_gather(expert_out, ("dp", "pass"), axis=2, tiled=True),
    )
    block_result = hidden_two + expert_result.reshape(-1, model_width)[slot_index]
    final_normed = normalize(block_result, norm_gains[3], biases[3]).astype(jnp.bfloat16)
    other_normed = swapped(final_normed, "pass", 0)
    shard_rows = embedding.shape[0]
    owner_block = targets // shard_rows
    lowest = jnp.full((seq_len,), -1e30, jnp.float32)
    zeros = jnp.zeros((seq_len,), jnp.float32)
    half_weight = 0.5 * valid_mask
    vocab_part = lax.all_gather(embedding, ("dp", "pass"), axis=0, tiled=True)
    vocab_ways = lax.axis_size("vocab")
    own_part = lax.axis_index("vocab")
    target_column = owner_block // vocab_ways * shard_rows + targets % shard_rows
    target_column = jnp.where(owner_block % vocab_ways == own_part, target_column, -1)
    block_rows = vocab_part.shape[0] // vocab_blocks
    vocab_stack = vocab_part.reshape(vocab_blocks, block_rows, model_width)
    block_starts = jnp.arange(vocab_blocks) * block_rows

    def block_logits(rows_block):
        mine = jnp.einsum("td,vd->tv", final_normed, rows_block, preferred_element_type=jnp.float32)
        theirs = jnp.einsum(
            "td,vd->tv", other_normed, rows_block, preferred_element_type=jnp.float32
        )
        return (mine, theirs)

    def first_sweep(carry, block_pair):
        rows_block, start = block_pair
        mine, theirs = block_logits(rows_block)
        target_hit = (start + jnp.arange(block_rows))[None, :] == target_column[:, None]
        stats = online_stats(mine, theirs) + (
            jnp.sum(jnp.where(target_hit, mine, 0.0), axis=1),
            jnp.sum(mine, axis=1),
        )
        return (combine_stats(carry, stats), None)

    initial = (lowest, zeros, zeros, zeros, lowest, zeros, zeros, zeros, zeros, zeros)
    local_stats, unused = lax.scan(first_sweep, initial, (vocab_stack, block_starts))
    merged = joined_2(local_stats, "vocab", combine_stats)
    lse_mine = merged[0] + jnp.log(merged[1])
    lse_theirs = merged[4] + jnp.log(merged[5])
    drift_mine = (merged[2] - merged[3]) / merged[1]
    drift_theirs = (merged[6] - merged[7]) / merged[5]
    cross_entropy = lse_mine - (1.0 - smoothing) * merged[8] - smoothing / VOCAB * merged[9]
    partial_loss = jnp.sum(
        valid_mask * (0.5 * cross_entropy + 0.25 * consistency * (drift_mine + drift_theirs))
    )

    def second_sweep(carry, block_pair):
        rows_block, start = block_pair
        mine, theirs = block_logits(rows_block)
        target_hit = ((start + jnp.arange(block_rows))[None, :] == target_column[:, None]).astype(
            jnp.float32
        )
        grad_low = logit_gradient(
            mine, theirs, lse_mine, lse_theirs, drift_mine, target_hit, half_weight
        )
        carry = carry + jnp.dot(grad_low, rows_block, preferred_element_type=jnp.float32)
        return (
            carry,
            jnp.einsum("tv,td->vd", grad_low, final_normed, preferred_element_type=jnp.float32),
        )

    hidden_part, block_grads = lax.scan(
        second_sweep, jnp.zeros((seq_len, model_width), jnp.float32), (vocab_stack, block_starts)
    )
    final_grad = lax.psum(hidden_part.astype(jnp.bfloat16), "vocab").astype(jnp.float32)
    embedding_grad = lax.psum_scatter(
        block_grads.reshape(-1, model_width), ("dp", "pass"), scatter_dimension=0, tiled=True
    )
    mean_loss = lax.psum(partial_loss, ("dp", "pass")) / token_count
    matrices = (
        lax.all_gather(self_project, ("dp", "pass"), axis=1, tiled=True),
        lax.all_gather(self_output, ("dp", "pass"), axis=1, tiled=True),
        lax.all_gather(cross_query, ("dp", "pass"), axis=1, tiled=True),
        lax.all_gather(memory_project, ("dp", "pass"), axis=1, tiled=True),
        lax.all_gather(cross_output, ("dp", "pass"), axis=1, tiled=True),
    )
    expert_back = (
        lax.all_gather(expert_in, ("dp", "pass"), axis=2, tiled=True),
        lax.all_gather(expert_out, ("dp", "pass"), axis=2, tiled=True),
    )
    block_grad, gain_three, bias_three = norm_back(
        block_result, norm_gains[3], biases[3], final_grad
    )
    grad_dispatched = (
        jnp.zeros((expert_count * capacity, model_width), jnp.bfloat16)
        .at[slot_index]
        .set(block_grad.astype(jnp.bfloat16))
        .reshape(expert_count, capacity, model_width)
    )
    pre_act = jnp.einsum(
        "ecd,edf->ecf", dispatched, expert_back[0], preferred_element_type=jnp.float32
    )
    activation, gelu_pull = jax.vjp(jax.nn.gelu, pre_act)
    act_grad = jnp.einsum(
        "ecd,edf->ecf", grad_dispatched, expert_back[1], preferred_element_type=jnp.float32
    )
    pre_grad = gelu_pull(act_grad)[0].astype(jnp.bfloat16)
    expert_in_grad = jnp.einsum(
        "ecd,ecf->edf", dispatched, pre_grad, preferred_element_type=jnp.float32
    )
    expert_out_grad = jnp.einsum(
        "ecd,ecf->edf",
        grad_dispatched,
        activation.astype(jnp.bfloat16),
        preferred_element_type=jnp.float32,
    )
    slot_grad = jnp.einsum(
        "ecf,edf->ecd", pre_grad, expert_back[0], preferred_element_type=jnp.float32
    ).reshape(-1, model_width)
    two_grad, gain_two, bias_two = norm_back(
        hidden_two, norm_gains[2], biases[2], slot_grad[slot_index]
    )
    hidden_two_grad = block_grad + two_grad
    cross_low = hidden_two_grad.astype(jnp.bfloat16)
    cross_output_grad = jnp.einsum(
        "sd,se->de", cross_attended, cross_low, preferred_element_type=jnp.float32
    )
    cross_upstream = jnp.einsum(
        "se,de->sd", cross_low, matrices[4], preferred_element_type=jnp.float32
    ).astype(jnp.bfloat16)
    query_grad, key_grad, value_grad = attend_backward(
        cross_heads,
        memory_heads[0],
        memory_heads[1],
        visible,
        cross_sums,
        split_heads(cross_upstream),
    )
    query_low = merge_heads(query_grad)
    cross_query_grad = jnp.einsum(
        "sd,se->de", normed_two, query_low, preferred_element_type=jnp.float32
    )
    pair_grad = jnp.concatenate([merge_heads(key_grad), merge_heads(value_grad)], axis=1)
    memory_project_grad = jnp.einsum(
        "md,me->de", memory, pair_grad, preferred_element_type=jnp.float32
    )
    memory_local = jnp.einsum(
        "me,de->md", pair_grad, matrices[3], preferred_element_type=jnp.float32
    )
    normed_two_grad = jnp.einsum(
        "se,de->sd", query_low, matrices[2], preferred_element_type=jnp.float32
    )
    one_grad, gain_one, bias_one = norm_back(hidden_one, norm_gains[1], biases[1], normed_two_grad)
    hidden_one_grad = hidden_two_grad + one_grad
    self_low = hidden_one_grad.astype(jnp.bfloat16)
    self_output_grad = jnp.einsum(
        "sd,se->de", self_attended, self_low, preferred_element_type=jnp.float32
    )
    self_upstream = jnp.einsum(
        "se,de->sd", self_low, matrices[1], preferred_element_type=jnp.float32
    ).astype(jnp.bfloat16)
    self_query_grad, self_key_grad, self_value_grad = attend_backward(
        self_heads[0], self_heads[1], self_heads[2], causal, self_sums, split_heads(self_upstream)
    )
    project_low = jnp.concatenate(
        [merge_heads(self_query_grad), merge_heads(self_key_grad), merge_heads(self_value_grad)],
        axis=1,
    )
    self_project_grad = jnp.einsum(
        "sd,se->de", normed_one, project_low, preferred_element_type=jnp.float32
    )
    normed_one_grad = jnp.einsum(
        "se,de->sd", project_low, matrices[0], preferred_element_type=jnp.float32
    )
    zero_grad, gain_zero, bias_zero = norm_back(tokens, norm_gains[0], biases[0], normed_one_grad)
    inputs_local = hidden_one_grad + zero_grad
    gain_grads = jnp.stack([gain_zero, gain_one, gain_two, gain_three])
    bias_grads = jnp.stack([bias_zero, bias_one, bias_two, bias_three])
    layer_grads = (
        lax.psum_scatter(gain_grads, ("dp", "pass"), scatter_dimension=1, tiled=True),
        lax.psum_scatter(bias_grads, ("dp", "pass"), scatter_dimension=1, tiled=True),
        lax.psum_scatter(self_project_grad, ("dp", "pass"), scatter_dimension=1, tiled=True),
        lax.psum_scatter(self_output_grad, ("dp", "pass"), scatter_dimension=1, tiled=True),
        lax.psum_scatter(cross_query_grad, ("dp", "pass"), scatter_dimension=1, tiled=True),
        lax.psum_scatter(memory_project_grad, ("dp", "pass"), scatter_dimension=1, tiled=True),
        lax.psum_scatter(cross_output_grad, ("dp", "pass"), scatter_dimension=1, tiled=True),
    )
    expert_grads = (
        lax.psum_scatter(expert_in_grad, ("dp", "pass"), scatter_dimension=2, tiled=True),
        lax.psum_scatter(expert_out_grad, ("dp", "pass"), scatter_dimension=2, tiled=True),
    )
    inputs_grad, memory_grad = (
        lax.psum(inputs_local.astype(jnp.bfloat16), "pass").astype(jnp.float32),
        lax.psum(memory_local.astype(jnp.bfloat16), "pass").astype(jnp.float32),
    )
    return (
        block_result[None],
        mean_loss,
        inputs_grad,
        memory_grad,
        layer_grads[0],
        layer_grads[1],
        layer_grads[2],
        layer_grads[3],
        layer_grads[4],
        layer_grads[5],
        layer_grads[6],
        expert_grads[0],
        expert_grads[1],
        embedding_grad,
    )


def solution(mesh):
    placed = (
        P("dp", None),
        P("dp", None),
        P("pass", "dp", None),
        P("dp"),
        P(),
        P("dp", None),
        P(None, ("dp", "pass")),
        P(None, ("dp", "pass")),
        P(None, ("dp", "pass")),
        P(None, ("dp", "pass")),
        P(None, ("dp", "pass")),
        P(None, ("dp", "pass")),
        P(None, ("dp", "pass")),
        P(None, None, ("dp", "pass")),
        P(None, None, ("dp", "pass")),
        P(("dp", "pass", "vocab"), None),
    )
    return jax.shard_map(
        local,
        mesh=mesh,
        in_specs=placed,
        out_specs=(
            P("pass", "dp", None),
            P(),
            P("dp", None),
            P("dp", None),
            P(None, ("dp", "pass")),
            P(None, ("dp", "pass")),
            P(None, ("dp", "pass")),
            P(None, ("dp", "pass")),
            P(None, ("dp", "pass")),
            P(None, ("dp", "pass")),
            P(None, ("dp", "pass")),
            P(None, None, ("dp", "pass")),
            P(None, None, ("dp", "pass")),
            P(("dp", "pass", "vocab"), None),
        ),
        check_vma=False,
    )
```

profile of v0, /device:TPU:0, one launch (start us, length us, event | category | flops | bytes accessed | tf_op | source)
XLA Modules:
  0.0 3228.2 jit_solution(968529956330734914)
XLA Ops:
  11.0 42.4 %all-gather.10 = bf16[16,32,4]{1,2,0:T(4,128)(2,1)S(1)} all-gather(bf16[1,32,4]{1,2,0:T(4,128)(2,1)S(1)} %bitcast.562), channel_id=1, replica_groups=mesh['dp'=8,'pass'=2,'vocab'=2] {'dp','pass'}, dimensions={0}, use_global_device_ids=true | all-gather | bytes 4352 | tf_op jit(solution)/shard_map/all_gather | solution.py:186
  53.5 35.6 %all-gather.11 = bf16[16,32,4]{1,2,0:T(4,128)(2,1)S(1)} all-gather(bf16[1,32,4]{1,2,0:T(4,128)(2,1)S(1)} %bitcast.563), channel_id=1, replica_groups=mesh['dp'=8,'pass'=2,'vocab'=2] {'dp','pass'}, dimensions={0}, use_global_device_ids=true | all-gather | bytes 4352 | tf_op jit(solution)/shard_map/all_gather | solution.py:187
  92.0 42.5 %all_gather.100 = bf16[512,512]{0,1:T(8,128)(2,1)S(1)} all-gather(bf16[512,32]{0,1:T(8,128)(2,1)S(1)} %copy-done.53), channel_id=1, replica_groups=mesh['dp'=8,'pass'=2,'vocab'=2] {'dp','pass'}, dimensions={1}, use_global_device_ids=true | all-gather | bytes 557056 | tf_op jit(solution)/shard_map/all_gather | solution.py:189
  134.5 42.8 %all_gather.101 = bf16[512,512]{0,1:T(8,128)(2,1)} all-gather(bf16[512,32]{0,1:T(8,128)(2,1)S(1)} %copy-done.54), channel_id=1, replica_groups=mesh['dp'=8,'pass'=2,'vocab'=2] {'dp','pass'}, dimensions={1}, use_global_device_ids=true | all-gather | bytes 557056 | tf_op jit(solution)/shard_map/all_gather | solution.py:190
  177.3 46.5 %all_gather.103 = bf16[512,512]{0,1:T(8,128)(2,1)} all-gather(bf16[512,32]{0,1:T(8,128)(2,1)S(1)} %copy-done.55), channel_id=1, replica_groups=mesh['dp'=8,'pass'=2,'vocab'=2] {'dp','pass'}, dimensions={1}, use_global_device_ids=true | all-gather | bytes 557056 | tf_op jit(solution)/shard_map/all_gather | solution.py:192
  243.4 27.4 while.114
  275.4 35.8 %while.115 = (s32[]{:T(128)}, bf16[8,512,64]{1,2,0:T(8,128)(2,1)}, f32[8,512]{1,0:T(8,128)S(1)}, bf16[8,512,64]{2,1,0:T(8,128)(2,1)}, bf16[8,1024,64]{2,1,0:T(8,...) while((s32[]{:T(128)}, bf16[8,512,64]{1,2,0:T(8,128)(2,1)}, ...), condition=%wide.region_11.12_spmd.clone, body=%wide.region_8.11_spmd.clone.sunk | while | flops 140541440 | bytes 7038049 | solution.py:76
  318.2 9.3 fusion.221
  327.5 98.8 %all-gather.34.cloned.1.call-done = bf16[4,512,2048]{2,1,0:T(8,128)(2,1)} async-done(((bf16[4,512,128]{2,1,0:T(8,128)(2,1)}), bf16[4,512,2048]{2,1,0:T(8,128)(2,1)}) %all-gather.34.cloned.1.call-update) | async-done | bytes 8388624 | tf_op jit(solution)/shard_map/all_gather | solution.py:234
  426.3 10.2 fusion.199
  436.4 3.9 gather_fusion
  445.8 11.6 collective-permute-done
  458.6 156.4 %all-gather.36.cloned.1.call-done = bf16[16000,512]{1,0:T(8,128)(2,1)} async-done(((bf16[1000,512]{1,0:T(8,128)(2,1)}), bf16[16000,512]{1,0:T(8,128)(2,1)}) %all-gather.36.cloned.1.call-update) | async-done | bytes 16384016 | tf_op jit(solution)/shard_map/all_gather | solution.py:244
  615.0 112.9 %while.118 = (s32[]{:T(128)}, f32[512]{0:T(512)S(1)}, f32[512]{0:T(512)S(1)}, f32[512]{0:T(512)S(1)}, f32[512]{0:T(512)S(1)}, /*index=5*/f32[512]{0:T(512)S(1)},...) while((s32[]{:T(128)}, f32[512]{0:T(512)S(1)}, ...), condition=%wide.region_31.32_spmd.clone, body=%wide.region_20.31_spmd.clone.sunk | while | flops 1057809408 | bytes 11406338 | solution.py:271
  749.5 210.8 %while.119 = (s32[]{:T(128)}, f32[512,512]{1,0:T(8,128)}, f32[16,1000,512]{2,1,0:T(8,128)}, bf16[16,1000,512]{2,1,0:T(8,128)(2,1)}, bf16[512,512]{1,0:T(8,128)(2...) while((s32[]{:T(128)}, f32[512,512]{1,0:T(8,128)}, ...), condition=%wide.region_36.37_spmd.clone, body=%wide.region_35.36_spmd.clone.sunk | while | flops 2104846336 | bytes 20076544 | solution.py:297
  798.3 3.5 convolution_add_fusion.3
  824.8 3.5 convolution_add_fusion.3
  838.0 3.5 convolution_add_fusion.3
  851.1 3.5 convolution_add_fusion.3
  864.3 3.5 convolution_add_fusion.3
  877.5 3.5 convolution_add_fusion.3
  890.7 3.5 convolution_add_fusion.3
  930.3 3.5 convolution_add_fusion.3
  943.6 3.5 convolution_add_fusion.3
  956.8 3.5 convolution_add_fusion.3
  962.6 17.0 all-reduce.4.cloned.1.call-done
  987.5 10.9 fusion.146
  998.5 8.7 fusion.222
  1007.2 4.3 gather_fusion.1
  1020.6 75.1 %while.116 = (s32[]{:T(128)}, bf16[8,512,64]{1,2,0:T(8,128)(2,1)}, bf16[8,1024,64]{1,2,0:T(8,128)(2,1)}, bf16[8,1024,64]{1,2,0:T(8,128)(2,1)}, bf16[8,512,64]{2,...) while((s32[]{:T(128)}, bf16[8,512,64]{1,2,0:T(8,128)(2,1)}, ...), condition=%wide.region_45.46_spmd.clone, body=%wide.region_43.45_spmd.clone.sunk | while | flops 340524544 | bytes 17383536 | solution.py:107
  1110.7 72.3 %while.117 = (s32[]{:T(128)}, bf16[8,512,64]{1,2,0:T(8,128)(2,1)}, bf16[8,512,64]{1,2,0:T(8,128)(2,1)}, bf16[8,512,64]{1,2,0:T(8,128)(2,1)}, bf16[8,512,64]{2,1,...) while((s32[]{:T(128)}, bf16[8,512,64]{1,2,0:T(8,128)(2,1)}, ...), condition=%wide.region_50.51_spmd.clone, body=%wide.region_48.50_spmd.clone.sunk | while | flops 170556928 | bytes 8993897 | solution.py:107
  1184.3 3.9 fusion.220
  1194.8 4.3 convolution_convert_fusion.6
  1207.7 4.1 convolution_bitcast_fusion
  1213.1 4.1 fusion.162
  1218.4 12.5 fusion.198
  1232.1 10.3 fusion.224
  1245.8 42.6 %psum.28 = f32[]{:T(128)} all-reduce(f32[]{:T(128)} %get-tuple-element.1054), channel_id=1, replica_groups=mesh['dp'=8,'pass'=2,'vocab'=2] {'dp','pass'}, use_global_device_ids=true, to_apply=%region_33.34 | all-reduce | flops 1 | bytes 8 | tf_op jit(solution)/shard_map/psum | solution.py:304
  1290.4 50.8 %reduce-scatter.31.cloned.1.call-done = f32[32,4]{1,0:T(8,128)} async-done(((f32[512,4]{1,0:T(8,128)}), f32[32,4]{1,0:T(8,128)}) %reduce-scatter.31.cloned.1.call-update) | async-done | bytes 528
  1342.6 49.7 %all-reduce.6.cloned.1.call-done = (bf16[512,512]{0,1:T(8,128)(2,1)}, bf16[1024,512]{1,0:T(8,128)(2,1)}) async-done(((bf16[512,512]{0,1:T(8,128)(2,1)}, bf16[1024,512]{1,0:T(8,128)(2,1)}), (bf16[512,512]{0,1:T(8,128)(2,1)}, bf16[1024,512]{1,0:T(8,128)(2,1)})) %all-reduce.6.cloned.1.call-update) | async-done | bytes 1572880 | tf_op jit(solution)/shard_map/psum | solution.py:418
  1396.3 76.5 %reduce-scatter.19.cloned.1.call-done = f32[512,32]{0,1:T(8,128)} async-done(((f32[512,512]{0,1:T(8,128)}), f32[512,32]{0,1:T(8,128)}) %reduce-scatter.19.cloned.1.call-update) | async-done | bytes 65552 | tf_op jit(solution)/shard_map/reduce_scatter | solution.py:409
  1472.8 77.0 %reduce-scatter.23.cloned.1.call-done = f32[512,32]{0,1:T(8,128)} async-done(((f32[512,512]{0,1:T(8,128)}), f32[512,32]{0,1:T(8,128)}) %reduce-scatter.23.cloned.1.call-update) | async-done | bytes 65552 | tf_op jit(solution)/shard_map/reduce_scatter | solution.py:411
  1549.8 77.0 %reduce-scatter.17.cloned.1.call-done = f32[512,32]{0,1:T(8,128)} async-done(((f32[512,512]{0,1:T(8,128)}), f32[512,32]{0,1:T(8,128)}) %reduce-scatter.17.cloned.1.call-update) | async-done | bytes 65552 | tf_op jit(solution)/shard_map/reduce_scatter | solution.py:408
  1626.8 80.0 %reduce-scatter.21.cloned.1.call-done = f32[512,64]{0,1:T(8,128)} async-done(((f32[512,1024]{0,1:T(8,128)}), f32[512,64]{0,1:T(8,128)}) %reduce-scatter.21.cloned.1.call-update) | async-done | bytes 131088 | tf_op jit(solution)/shard_map/reduce_scatter | solution.py:410
  1706.8 133.8 %reduce-scatter.15.cloned.1.call-done = f32[512,96]{0,1:T(8,128)} async-done(((f32[512,1536]{0,1:T(8,128)}), f32[512,96]{0,1:T(8,128)}) %reduce-scatter.15.cloned.1.call-update) | async-done | bytes 196624 | tf_op jit(solution)/shard_map/reduce_scatter | solution.py:407
  1840.6 348.5 %reduce-scatter.27.cloned.1.call-done = f32[4,512,128]{2,1,0:T(8,128)} async-done(((f32[4,512,2048]{2,1,0:T(8,128)}), f32[4,512,128]{2,1,0:T(8,128)}) %reduce-scatter.27.cloned.1.call-update) | async-done | bytes 1048592 | tf_op jit(solution)/shard_map/reduce_scatter | solution.py:415
  2189.1 354.9 %reduce-scatter.25.cloned.1.call-done = f32[4,512,128]{2,1,0:T(8,128)} async-done(((f32[4,512,2048]{2,1,0:T(8,128)}), f32[4,512,128]{2,1,0:T(8,128)}) %reduce-scatter.25.cloned.1.call-update) | async-done | bytes 1048592 | tf_op jit(solution)/shard_map/reduce_scatter | solution.py:414
  2543.9 676.2 %reduce-scatter.29.cloned.1.call-done = f32[1000,512]{1,0:T(8,128)} async-done(((f32[16000,512]{1,0:T(8,128)}), f32[1000,512]{1,0:T(8,128)}) %reduce-scatter.29.cloned.1.call-update) | async-done | bytes 2048016 | tf_op jit(solution)/shard_map/reduce_scatter | solution.py:301
  (837 shorter events, 625.3 us)
Async XLA Ops:
  7.2 216.7 %copy-start = (bf16[1024,512]{1,0:T(8,128)(2,1)S(1)}, bf16[1024,512]{1,0:T(8,128)(2,1)}, u32[]{:S(2)}) copy-start(bf16[1024,512]{1,0:T(8,128)(2,1)} %param.29) | copy-start | bytes 3145732
  7.2 46.2 %copy-start.74 = (bf16[4,32]{1,0:T(4,128)(2,1)S(1)}, bf16[4,32]{1,0:T(4,128)(2,1)}, u32[]{:S(2)}) copy-start(bf16[4,32]{1,0:T(4,128)(2,1)} %param.35) | copy-start | bytes 772
  7.2 82.0 %copy-start.66 = (s32[1,512,1]{1,2,0:T(1,128)S(1)}, s32[1,512,1]{1,2,0:T(1,128)}, u32[]{:S(2)}) copy-start(s32[1,512,1]{1,2,0:T(1,128)} %param.30) | copy-start | bytes 6148
  7.2 83.7 %copy-start.69 = (s32[1,1024]{1,0:T(1,128)S(1)}, s32[1,1024]{1,0:T(1,128)}, u32[]{:S(2)}) copy-start(s32[1,1024]{1,0:T(1,128)} %param.33) | copy-start | bytes 12292
  7.2 216.6 %all-gather.30.cloned.1.call-start = ((), (), s32[]{:S(2)}) async-start(), calls=%async_computation.11 | async-start | bytes 1114112 | tf_op jit(solution)/shard_map/all_gather | solution.py:191
  8.0 224.1 %all-gather.28.cloned.1.call-start = ((), (), s32[]{:S(2)}) async-start(), calls=%async_computation.10 | async-start | bytes 1671168 | tf_op jit(solution)/shard_map/all_gather | solution.py:188
  8.7 309.4 %all-gather.32.cloned.1.call-start = ((), (), s32[]{:S(2)}) async-start(), calls=%async_computation.12 | async-start | bytes 8912896 | tf_op jit(solution)/shard_map/all_gather | solution.py:233
  9.5 82.5 %copy-start.53 = (bf16[512,32]{0,1:T(8,128)(2,1)S(1)}, bf16[512,32]{0,1:T(8,128)(2,1)}, u32[]{:S(2)}) copy-start(bf16[512,32]{0,1:T(8,128)(2,1)} %param.37) | copy-start | bytes 98308
  9.5 416.8 %all-gather.34.cloned.1.call-start = ((), (), s32[]{:S(2)}) async-start(), calls=%async_computation.13 | async-start | bytes 8912896 | tf_op jit(solution)/shard_map/all_gather | solution.py:234
  10.1 124.4 %copy-start.54 = (bf16[512,32]{0,1:T(8,128)(2,1)S(1)}, bf16[512,32]{0,1:T(8,128)(2,1)}, u32[]{:S(2)}) copy-start(bf16[512,32]{0,1:T(8,128)(2,1)} %param.38) | copy-start | bytes 98308
  10.1 167.3 %copy-start.55 = (bf16[512,32]{0,1:T(8,128)(2,1)S(1)}, bf16[512,32]{0,1:T(8,128)(2,1)}, u32[]{:S(2)}) copy-start(bf16[512,32]{0,1:T(8,128)(2,1)} %param.40) | copy-start | bytes 98308
  10.1 604.9 %all-gather.36.cloned.1.call-start = ((), (), s32[]{:S(2)}) async-start(), calls=%async_computation.14 | async-start | bytes 17408000 | tf_op jit(solution)/shard_map/all_gather | solution.py:244
  10.7 969.0 %all-reduce.4.cloned.1.call-start = ((), (), s32[]{:S(2)}) async-start(), calls=%async_computation.15 | async-start | bytes 1048576 | tf_op jit(solution)/shard_map/psum | solution.py:300
  10.9 259.9 %copy-start.9 = (bf16[512,512]{0,1:T(8,128)(2,1)}, bf16[512,512]{0,1:T(8,128)(2,1)S(1)}, u32[]{:S(2)}) copy-start(bf16[512,512]{0,1:T(8,128)(2,1)S(1)} %copy.125) | copy-start | bytes 1572868
  91.1 140.9 %copy-start.46 = (f32[512]{0:T(512)}, f32[512]{0:T(512)S(1)}, u32[]{:S(2)}) copy-start(f32[512]{0:T(512)S(1)} %broadcast_multiply_fusion.3) | copy-start | bytes 6148
  91.9 140.2 %copy-start.60 = (f32[512]{0:T(512)}, f32[512]{0:T(512)S(1)}, u32[]{:S(2)}) copy-start(f32[512]{0:T(512)S(1)} %fusion.185) | copy-start | bytes 6148
  91.9 140.2 %copy-start.51 = (f32[1,512]{1,0:T(1,128)}, f32[1,512]{1,0:T(1,128)S(1)}, u32[]{:S(2)}) copy-start(f32[1,512]{1,0:T(1,128)S(1)} %get-tuple-element.1087) | copy-start | bytes 6148
  91.9 180.7 %copy-start.58 = (f32[1,512]{1,0:T(1,128)}, f32[1,512]{1,0:T(1,128)S(1)}, u32[]{:S(2)}) copy-start(f32[1,512]{1,0:T(1,128)S(1)} %get-tuple-element.1086) | copy-start | bytes 6148
  91.9 140.1 %copy-start.71 = (f32[1,512]{1,0:T(1,128)}, f32[1,512]{1,0:T(1,128)S(1)}, u32[]{:S(2)}) copy-start(f32[1,512]{1,0:T(1,128)S(1)} %get-tuple-element.1091) | copy-start | bytes 6148
  91.9 180.7 %copy-start.67 = (f32[1,512]{1,0:T(1,128)}, f32[1,512]{1,0:T(1,128)S(1)}, u32[]{:S(2)}) copy-start(f32[1,512]{1,0:T(1,128)S(1)} %get-tuple-element.1090) | copy-start | bytes 6148
  134.5 136.3 %copy-start.24 = (bf16[512,512]{0,1:T(8,128)(2,1)}, bf16[512,512]{0,1:T(8,128)(2,1)S(1)}, u32[]{:S(2)}) copy-start(bf16[512,512]{0,1:T(8,128)(2,1)S(1)} %all_gather.100) | copy-start | bytes 1572868
  313.2 128.4 %copy-start.1 = (f32[512,512]{0,1:T(8,128)}, f32[512,512]{0,1:T(8,128)S(1)}, u32[]{:S(2)}) copy-start(f32[512,512]{0,1:T(8,128)S(1)} %get-tuple-element.1111) | copy-start | bytes 3145732
  318.1 9.3 copy-start.20
  443.5 13.8 collective-permute-start
  727.9 6.4 copy-start.41
  727.9 8.4 copy-start.43
  727.9 10.4 copy-start.38
  727.9 12.3 copy-start.44
  728.0 14.2 copy-start.42
  728.0 16.1 copy-start.45
  962.6 326.4 %reduce-scatter.33.cloned.1.call-start = ((), (), s32[]{:S(2)}) async-start(), calls=%async_computation.25 | async-start | bytes 278528
  987.5 11.0 copy-start.30
  998.5 8.7 copy-start.32
  1095.7 5.3 copy-start.4
  1095.7 5.3 copy-start.49
  1095.7 5.3 copy-start.57
  1095.7 5.3 copy-start.59
  1104.5 5.3 copy-start.26
  1189.1 152.0 %reduce-scatter.31.cloned.1.call-start = ((), (), s32[]{:S(2)}) async-start(), calls=%async_computation.24 | async-start | bytes 278528
  1194.7 197.5 %all-reduce.6.cloned.1.call-start = ((), (), s32[]{:S(2)}) async-start(), calls=%async_computation.26 | async-start | bytes 3145728 | tf_op jit(solution)/shard_map/psum | solution.py:418
  1200.4 272.4 %reduce-scatter.19.cloned.1.call-start = ((), (), s32[]{:S(2)}) async-start(), calls=%async_computation.18 | async-start | bytes 1114112 | tf_op jit(solution)/shard_map/reduce_scatter | solution.py:409
  1203.1 346.7 %reduce-scatter.23.cloned.1.call-start = ((), (), s32[]{:S(2)}) async-start(), calls=%async_computation.20 | async-start | bytes 1114112 | tf_op jit(solution)/shard_map/reduce_scatter | solution.py:411
  1206.1 420.6 %reduce-scatter.17.cloned.1.call-start = ((), (), s32[]{:S(2)}) async-start(), calls=%async_computation.17 | async-start | bytes 1114112 | tf_op jit(solution)/shard_map/reduce_scatter | solution.py:408
  1207.7 499.1 %reduce-scatter.21.cloned.1.call-start = ((), (), s32[]{:S(2)}) async-start(), calls=%async_computation.19 | async-start | bytes 2228224 | tf_op jit(solution)/shard_map/reduce_scatter | solution.py:410
  1211.9 628.7 %reduce-scatter.15.cloned.1.call-start = ((), (), s32[]{:S(2)}) async-start(), calls=%async_computation.16 | async-start | bytes 3342336 | tf_op jit(solution)/shard_map/reduce_scatter | solution.py:407
  1217.2 971.9 %reduce-scatter.27.cloned.1.call-start = ((), (), s32[]{:S(2)}) async-start(), calls=%async_computation.22 | async-start | bytes 17825792 | tf_op jit(solution)/shard_map/reduce_scatter | solution.py:415
  1230.9 1313.0 %reduce-scatter.25.cloned.1.call-start = ((), (), s32[]{:S(2)}) async-start(), calls=%async_computation.21 | async-start | bytes 17825792 | tf_op jit(solution)/shard_map/reduce_scatter | solution.py:414
  1242.5 1977.7 %reduce-scatter.29.cloned.1.call-start = ((), (), s32[]{:S(2)}) async-start(), calls=%async_computation.23 | async-start | bytes 34816000 | tf_op jit(solution)/shard_map/reduce_scatter | solution.py:301
  (62 other events, 130.4 us)
Sparse Core Ops, SparseCore 0:
  10.8 58.0 all-gather.29
  71.7 59.0 all-gather.27
  133.5 148.9 all-gather.31
  285.0 141.1 all-gather.33
  428.8 186.1 all-gather.35
  962.7 16.8 all-reduce.3
  1189.3 77.3 reduce-scatter.32
  1268.9 72.2 reduce-scatter.30
  1344.2 47.9 all-reduce.5
  1394.9 77.8 reduce-scatter.18
  1475.7 74.0 reduce-scatter.22
  1552.5 74.2 reduce-scatter.16
  1629.7 76.9 reduce-scatter.20
  1712.9 127.6 reduce-scatter.14
  1843.4 345.5 reduce-scatter.26
  2191.9 352.0 reduce-scatter.24
  2546.9 673.2 reduce-scatter.28
where the time goes:
time: 3250 us; the launch traced here: 3230 us
  waiting for transfers between devices  2210 us (68%)
  matrix products  520 us (16%)
  blocking collectives  272 us (8%)
  local copies, waits for them, and re-layouts  109 us (3%)
  other arithmetic  92.2 us (3%)
    reduce_scatter x1, waiting for transfers between devices, local(): lax.psum_scatter(block_grads.reshape(-1, model_width), ('dp', 'pass'), sc...  676 us
    reduce_scatter x1, waiting for transfers between devices, local(): lax.psum_scatter(expert_in_grad, ('dp', 'pass'), scatter_dimension=2, til...  355 us
    reduce_scatter x1, waiting for transfers between devices, local(): lax.psum_scatter(expert_out_grad, ('dp', 'pass'), scatter_dimension=2, ti...  348 us
    all_gather x1, waiting for transfers between devices, local(): vocab_part = lax.all_gather(embedding, ('dp', 'pass'), axis=0, tiled=True)  156 us
    reduce_scatter x1, waiting for transfers between devices, local(): lax.psum_scatter(self_project_grad, ('dp', 'pass'), scatter_dimension=1,...  134 us
    all_gather x1, waiting for transfers between devices, local(): lax.all_gather(expert_out, ('dp', 'pass'), axis=2, tiled=True)  98.8 us
    reduce_scatter x1, waiting for transfers between devices, local(): lax.psum_scatter(memory_project_grad, ('dp', 'pass'), scatter_dimension=1...  80 us
    reduce_scatter x1, waiting for transfers between devices, local(): lax.psum_scatter(cross_output_grad, ('dp', 'pass'), scatter_dimension=1,...  77 us
  transfers between devices with their start and end apart: 18, of which 14 were waited for; matrix products, arithmetic and copies ran while one was open for 6% of the time, Pallas kernels for 0%

commit v1 on v0

v1 whole, which is shorter than its diff:
```python
import functools

import jax
import jax.numpy as jnp
from jax import lax
from jax.experimental import pallas as pl
from jax.experimental.pallas import tpu as pltpu
from jax.sharding import PartitionSpec as P

HEADS = 8
VOCAB = 32000
GROUPS = 4
EPSILON = 1e-05
SMOOTH = 0.1
F32 = jnp.float32
BF16 = jnp.bfloat16
PARAMS = pltpu.CompilerParams(vmem_limit_bytes=56 * 1024 * 1024)


def swap(block, axis, mask):
    count = lax.axis_size(axis)
    return lax.ppermute(block, axis, [(i, i ^ mask) for i in range(count)])


def after(value, *others):
    return lax.optimization_barrier((value,) + others)[0]


def gather_xor(block, axis):
    count = lax.axis_size(axis)
    if count == 8:
        far = {g: swap(block, axis, 2 * g) for g in (2, 3, 1)}
        near = {0: swap(block, axis, 1)}
        for g in (1, 3, 2):
            near[g] = swap(far[g], axis, 1)
        far[0] = block
        return [part for g in range(4) for part in (far[g], near[g])]
    blocks = [block]
    step = 1
    while step < count:
        blocks = blocks + [swap(part, axis, step) for part in blocks]
        step *= 2
    return blocks


def scatter_sum_xor(blocks, axis):
    count = lax.axis_size(axis)
    if count == 8:
        near = {g: swap(blocks[2 * g + 1].astype(BF16), axis, 1) for g in (2, 3, 1, 0)}
        total = None
        for g in (2, 3, 1, 0):
            part = blocks[2 * g].astype(F32) + near[g].astype(F32)
            if g:
                part = swap(part.astype(BF16), axis, 2 * g).astype(F32)
            total = part if total is None else total + part
        return total
    step = count // 2
    while step >= 1:
        blocks = [
            blocks[k].astype(F32) + swap(blocks[k + step].astype(BF16), axis, step).astype(F32)
            for k in range(step)
        ]
        step //= 2
    return blocks[0]


def dot(left, right):
    return jnp.dot(left, right, preferred_element_type=F32)


def ein(spec, left, right):
    return jnp.einsum(spec, left, right, preferred_element_type=F32)


def attend_forward_kernel(causal, kn_ref, qt_ref, vt_ref, bias_ref, ot_ref, lse_ref):
    keys, tokens = kn_ref.shape[0], qt_ref.shape[1]
    head = qt_ref.shape[0] // 2
    zeros = jnp.zeros((head, tokens), BF16)
    if causal:
        rows = lax.broadcasted_iota(jnp.int32, (keys, tokens), 0)
        cols = lax.broadcasted_iota(jnp.int32, (keys, tokens), 1)
        allowed = rows <= cols
    for h in range(2):
        q = qt_ref[h * head : (h + 1) * head, :]
        q = jnp.concatenate([zeros, q] if h else [q, zeros], axis=0)
        s = dot(kn_ref[...], q)
        s = jnp.where(allowed, s, -1e30) if causal else s + bias_ref[...]
        m = jnp.max(s, axis=0, keepdims=True)
        e = jnp.exp(s - m)
        total = jnp.sum(e, axis=0, keepdims=True)
        p = (e * (1.0 / total)).astype(BF16)
        ot_ref[h * head : (h + 1) * head, :] = dot(
            vt_ref[h * head : (h + 1) * head, :], p
        ).astype(BF16)
        lse_ref[0, h : h + 1, :] = m + jnp.log(total)


def attend_forward(kn, qt, vt, bias, causal):
    keys, width = kn.shape
    tokens = qt.shape[1]
    pair = 2 * width // HEADS
    wide = pl.BlockSpec((pair, tokens), lambda j: (j, 0))
    return pl.pallas_call(
        functools.partial(attend_forward_kernel, causal),
        grid=(HEADS // 2,),
        in_specs=[
            pl.BlockSpec((keys, pair), lambda j: (0, j)),
            wide,
            pl.BlockSpec((pair, keys), lambda j: (j, 0)),
            pl.BlockSpec((keys, 1), lambda j: (0, 0)),
        ],
        out_specs=[wide, pl.BlockSpec((1, 2, tokens), lambda j: (j, 0, 0))],
        out_shape=[
            jax.ShapeDtypeStruct((width, tokens), BF16),
            jax.ShapeDtypeStruct((HEADS // 2, 2, tokens), F32),
        ],
        compiler_params=PARAMS,
    )(kn, qt, vt, bias)


def attend_backward_kernel(
    causal, kn_ref, kt_ref, vn_ref, qt_ref, qn_ref, dot_ref, don_ref, lse_ref, bias_ref, dqt_ref, dk_ref, dv_ref
):
    keys, tokens = kn_ref.shape[0], qt_ref.shape[1]
    head = qt_ref.shape[0] // 2
    zeros = jnp.zeros((head, tokens), BF16)
    lanes = lax.broadcasted_iota(jnp.int32, (tokens, 2 * head), 1)
    if causal:
        rows = lax.broadcasted_iota(jnp.int32, (keys, tokens), 0)
        cols = lax.broadcasted_iota(jnp.int32, (keys, tokens), 1)
        allowed = rows <= cols
    dk = jnp.zeros((keys, 2 * head), F32)
    dv = jnp.zeros((keys, 2 * head), F32)
    for h in range(2):
        mine = (lanes >= head) if h else (lanes < head)
        span = slice(h * head, (h + 1) * head)
        q, do = qt_ref[span, :], dot_ref[span, :]
        q = jnp.concatenate([zeros, q] if h else [q, zeros], axis=0)
        do = jnp.concatenate([zeros, do] if h else [do, zeros], axis=0)
        s = dot(kn_ref[...], q)
        s = jnp.where(allowed, s, -1e30) if causal else s + bias_ref[...]
        p = jnp.exp(s - lse_ref[0, h : h + 1, :])
        dp = dot(vn_ref[...], do)
        pdp = p * dp
        total = jnp.sum(pdp, axis=0, keepdims=True)
        ds = (pdp - p * total).astype(BF16)
        dqt_ref[span, :] = (dot(kt_ref[span, :], ds) * head**-0.5).astype(BF16)
        dk = dk + dot(ds, jnp.where(mine, qn_ref[...], jnp.zeros_like(qn_ref[...])))
        dv = dv + dot(p.astype(BF16), jnp.where(mine, don_ref[...], jnp.zeros_like(don_ref[...])))
    dk_ref[...] = dk.astype(BF16)
    dv_ref[...] = dv.astype(BF16)


def attend_backward(kn, kt, vn, qt, qn, do_t, do_n, lse, bias, causal):
    keys, width = kn.shape
    tokens = qt.shape[1]
    pair = 2 * width // HEADS
    key_rows = pl.BlockSpec((keys, pair), lambda j: (0, j))
    wide = pl.BlockSpec((pair, tokens), lambda j: (j, 0))
    tall = pl.BlockSpec((tokens, pair), lambda j: (0, j))
    return pl.pallas_call(
        functools.partial(attend_backward_kernel, causal),
        grid=(HEADS // 2,),
        in_specs=[
            key_rows,
            pl.BlockSpec((pair, keys), lambda j: (j, 0)),
            key_rows,
            wide,
            tall,
            wide,
            tall,
            pl.BlockSpec((1, 2, tokens), lambda j: (j, 0, 0)),
            pl.BlockSpec((keys, 1), lambda j: (0, 0)),
        ],
        out_specs=[wide, key_rows, key_rows],
        out_shape=[
            jax.ShapeDtypeStruct((width, tokens), BF16),
            jax.ShapeDtypeStruct((keys, width), BF16),
            jax.ShapeDtypeStruct((keys, width), BF16),
        ],
        compiler_params=PARAMS,
    )(kn, kt, vn, qt, qn, do_t, do_n, lse, bias)


def first_sweep_kernel(e_ref, ht_ref, stat_in_ref, sum_in_ref, stat_ref, sum_ref):
    half = ht_ref.shape[1] // 2

    @pl.when(pl.program_id(0) == 0)
    def _():
        stat_ref[...] = stat_in_ref[...]
        sum_ref[...] = sum_in_ref[...]

    rows = e_ref[...]
    z = dot(rows, ht_ref[...])
    old = stat_ref[0:1, :]
    top = jnp.maximum(old, jnp.max(z, axis=0, keepdims=True))
    e = jnp.exp(z - top)
    gap = z[:, :half] - z[:, half:]
    drift = jnp.concatenate(
        [
            jnp.sum(e[:, :half] * gap, axis=0, keepdims=True),
            -jnp.sum(e[:, half:] * gap, axis=0, keepdims=True),
        ],
        axis=1,
    )
    factor = jnp.exp(old - top)
    stat_ref[0:1, :] = top
    stat_ref[1:2, :] = stat_ref[1:2, :] * factor + jnp.sum(e, axis=0, keepdims=True)
    stat_ref[2:3, :] = stat_ref[2:3, :] * factor + drift
    sum_ref[...] += dot(jnp.ones((8, rows.shape[0]), BF16), rows)


def block_of(rows):
    for size in (400, 200, 80, 40, 16):
        if rows % size == 0:
            return size
    return rows


def first_sweep(rows, ht, stats, sums):
    count, width = rows.shape
    block = block_of(count)
    whole = lambda a: pl.BlockSpec(a.shape, lambda i: (0, 0))
    return pl.pallas_call(
        first_sweep_kernel,
        grid=(count // block,),
        in_specs=[pl.BlockSpec((block, width), lambda i: (i, 0)), whole(ht), whole(stats), whole(sums)],
        out_specs=[whole(stats), whole(sums)],
        out_shape=[jax.ShapeDtypeStruct(stats.shape, F32), jax.ShapeDtypeStruct(sums.shape, F32)],
        compiler_params=PARAMS,
    )(rows, ht, stats, sums)


def second_sweep_kernel(
    base, e_ref, ht_ref, hn_ref, row_ref, target_ref, flat_ref, acc_in_ref, hit_in_ref, de_ref, acc_ref, hit_ref
):
    half = ht_ref.shape[1] // 2
    block = e_ref.shape[0]
    step = pl.program_id(0)

    @pl.when(step == 0)
    def _():
        acc_ref[...] = acc_in_ref[...]
        hit_ref[...] = hit_in_ref[...]

    rows = e_ref[...]
    z = dot(rows, ht_ref[...])
    z0, z1 = z[:, :half], z[:, half:]
    p0 = jnp.exp(z0 - row_ref[0:1, :half])
    p1 = jnp.exp(z1 - row_ref[0:1, half:])
    gap = z0 - z1
    spot = lax.broadcasted_iota(jnp.int32, (block, half), 0)
    hit = spot == target_ref[0:1, :] - (base + step * block)
    picked = jnp.where(hit, row_ref[2:3, :half], 0.0)
    hit_ref[0:1, :] += jnp.sum(jnp.where(hit, z0 + z1, 0.0), axis=0, keepdims=True)
    g0 = p0 * (row_ref[1:2, :half] + gap) - p1 - picked
    g1 = p1 * (row_ref[1:2, half:] - gap) - p0 - picked
    dz = jnp.concatenate([g0.astype(BF16), g1.astype(BF16)], axis=1)
    de_ref[...] = (dot(dz, hn_ref[...]) + flat_ref[0:1, :]).astype(BF16)
    acc_ref[...] += lax.dot_general(rows, dz, (((0,), (0,)), ((), ())), preferred_element_type=F32)


def second_sweep(base, rows, ht, hn, row_stats, target, flat, acc, hits):
    count, width = rows.shape
    block = block_of(count)
    whole = lambda a: pl.BlockSpec(a.shape, lambda i: (0, 0))
    tall = pl.BlockSpec((block, width), lambda i: (i, 0))
    return pl.pallas_call(
        functools.partial(second_sweep_kernel, base),
        grid=(count // block,),
        in_specs=[tall] + [whole(a) for a in (ht, hn, row_stats, target, flat, acc, hits)],
        out_specs=[tall, whole(acc), whole(hits)],
        out_shape=[
            jax.ShapeDtypeStruct((count, width), BF16),
            jax.ShapeDtypeStruct(acc.shape, F32),
            jax.ShapeDtypeStruct(hits.shape, F32),
        ],
        compiler_params=PARAMS,
    )(rows, ht, hn, row_stats, target, flat, acc, hits)


def pick_kernel(order_ref, block_ref, out_ref):
    out_ref[...] = block_ref[...].astype(out_ref.dtype)


def pick_blocks(stack, order, dtype):
    shape = stack.shape[1:]
    return pl.pallas_call(
        pick_kernel,
        grid_spec=pltpu.PrefetchScalarGridSpec(
            num_scalar_prefetch=1,
            grid=(order.shape[0],),
            in_specs=[pl.BlockSpec((1,) + shape, lambda j, order_ref: (order_ref[j], 0, 0))],
            out_specs=pl.BlockSpec((1,) + shape, lambda j, order_ref: (j, 0, 0)),
        ),
        out_shape=jax.ShapeDtypeStruct((order.shape[0],) + shape, dtype),
        compiler_params=PARAMS,
    )(order, stack)


def norm_forward(values, gain, bias):
    average = jnp.mean(values, axis=0, keepdims=True)
    centered = values - average
    scale = lax.rsqrt(jnp.mean(centered * centered, axis=0, keepdims=True) + EPSILON)
    return centered * scale * gain + bias


def norm_backward(values, gain, upstream):
    average = jnp.mean(values, axis=0, keepdims=True)
    centered = values - average
    scale = lax.rsqrt(jnp.mean(centered * centered, axis=0, keepdims=True) + EPSILON)
    unit = centered * scale
    grad = upstream * gain
    result = scale * (
        grad - jnp.mean(grad, axis=0, keepdims=True) - unit * jnp.mean(grad * unit, axis=0, keepdims=True)
    )
    return result, jnp.sum(upstream * unit, axis=1), jnp.sum(upstream, axis=1)


def group_sum(first, second):
    core = lax.axis_index("vocab")
    mine = jnp.where(core == 0, first, second)
    theirs = jnp.where(core == 0, second, first)
    part = mine + swap(theirs.astype(BF16), "vocab", 1).astype(F32)
    part = part.astype(BF16)
    part = part.astype(F32) + swap(part, "pass", 1).astype(F32)
    other = swap(part, "vocab", 1)
    return jnp.where(core == 0, part, other), jnp.where(core == 0, other, part)


def local(
    inputs,
    memory,
    expert_ids,
    targets,
    lengths,
    memory_mask,
    norm_gain,
    norm_bias,
    self_project,
    self_output,
    cross_query,
    memory_project,
    cross_output,
    expert_in,
    expert_out,
    embedding,
):
    seq_len, width = inputs.shape
    rows_axis = lax.axis_size("dp")
    here = lax.axis_index("dp")
    which = lax.axis_index("pass")
    core = lax.axis_index("vocab")
    shards = 2 * rows_axis

    matrices = (self_project, self_output, cross_query, memory_project, cross_output)
    sizes = [matrix.shape[1] for matrix in matrices]
    half_rows = sizes[0] + sizes[1]
    norm_width = norm_gain.shape[1]
    norm_pack = jnp.concatenate([norm_gain, norm_bias], axis=0).reshape(1, 8 * norm_width)
    norm_pack = jnp.pad(norm_pack, ((0, 15), (0, width - 8 * norm_width)))
    packed = jnp.concatenate(matrices, axis=1).T
    mine = jnp.concatenate(
        [jnp.where(core == 0, packed[:half_rows], packed[half_rows:]), norm_pack], axis=0
    )
    got = gather_xor(mine, "dp")
    got = jnp.stack(got)
    got = jnp.stack([got, swap(got, "pass", 1)], axis=1)
    twin = swap(got, "vocab", 1)
    order = jnp.arange(rows_axis)[:, None] ^ here
    order = (2 * order + (jnp.arange(2)[None, :] ^ which)).reshape(-1).astype(jnp.int32)
    flat = (shards,) + mine.shape
    got = pick_blocks(got.reshape(flat), order, BF16)
    twin = pick_blocks(twin.reshape(flat), order, BF16)
    self_pack = jnp.where(core == 0, got, twin)
    cross_pack = jnp.where(core == 0, twin, got)
    norms = self_pack[:, half_rows, : 8 * norm_width].reshape(shards, 8, norm_width)
    norms = norms.transpose(1, 0, 2).reshape(8, width).astype(F32)
    gains = [norms[j][:, None] for j in range(4)]
    biases = [norms[4 + j][:, None] for j in range(4)]
    project_t = self_pack[:, : sizes[0]].reshape(-1, width)
    self_output_t = self_pack[:, sizes[0] : half_rows].reshape(-1, width)
    cross_query_t = cross_pack[:, : sizes[2]].reshape(-1, width)
    memory_project_t = cross_pack[:, sizes[2] : sizes[2] + sizes[3]].reshape(-1, width)
    cross_output_t = cross_pack[:, sizes[2] + sizes[3] : half_rows].reshape(-1, width)

    experts = expert_in.shape[0] // 2
    hidden = expert_in.shape[2]

    def core_half(weights):
        halves = weights.reshape(2, experts, width, hidden)
        return jnp.where(core == 0, halves[0], halves[1]).transpose(0, 2, 1)

    expert_block = jnp.stack([core_half(expert_in), core_half(expert_out)])
    expert_got = gather_xor(after(expert_block, got), "dp")
    weight_in = jnp.concatenate([part[0].reshape(-1, width) for part in expert_got])
    weight_out = jnp.concatenate([part[1].reshape(-1, width) for part in expert_got])

    word_got = gather_xor(after(embedding, expert_got[-1]), "dp")
    per_group = rows_axis // GROUPS
    words = [
        jnp.concatenate(word_got[g * per_group : (g + 1) * per_group]) for g in range(GROUPS)
    ]
    group_rows = words[0].shape[0]

    scaling = (width // HEADS) ** -0.5
    tokens = inputs.T.astype(F32)
    a1 = norm_forward(tokens, gains[0], biases[0]).astype(BF16)
    qkv_t = dot(project_t, a1).astype(BF16)
    query_t = qkv_t[:width] * jnp.asarray(scaling, BF16)
    key_t, value_t = qkv_t[width : 2 * width], qkv_t[2 * width :]
    key_n, value_n = key_t.T, value_t.T
    no_bias = jnp.zeros((seq_len, 1), F32)
    attended_t, self_lse = attend_forward(key_n, query_t, value_t, no_bias, True)
    h1 = tokens + dot(self_output_t, attended_t)
    a2 = norm_forward(h1, gains[1], biases[1]).astype(BF16)
    cross_t = dot(cross_query_t, a2).astype(BF16) * jnp.asarray(scaling, BF16)
    memory_kv = ein("mi,oi->mo", memory, memory_project_t).astype(BF16)
    mem_key, mem_value = memory_kv[:, :width], memory_kv[:, width:]
    mem_bias = jnp.where(memory_mask[0][:, None] == 1, 0.0, -1e30).astype(F32)
    cross_att_t, cross_lse = attend_forward(mem_key, cross_t, mem_value.T, mem_bias, False)
    h2 = h1 + dot(cross_output_t, cross_att_t)
    a3 = norm_forward(h2, gains[2], biases[2]).astype(BF16)

    my_route = expert_ids[0, :, 0].astype(F32)[None, :]
    other_route = swap(my_route, "pass", 1)
    routes = (jnp.where(which == 0, my_route, other_route), jnp.where(which == 0, other_route, my_route))
    names = (core * experts + jnp.arange(experts)).astype(F32)
    masks = [(route == names[:, None])[None, :, None, :] for route in routes]
    shape4 = (rows_axis, experts, hidden, seq_len)

    def routed(values, mask):
        return jnp.where(mask, values.reshape(shape4), jnp.zeros((), values.dtype)).reshape(values.shape)

    pre_act = dot(weight_in, a3)
    activation = jax.nn.gelu(pre_act).astype(BF16)
    active = jnp.concatenate([routed(activation, mask) for mask in masks], axis=1)
    part = ein("fd,ft->dt", weight_out, active)
    y0, y1 = group_sum(part[:, :seq_len], part[:, seq_len:])
    block0, block1 = h2 + y0, h2 + y1
    final0 = norm_forward(block0, gains[3], biases[3]).astype(BF16)
    final1 = norm_forward(block1, gains[3], biases[3]).astype(BF16)
    block_out = jnp.where(which == 0, block0, block1).T[None]

    final_t = jnp.concatenate([final0, final1], axis=1)
    final_n = final_t.T
    valid = (jnp.arange(seq_len) < lengths[here]).astype(F32)
    half_weight = 0.5 * valid
    stats = jnp.concatenate(
        [jnp.full((1, 2 * seq_len), -1e30, F32), jnp.zeros((7, 2 * seq_len), F32)], axis=0
    )
    sums = jnp.zeros((8, width), F32)
    for g in range(GROUPS):
        stats, sums = first_sweep(words[g], final_t, stats, sums)

    def merge(left, axis):
        right = swap(left, axis, 1)
        top = jnp.maximum(left[0:1], right[0:1])
        total = left[1:] * jnp.exp(left[0:1] - top) + right[1:] * jnp.exp(right[0:1] - top)
        return jnp.concatenate([top, total], axis=0)

    merged = merge(merge(stats, "vocab"), "pass")
    lse = merged[0:1] + jnp.log(merged[1:2])
    drift = merged[2:3] / merged[1:2]
    weight2 = jnp.concatenate([half_weight, half_weight])[None, :]
    valid2 = weight2 > 0
    row_stats = jnp.concatenate(
        [
            jnp.where(valid2, lse + jnp.log(2.0), 1e30),
            2.0 - drift,
            (1.0 - SMOOTH) * weight2,
            jnp.zeros((5, 2 * seq_len), F32),
        ],
        axis=0,
    )
    shard_rows = embedding.shape[0]
    owner = targets // shard_rows
    in_quarter = (owner % 2 == core) & (owner // 2 % 2 == which)
    column = ((owner // 4) ^ here) * shard_rows + targets % shard_rows
    target = jnp.broadcast_to(jnp.where(in_quarter, column, -1)[None, :], (8, seq_len)).astype(jnp.int32)
    hidden_sum = jnp.sum(final_t.astype(F32) * weight2, axis=1)
    level = SMOOTH / VOCAB
    flat_grad = jnp.broadcast_to(-level * hidden_sum[None, :], (8, width))
    hits = jnp.zeros((8, seq_len), F32)
    acc = -level * sums[0][:, None] * weight2
    word_grads = []
    for g in range(GROUPS):
        grads, acc, hits = second_sweep(
            g * group_rows, words[g], final_t, final_n, row_stats, target, flat_grad, acc, hits
        )
        word_grads += [
            grads[k * shard_rows : (k + 1) * shard_rows] for k in range(per_group)
        ]
    embedding_grad = scatter_sum_xor(word_grads, "dp")
    loss = (
        0.25 * jnp.sum(weight2 * (lse + drift))
        - (1.0 - SMOOTH) * jnp.sum(half_weight * hits[0])
        - level * jnp.sum(hidden_sum * sums[0])
    )
    loss = jnp.broadcast_to(loss, (8, 128))
    for axis in ("vocab", "pass"):
        loss = loss + swap(loss, axis, 1)
    step = 1
    while step < rows_axis:
        loss = loss + swap(loss, "dp", step)
        step *= 2
    mean_loss = loss[0, 0] / jnp.sum(lengths).astype(F32)

    dh0, dh1 = group_sum(acc[:, :seq_len], acc[:, seq_len:])
    db0, gain0, bias0 = norm_backward(block0, gains[3], dh0)
    db1, gain1, bias1 = norm_backward(block1, gains[3], dh1)
    gain_three, bias_three = gain0 + gain1, bias0 + bias1
    dy = jnp.concatenate([db0, db1], axis=1).astype(BF16)
    d_act = dot(weight_out, dy)
    picked = routed(d_act[:, :seq_len], masks[0]) + routed(d_act[:, seq_len:], masks[1])
    unused, pull = jax.vjp(jax.nn.gelu, pre_act)
    du = pull(picked)[0].astype(BF16)
    da3_part = ein("fd,ft->dt", weight_in, du)
    in_grad = ein("ft,dt->fd", du, a3).reshape(rows_axis, experts, hidden, width)
    out_grad = ein("ft,dt->fd", active, dy).reshape(rows_axis, experts, hidden, width)
    expert_grad = scatter_sum_xor(
        [jnp.stack([in_grad[k], out_grad[k]]).astype(BF16) for k in range(rows_axis)], "dp"
    )
    expert_twin = swap(expert_grad, "vocab", 1)
    expert_grad = jnp.concatenate(
        [
            jnp.where(core == 0, expert_grad, expert_twin),
            jnp.where(core == 0, expert_twin, expert_grad),
        ],
        axis=1,
    ).transpose(0, 1, 3, 2)
    half = seq_len // 2
    left, right = group_sum(da3_part[:, :half], da3_part[:, half:])
    da3 = jnp.concatenate([left, right], axis=1)
    two_grad, gain_two, bias_two = norm_backward(h2, gains[2], da3)
    dh2 = db0 + db1 + two_grad

    cross_low = dh2.astype(BF16)
    cross_output_grad = ein("ot,it->oi", cross_low, cross_att_t)
    do_t = ein("oi,ot->it", cross_output_t, cross_low).astype(BF16)
    dq_t, dk, dv = attend_backward(
        mem_key, mem_key.T, mem_value, cross_t, cross_t.T, do_t, do_t.T, cross_lse, mem_bias, False
    )
    cross_query_grad = ein("ot,it->oi", dq_t, a2)
    pair_grad = jnp.concatenate([dk, dv], axis=1)
    memory_project_grad = ein("mo,mi->oi", pair_grad, memory)
    memory_grad = dot(pair_grad, memory_project_t)
    da2 = ein("oi,ot->it", cross_query_t, dq_t)
    one_grad, gain_one, bias_one = norm_backward(h1, gains[1], da2)
    dh1 = dh2 + one_grad
    self_low = dh1.astype(BF16)
    self_output_grad = ein("ot,it->oi", self_low, attended_t)
    so_t = ein("oi,ot->it", self_output_t, self_low).astype(BF16)
    sq_t, sk, sv = attend_backward(
        key_n, key_t, value_n, query_t, query_t.T, so_t, so_t.T, self_lse, no_bias, True
    )
    project_low = jnp.concatenate([sq_t, sk.T, sv.T], axis=0)
    self_project_grad = ein("ot,it->oi", project_low, a1)
    da1 = ein("oi,ot->it", project_t, project_low)
    zero_grad, gain_zero, bias_zero = norm_backward(tokens, gains[0], da1)
    inputs_grad = (dh1 + zero_grad).T

    norm_grads = jnp.stack(
        [gain_zero, gain_one, gain_two, gain_three, bias_zero, bias_one, bias_two, bias_three]
    )
    norm_grads = norm_grads.reshape(8, shards, norm_width).transpose(1, 0, 2).reshape(shards, 1, -1)
    norm_grads = jnp.pad(norm_grads, ((0, 0), (0, 15), (0, width - 8 * norm_width)))

    def shard_blocks(grads):
        return jnp.concatenate(
            [grad.reshape(shards, -1, width) for grad in grads] + [norm_grads], axis=1
        ).astype(BF16)

    stack = jnp.concatenate(
        [
            shard_blocks([self_project_grad, self_output_grad]),
            shard_blocks([cross_query_grad, memory_project_grad, cross_output_grad]),
        ]
    )
    order = core * shards + 2 * (jnp.arange(rows_axis) ^ here) + which
    blocks = pick_blocks(stack, order.astype(jnp.int32), BF16)
    layer_grad = scatter_sum_xor([blocks[k] for k in range(rows_axis)], "dp")
    layer_twin = swap(layer_grad, "vocab", 1)
    first = jnp.where(core == 0, layer_grad, layer_twin)
    second = jnp.where(core == 0, layer_twin, layer_grad)
    norm_out = first[half_rows, : 8 * norm_width].reshape(8, norm_width)
    first, second = first[:half_rows].T, second[:half_rows].T
    return (
        block_out,
        mean_loss,
        inputs_grad,
        memory_grad,
        norm_out[:4],
        norm_out[4:],
        first[:, : sizes[0]],
        first[:, sizes[0] :],
        second[:, : sizes[2]],
        second[:, sizes[2] : sizes[2] + sizes[3]],
        second[:, sizes[2] + sizes[3] :],
        expert_grad[0],
        expert_grad[1],
        embedding_grad,
    )


def solution(mesh):
    shared = P(None, ("dp", "pass"))
    placed = (
        P("dp", None),
        P("dp", None),
        P("pass", "dp", None),
        P("dp"),
        P(),
        P("dp", None),
        shared,
        shared,
        shared,
        shared,
        shared,
        shared,
        shared,
        P(None, None, ("dp", "pass")),
        P(None, None, ("dp", "pass")),
        P(("dp", "pass", "vocab"), None),
    )
    return jax.shard_map(
        local,
        mesh=mesh,
        in_specs=placed,
        out_specs=(
            P("pass", "dp", None),
            P(),
            P("dp", None),
            P("dp", None),
            shared,
            shared,
            shared,
            shared,
            shared,
            shared,
            shared,
            P(None, None, ("dp", "pass")),
            P(None, None, ("dp", "pass")),
            P(("dp", "pass", "vocab"), None),
        ),
        check_vma=False,
    )
```

time: 3250 us -> 804 us (0.25)
  waiting for transfers between devices: 2210 us -> 318 us
  matrix products: 520 us -> 39.7 us
  blocking collectives: 272 us -> 0 us
  Pallas kernels: 0 us -> 153 us
  starting transfers between devices: 2.28 us -> 68.4 us
    reduce_scatter x8 -> x0, waiting for transfers between devices: 1820 us -> none  [the longest x1 676 us: local(): lax.psum_scatter(block_grads.reshape(-1, model_width), ('dp', 'pass'), sc...]
    dot_general x229 -> x21, matrix products: 520 us -> 39.7 us  [the longest x14 24 us: ein(): return jnp.einsum(spec, left, right, preferred_element_type=F32)]
    ppermute x1 -> x63, waiting for transfers between devices: 11.6 us -> 318 us  [swap(): return lax.ppermute(block, axis, [(i, i ^ mask) for i in range(count)])]
    all_gather x5 -> x0, waiting for transfers between devices: 255 us -> none  [the longest x1 156 us: local(): vocab_part = lax.all_gather(embedding, ('dp', 'pass'), axis=0, tiled=True)]
    all_gather x15 -> x0, blocking collectives: 230 us -> none  [the longest x1 46.5 us: local(): lax.all_gather(cross_output, ('dp', 'pass'), axis=1, tiled=True)]
    pallas_call x0 -> x15, Pallas kernels: none -> 153 us  [the longest x4 52.7 us: second_sweep(): pl.pallas_call(functools.partial(second_sweep_kernel, base), grid=(count...]
    ppermute x1 -> x63, starting transfers between devices: 1.34 us -> 68.4 us  [swap(): return lax.ppermute(block, axis, [(i, i ^ mask) for i in range(count)])]
    psum x2 -> x0, waiting for transfers between devices: 66.7 us -> none  [the longest x1 49.7 us: local(): lax.psum(inputs_local.astype(jnp.bfloat16), 'pass').astype(jnp.float32)]
  transfers between devices with their start and end apart: 18 -> 63, of which waited for: 14 -> 20; matrix products, arithmetic and copies ran while one was open for 6% -> 21% of each run, Pallas kernels for 0% -> 4%
where the time goes in v1:
time: 804 us; the launch traced here: 797 us
  waiting for transfers between devices  318 us (40%)
  Pallas kernels  153 us (19%)
  local copies, waits for them, and re-layouts  123 us (15%)
  other arithmetic  87.7 us (11%)
  starting transfers between devices  68.4 us (9%)
  matrix products  39.7 us (5%)
    ppermute x63, waiting for transfers between devices, swap(): return lax.ppermute(block, axis, [(i, i ^ mask) for i in range(count)])  318 us
    ppermute x63, starting transfers between devices, swap(): return lax.ppermute(block, axis, [(i, i ^ mask) for i in range(count)])  68.4 us
    pallas_call x4, Pallas kernels, second_sweep(): pl.pallas_call(functools.partial(second_sweep_kernel, base), grid=(count...  52.7 us
    pallas_call x4, Pallas kernels, first_sweep(): pl.pallas_call(first_sweep_kernel, grid=(count // block,), in_specs=[pl.B...  30.3 us
    unnamed x209, local copies, waits for them, and re-layouts  29.5 us
    pallas_call x3, Pallas kernels, pick_blocks(): pl.pallas_call(pick_kernel, grid_spec=pltpu.PrefetchScalarGridSpec(num_sc...  27.1 us
    pallas_call x2, Pallas kernels, attend_backward(): pl.pallas_call(functools.partial(attend_backward_kernel, causal), grid=(H...  26.4 us
    dot_general x14, matrix products, ein(): return jnp.einsum(spec, left, right, preferred_element_type=F32)  24 us
  transfers between devices with their start and end apart: 63, of which 20 were waited for; matrix products, arithmetic and copies ran while one was open for 21% of the time, Pallas kernels for 4%

profile of v1, /device:TPU:0, one launch (start us, length us, event | category | flops | bytes accessed | tf_op | source)
XLA Modules:
  0.0 797.5 jit_solution(16995692280365792325)
XLA Ops:
  6.3 4.0 collective-permute-start.3
  26.9 3.8 collective-permute-done.2
  35.3 21.6 %collective-permute-done.7 = bf16[8,144,512]{2,1,0:T(8,128)(2,1)} collective-permute-done((bf16[8,144,512]{2,1,0:T(8,128)(2,1)S(1)}, bf16[8,144,512]{2,1,0:T(8,128)(2,1)}, u32[]{:S(2)}, u32[]{:S(2)}) %collective-permute-start.7) | collective-permute-done | bytes 1179680 | tf_op jit(solution)/shard_map/ppermute | solution.py:22
  60.1 10.7 %shard_map.263 = bf16[16,144,512]{2,1,0:T(8,128)(2,1)} custom-call(s32[16]{0:T(128)} %add.338.order_ref, bf16[16,144,512]{2,1,0:T(8,128)(2,1)} %bitcast.223), custom_call_target="tpu_custom_call" | custom-call | tf_op jit(solution)/shard_map/pallas_call | solution.py:288
  70.8 3.5 collective-permute-start.14
  82.0 5.4 collective-permute-done.14
  87.8 10.0 %collective-permute-done.10 = bf16[2,2,128,512]{3,2,1,0:T(8,128)(2,1)S(1)} collective-permute-done((bf16[2,2,128,512]{3,2,1,0:T(8,128)(2,1)S(1)}, bf16[2,2,128,512]{3,2,1,0:T(8,128)(2,1)S(1)}, u32[]{:S(2)}, u32[]{:S(2)}) %collective-permute-start.10) | collective-permute-done | bytes 524320 | tf_op jit(solution)/shard_map/ppermute | solution.py:22
  98.6 16.9 %collective-permute-done.12 = bf16[2,2,128,512]{3,2,1,0:T(8,128)(2,1)S(1)} collective-permute-done((bf16[2,2,128,512]{3,2,1,0:T(8,128)(2,1)S(1)}, bf16[2,2,128,512]{3,2,1,0:T(8,128)(2,1)S(1)}, u32[]{:S(2)}, u32[]{:S(2)}) %collective-permute-start.12) | collective-permute-done | bytes 524320 | tf_op jit(solution)/shard_map/ppermute | solution.py:22
  116.2 13.1 %collective-permute-done.13 = bf16[2,2,128,512]{3,2,1,0:T(8,128)(2,1)S(1)} collective-permute-done((bf16[2,2,128,512]{3,2,1,0:T(8,128)(2,1)S(1)}, bf16[2,2,128,512]{3,2,1,0:T(8,128)(2,1)S(1)}, u32[]{:S(2)}, u32[]{:S(2)}) %collective-permute-start.13) | collective-permute-done | bytes 524320 | tf_op jit(solution)/shard_map/ppermute | solution.py:22
  133.8 10.3 %shard_map.264 = bf16[16,144,512]{2,1,0:T(8,128)(2,1)} custom-call(s32[16]{0:T(128)} %add.338.order_ref, bf16[16,144,512]{2,1,0:T(8,128)(2,1)} %bitcast.222), custom_call_target="tpu_custom_call" | custom-call | tf_op jit(solution)/shard_map/pallas_call | solution.py:288
  157.1 6.2 shard_map.265
  172.5 10.4 %shard_map.266 = (bf16[512,512]{1,0:T(8,128)(2,1)}, f32[4,2,512]{2,1,0:T(2,128)}) custom-call(bf16[1024,512]{1,0:T(8,128)(2,1)} %get-tuple-element.160.kn_ref, bf16[512,512]{1,0:T(8,128)(2,1)} %copy.93.qt_ref, bf16[512,1024]{1,0:T(8,128)(2,1)} %copy.94.vt_ref, f32[1024,1]{1,0:T(8,128)} %copy.95.bias_ref), custom_call_target="tpu_custom_call" | custom-call | tf_op jit(solution)/shard_map/pallas_call | solution.py:103
  185.3 4.2 broadcast_select_fusion.3
  192.1 3.5 collective-permute-start.20
  195.6 5.3 collective-permute-start.24
  205.0 14.8 %collective-permute-done.20 = bf16[1000,512]{1,0:T(8,128)(2,1)} collective-permute-done((bf16[1000,512]{1,0:T(8,128)(2,1)}, bf16[1000,512]{1,0:T(8,128)(2,1)}, u32[]{:S(2)}, u32[]{:S(2)}) %collective-permute-start.20) | collective-permute-done | bytes 1024032 | tf_op jit(solution)/shard_map/ppermute | solution.py:22
  220.1 21.2 %collective-permute-done.24 = bf16[1000,512]{1,0:T(8,128)(2,1)} collective-permute-done((bf16[1000,512]{1,0:T(8,128)(2,1)}, bf16[1000,512]{1,0:T(8,128)(2,1)}, u32[]{:S(2)}, u32[]{:S(2)}) %collective-permute-start.24) | collective-permute-done | bytes 1024032 | tf_op jit(solution)/shard_map/ppermute | solution.py:22
  241.5 43.6 %collective-permute-done.22 = bf16[1000,512]{1,0:T(8,128)(2,1)} collective-permute-done((bf16[1000,512]{1,0:T(8,128)(2,1)}, bf16[1000,512]{1,0:T(8,128)(2,1)}, u32[]{:S(2)}, u32[]{:S(2)}) %collective-permute-start.22) | collective-permute-done | bytes 1024032 | tf_op jit(solution)/shard_map/ppermute | solution.py:22
  299.2 10.8 %collective-permute-done.23 = bf16[1000,512]{1,0:T(8,128)(2,1)} collective-permute-done((bf16[1000,512]{1,0:T(8,128)(2,1)}, bf16[1000,512]{1,0:T(8,128)(2,1)}, u32[]{:S(2)}, u32[]{:S(2)}) %collective-permute-start.23) | collective-permute-done | bytes 1024032 | tf_op jit(solution)/shard_map/ppermute | solution.py:22
  322.7 7.5 shard_map.267
  330.3 7.5 shard_map.268
  337.8 7.7 shard_map.269
  345.5 7.6 shard_map.270
  357.3 2.9 copy.110.acc_in_ref
  363.5 13.1 %shard_map.271 = (bf16[2000,512]{1,0:T(8,128)(2,1)}, f32[512,1024]{1,0:T(8,128)}, f32[8,512]{1,0:T(8,128)}) custom-call(bf16[2000,512]{1,0:T(8,128)(2,1)} %constant_dynamic-update-slice_fusion.27.e_ref, bf16[512,1024]{1,0:T(8,128)(2,1)} %copy.108.ht_ref, bf16[1024,512]{1,0:T(8,128)(2,1)} %get-tuple-element.176.hn_ref, ...), custom_call_target="tpu_custom_call" | custom-call | tf_op jit(solution)/shard_map/pallas_call | solution.py:268
  376.6 13.2 %shard_map.272 = (bf16[2000,512]{1,0:T(8,128)(2,1)}, f32[512,1024]{1,0:T(8,128)}, f32[8,512]{1,0:T(8,128)}) custom-call(bf16[2000,512]{1,0:T(8,128)(2,1)} %copy-done.11, bf16[512,1024]{1,0:T(8,128)(2,1)} %copy.108.ht_ref, bf16[1024,512]{1,0:T(8,128)(2,1)} %get-tuple-element.176.hn_ref, f32[8,1024]{1,0:T(8,128)} %maximum_maximum_fusion.1.row_ref, ...), custom_call_target="tpu_custom_call" | custom-call | tf_op jit(solution)/shard_map/pallas_call | solution.py:268
  389.8 13.1 %shard_map.273 = (bf16[2000,512]{1,0:T(8,128)(2,1)}, f32[512,1024]{1,0:T(8,128)}, f32[8,512]{1,0:T(8,128)}) custom-call(bf16[2000,512]{1,0:T(8,128)(2,1)} %constant_dynamic-update-slice_fusion.23.e_ref, bf16[512,1024]{1,0:T(8,128)(2,1)} %copy.108.ht_ref, bf16[1024,512]{1,0:T(8,128)(2,1)} %get-tuple-element.176.hn_ref, ...), custom_call_target="tpu_custom_call" | custom-call | tf_op jit(solution)/shard_map/pallas_call | solution.py:268
  402.9 13.3 %shard_map.274 = (bf16[2000,512]{1,0:T(8,128)(2,1)}, f32[512,1024]{1,0:T(8,128)}, f32[8,512]{1,0:T(8,128)}) custom-call(bf16[2000,512]{1,0:T(8,128)(2,1)} %constant_dynamic-update-slice_fusion.21.e_ref, bf16[512,1024]{1,0:T(8,128)(2,1)} %copy.108.ht_ref, bf16[1024,512]{1,0:T(8,128)(2,1)} %get-tuple-element.176.hn_ref, ...), custom_call_target="tpu_custom_call" | custom-call | tf_op jit(solution)/shard_map/pallas_call | solution.py:268
  419.7 3.3 copy.114
  438.0 48.9 %collective-permute-done.31 = f32[8,128]{1,0:T(8,128)S(1)} collective-permute-done((f32[8,128]{1,0:T(8,128)S(1)}, f32[8,128]{1,0:T(8,128)S(1)}, u32[]{:S(2)}, u32[]{:S(2)}) %collective-permute-start.31) | collective-permute-done | bytes 4128 | tf_op jit(solution)/shard_map/ppermute | solution.py:22
  491.4 2.9 add_convert_fusion
  496.6 3.0 collective-permute-start.57
  503.7 3.2 collective-permute-start.33
  508.0 79.2 %collective-permute-done.33 = f32[8,128]{1,0:T(8,128)S(1)} collective-permute-done((f32[8,128]{1,0:T(8,128)S(1)}, f32[8,128]{1,0:T(8,128)S(1)}, u32[]{:S(2)}, u32[]{:S(2)}) %collective-permute-start.33) | collective-permute-done | bytes 4128 | tf_op jit(solution)/shard_map/ppermute | solution.py:22
  594.7 4.6 add_add_fusion
  599.3 3.1 multiply_reduce_fusion.1
  610.7 3.9 fusion.6
  659.4 5.2 collective-permute-done.50
  665.5 3.2 collective-permute-start.51
  668.7 7.1 collective-permute-done.52
  683.8 16.7 %shard_map.275 = (bf16[512,512]{1,0:T(8,128)(2,1)}, bf16[1024,512]{1,0:T(8,128)(2,1)}, bf16[1024,512]{1,0:T(8,128)(2,1)}) custom-call(bf16[1024,512]{1,0:T(8,128)(2,1)} %get-tuple-element.160.kn_ref, bf16[512,1024]{1,0:T(8,128)(2,1)} %copy.121.kt_ref, bf16[1024,512]{1,0:T(8,128)(2,1)} %get-tuple-element.157.vn_ref, bf16[512,512]{1,0:T(8,128)(2,1)} %copy.93.qt_ref, ...), custom_call_target="tpu_custom_call" | custom-call | tf_op jit(solution)/shard_map/pallas_call | solution.py:161
  711.9 9.7 %shard_map.276 = (bf16[512,512]{1,0:T(8,128)(2,1)}, bf16[512,512]{1,0:T(8,128)(2,1)}, bf16[512,512]{1,0:T(8,128)(2,1)}) custom-call(bf16[512,512]{1,0:T(8,128)(2,1)} %get-tuple-element.162.kn_ref, bf16[512,512]{1,0:T(8,128)(2,1)} %copy.127.kt_ref, bf16[512,512]{1,0:T(8,128)(2,1)} %get-tuple-element.163.vn_ref, bf16[512,512]{1,0:T(8,128)(2,1)} %copy.88.qt_ref, ...), custom_call_target="tpu_custom_call" | custom-call | tf_op jit(solution)/shard_map/pallas_call | solution.py:161
  723.7 4.0 fusion.88
  738.4 14.4 %maximum_maximum_fusion.block_ref = bf16[32,144,512]{2,1,0:T(8,128)(2,1)} fusion(bf16[16,16,512]{2,1,0:T(8,128)(2,1)S(1)} %pad_convert_fusion, bf16[16,32,512]{2,1,0:T(8,128)(2,1)S(1)} %bitcast.232, bf16[16,64,512]{2,1,0:T(8,128)(2,1)S(1)} %bitcast.241, bf16[16,32,512]{2,1,0:T(8,128)(2,1)S(1)} %bitcast.276, bf16[16,32,512]{2,1,0:T(8,128)(2,1)S(1)} %bitcast.233, ...), kind=kLoop, calls=%fused_computation.2 | loop fusion | flops 33030144 | bytes 9175040 | tf_op jit(solution)/shard_map/concatenate | solution.py:574
  752.7 6.1 shard_map.277
  769.5 3.3 collective-permute-done.44
  774.5 3.3 collective-permute-start.41
  779.3 7.6 collective-permute-done.41
  (545 shorter events, 252.8 us)
Async XLA Ops:
  6.3 16.2 %collective-permute-start.3 = (bf16[144,512]{1,0:T(8,128)(2,1)}, bf16[144,512]{1,0:T(8,128)(2,1)}, u32[]{:S(2)}, u32[]{:S(2)}) collective-permute-start(bf16[144,512]{1,0:T(8,128)(2,1)} %fusion.38), channel_id=1, source_target_pairs={{0,16},{4,20},{8,24},{12,28},{16,0},{20,4},{24,8},{28,12},{1,17},{... | collective-permute-start | bytes 442376 | tf_op jit(solution)/shard_map/ppermute | solution.py:22
  10.3 12.7 %collective-permute-start.1 = (bf16[144,512]{1,0:T(8,128)(2,1)}, bf16[144,512]{1,0:T(8,128)(2,1)}, u32[]{:S(2)}, u32[]{:S(2)}) collective-permute-start(bf16[144,512]{1,0:T(8,128)(2,1)} %fusion.38), channel_id=1, source_target_pairs={{0,8},{4,12},{8,0},{12,4},{16,24},{20,28},{24,16},{28,20},{1,9},{5... | collective-permute-start | bytes 442376 | tf_op jit(solution)/shard_map/ppermute | solution.py:22
  11.9 13.2 %collective-permute-start = (bf16[144,512]{1,0:T(8,128)(2,1)}, bf16[144,512]{1,0:T(8,128)(2,1)}, u32[]{:S(2)}, u32[]{:S(2)}) collective-permute-start(bf16[144,512]{1,0:T(8,128)(2,1)} %fusion.38), channel_id=1, source_target_pairs={{0,4},{4,0},{8,12},{12,8},{16,20},{20,16},{24,28},{28,24},{1,5},{5... | collective-permute-start | bytes 442376 | tf_op jit(solution)/shard_map/ppermute | solution.py:22
  13.4 11.1 %collective-permute-start.5 = (bf16[144,512]{1,0:T(8,128)(2,1)}, bf16[144,512]{1,0:T(8,128)(2,1)}, u32[]{:S(2)}, u32[]{:S(2)}) collective-permute-start(bf16[144,512]{1,0:T(8,128)(2,1)} %fusion.38), channel_id=1, source_target_pairs={{0,24},{4,28},{8,16},{12,20},{16,8},{20,12},{24,0},{28,4},{1,25},{... | collective-permute-start | bytes 442376 | tf_op jit(solution)/shard_map/ppermute | solution.py:22
  14.3 21.0 %collective-permute-start.16 = (f32[1,512]{1,0:T(1,128)S(1)}, f32[1,512]{1,0:T(1,128)S(1)}, u32[]{:S(2)}, u32[]{:S(2)}) collective-permute-start(f32[1,512]{1,0:T(1,128)S(1)} %convert_bitcast_fusion.2), channel_id=1, source_target_pairs={{0,2},{2,0},{1,3},{3,1},{4,6},{6,4},{5,7},{7,5},{8,10},{10,8},{9,1... | collective-permute-start | bytes 6152 | tf_op jit(solution)/shard_map/ppermute | solution.py:22
  32.7 24.3 %collective-permute-start.7 = (bf16[8,144,512]{2,1,0:T(8,128)(2,1)S(1)}, bf16[8,144,512]{2,1,0:T(8,128)(2,1)}, u32[]{:S(2)}, u32[]{:S(2)}) collective-permute-start(bf16[8,144,512]{2,1,0:T(8,128)(2,1)S(1)} %bitcast_dynamic-update-slice_fusion), channel_id=1, source_target_pairs={{0,2},{2,0},{1,3},{3,1},{4,6},{6,4},{5,7},{7,5},{8,10},{10,8},{9,1... | collective-permute-start | bytes 3538952 | tf_op jit(solution)/shard_map/ppermute | solution.py:22
  70.8 16.7 %collective-permute-start.14 = (bf16[2,2,128,512]{3,2,1,0:T(8,128)(2,1)S(1)}, bf16[2,2,128,512]{3,2,1,0:T(8,128)(2,1)S(1)}, u32[]{:S(2)}, u32[]{:S(2)}) collective-permute-start(bf16[2,2,128,512]{3,2,1,0:T(8,128)(2,1)S(1)} %pad_maximum_fusion.12), channel_id=1, source_target_pairs={{0,24},{4,28},{8,16},{12,20},{16,8},{20,12},{24,0},{28,4},{1,25},{... | collective-permute-start | bytes 1572872 | tf_op jit(solution)/shard_map/ppermute | solution.py:22
  74.3 23.5 %collective-permute-start.10 = (bf16[2,2,128,512]{3,2,1,0:T(8,128)(2,1)S(1)}, bf16[2,2,128,512]{3,2,1,0:T(8,128)(2,1)S(1)}, u32[]{:S(2)}, u32[]{:S(2)}) collective-permute-start(bf16[2,2,128,512]{3,2,1,0:T(8,128)(2,1)S(1)} %pad_maximum_fusion.12), channel_id=1, source_target_pairs={{0,8},{4,12},{8,0},{12,4},{16,24},{20,28},{24,16},{28,20},{1,9},{5... | collective-permute-start | bytes 1572872 | tf_op jit(solution)/shard_map/ppermute | solution.py:22
  80.3 18.2 %collective-permute-start.9 = (bf16[2,2,128,512]{3,2,1,0:T(8,128)(2,1)S(1)}, bf16[2,2,128,512]{3,2,1,0:T(8,128)(2,1)S(1)}, u32[]{:S(2)}, u32[]{:S(2)}) collective-permute-start(bf16[2,2,128,512]{3,2,1,0:T(8,128)(2,1)S(1)} %pad_maximum_fusion.12), channel_id=1, source_target_pairs={{0,4},{4,0},{8,12},{12,8},{16,20},{20,16},{24,28},{28,24},{1,5},{5... | collective-permute-start | bytes 1572872 | tf_op jit(solution)/shard_map/ppermute | solution.py:22
  81.8 33.6 %collective-permute-start.12 = (bf16[2,2,128,512]{3,2,1,0:T(8,128)(2,1)S(1)}, bf16[2,2,128,512]{3,2,1,0:T(8,128)(2,1)S(1)}, u32[]{:S(2)}, u32[]{:S(2)}) collective-permute-start(bf16[2,2,128,512]{3,2,1,0:T(8,128)(2,1)S(1)} %pad_maximum_fusion.12), channel_id=1, source_target_pairs={{0,16},{4,20},{8,24},{12,28},{16,0},{20,4},{24,8},{28,12},{1,17},{... | collective-permute-start | bytes 1572872 | tf_op jit(solution)/shard_map/ppermute | solution.py:22
  81.9 50.3 %collective-permute-start.8 = (bf16[8,2,144,512]{3,2,0,1:T(8,128)(2,1)S(1)}, bf16[8,2,144,512]{3,2,0,1:T(8,128)(2,1)S(1)}, u32[]{:S(2)}, u32[]{:S(2)}) collective-permute-start(bf16[8,2,144,512]{3,2,0,1:T(8,128)(2,1)S(1)} %pad_maximum_fusion.3), channel_id=1, source_target_pairs={{0,1},{1,0},{2,3},{3,2},{4,5},{5,4},{6,7},{7,6},{8,9},{9,8},{10,11... | collective-permute-start | bytes 7077896 | tf_op jit(solution)/shard_map/ppermute | solution.py:22
  87.5 41.9 %collective-permute-start.15 = (bf16[2,2,128,512]{3,2,1,0:T(8,128)(2,1)S(1)}, bf16[2,2,128,512]{3,2,1,0:T(8,128)(2,1)S(1)}, u32[]{:S(2)}, u32[]{:S(2)}) collective-permute-start(bf16[2,2,128,512]{3,2,1,0:T(8,128)(2,1)S(1)} %collective-permute-done.14), channel_id=1, source_target_pairs={{0,4},{4,0},{8,12},{12,8},{16,20},{20,16},{24,28},{28,24},{1,5},{5... | collective-permute-start | bytes 1572872 | tf_op jit(solution)/shard_map/ppermute | solution.py:22
  97.8 18.3 %collective-permute-start.11 = (bf16[2,2,128,512]{3,2,1,0:T(8,128)(2,1)S(1)}, bf16[2,2,128,512]{3,2,1,0:T(8,128)(2,1)S(1)}, u32[]{:S(2)}, u32[]{:S(2)}) collective-permute-start(bf16[2,2,128,512]{3,2,1,0:T(8,128)(2,1)S(1)} %collective-permute-done.10), channel_id=1, source_target_pairs={{0,4},{4,0},{8,12},{12,8},{16,20},{20,16},{24,28},{28,24},{1,5},{5... | collective-permute-start | bytes 1572872 | tf_op jit(solution)/shard_map/ppermute | solution.py:22
  115.5 13.8 %collective-permute-start.13 = (bf16[2,2,128,512]{3,2,1,0:T(8,128)(2,1)S(1)}, bf16[2,2,128,512]{3,2,1,0:T(8,128)(2,1)S(1)}, u32[]{:S(2)}, u32[]{:S(2)}) collective-permute-start(bf16[2,2,128,512]{3,2,1,0:T(8,128)(2,1)S(1)} %collective-permute-done.12), channel_id=1, source_target_pairs={{0,4},{4,0},{8,12},{12,8},{16,20},{20,16},{24,28},{28,24},{1,5},{5... | collective-permute-start | bytes 1572872 | tf_op jit(solution)/shard_map/ppermute | solution.py:22
  192.1 27.7 %collective-permute-start.20 = (bf16[1000,512]{1,0:T(8,128)(2,1)}, bf16[1000,512]{1,0:T(8,128)(2,1)}, u32[]{:S(2)}, u32[]{:S(2)}) collective-permute-start(bf16[1000,512]{1,0:T(8,128)(2,1)} %param.31), channel_id=1, source_target_pairs={{0,24},{4,28},{8,16},{12,20},{16,8},{20,12},{24,0},{28,4},{1,25},{... | collective-permute-start | bytes 3072008 | tf_op jit(solution)/shard_map/ppermute | solution.py:22
  195.6 45.6 %collective-permute-start.24 = (bf16[1000,512]{1,0:T(8,128)(2,1)}, bf16[1000,512]{1,0:T(8,128)(2,1)}, u32[]{:S(2)}, u32[]{:S(2)}) collective-permute-start(bf16[1000,512]{1,0:T(8,128)(2,1)} %param.31), channel_id=1, source_target_pairs={{0,8},{4,12},{8,0},{12,4},{16,24},{20,28},{24,16},{28,20},{1,9},{5... | collective-permute-start | bytes 3072008 | tf_op jit(solution)/shard_map/ppermute | solution.py:22
  200.9 84.2 %collective-permute-start.22 = (bf16[1000,512]{1,0:T(8,128)(2,1)}, bf16[1000,512]{1,0:T(8,128)(2,1)}, u32[]{:S(2)}, u32[]{:S(2)}) collective-permute-start(bf16[1000,512]{1,0:T(8,128)(2,1)} %param.31), channel_id=1, source_target_pairs={{0,16},{4,20},{8,24},{12,28},{16,0},{20,4},{24,8},{28,12},{1,17},{... | collective-permute-start | bytes 3072008 | tf_op jit(solution)/shard_map/ppermute | solution.py:22
  201.2 84.2 %collective-permute-start.18 = (bf16[512,512]{0,1:T(8,128)(2,1)S(1)}, bf16[512,512]{0,1:T(8,128)(2,1)S(1)}, u32[]{:S(2)}, u32[]{:S(2)}) collective-permute-start(bf16[512,512]{0,1:T(8,128)(2,1)S(1)} %add_convert_fusion.9), channel_id=1, source_target_pairs={{0,2},{2,0},{1,3},{3,1},{4,6},{6,4},{5,7},{7,5},{8,10},{10,8},{9,1... | collective-permute-start | bytes 1572872 | tf_op jit(solution)/shard_map/ppermute | solution.py:22
  202.5 93.1 %collective-permute-start.26 = (bf16[1000,512]{1,0:T(8,128)(2,1)}, bf16[1000,512]{1,0:T(8,128)(2,1)S(1)}, u32[]{:S(2)}, u32[]{:S(2)}) collective-permute-start(bf16[1000,512]{1,0:T(8,128)(2,1)} %param.31), channel_id=1, source_target_pairs={{0,4},{4,0},{8,12},{12,8},{16,20},{20,16},{24,28},{28,24},{1,5},{5... | collective-permute-start | bytes 3072008 | tf_op jit(solution)/shard_map/ppermute | solution.py:22
  219.8 77.1 %collective-permute-start.21 = (bf16[1000,512]{1,0:T(8,128)(2,1)}, bf16[1000,512]{1,0:T(8,128)(2,1)}, u32[]{:S(2)}, u32[]{:S(2)}) collective-permute-start(bf16[1000,512]{1,0:T(8,128)(2,1)} %collective-permute-done.20), channel_id=1, source_target_pairs={{0,4},{4,0},{8,12},{12,8},{16,20},{20,16},{24,28},{28,24},{1,5},{5... | collective-permute-start | bytes 3072008 | tf_op jit(solution)/shard_map/ppermute | solution.py:22
  241.2 71.1 %collective-permute-start.25 = (bf16[1000,512]{1,0:T(8,128)(2,1)}, bf16[1000,512]{1,0:T(8,128)(2,1)}, u32[]{:S(2)}, u32[]{:S(2)}) collective-permute-start(bf16[1000,512]{1,0:T(8,128)(2,1)} %collective-permute-done.24), channel_id=1, source_target_pairs={{0,4},{4,0},{8,12},{12,8},{16,20},{20,16},{24,28},{28,24},{1,5},{5... | collective-permute-start | bytes 3072008 | tf_op jit(solution)/shard_map/ppermute | solution.py:22
  285.1 24.9 %collective-permute-start.23 = (bf16[1000,512]{1,0:T(8,128)(2,1)}, bf16[1000,512]{1,0:T(8,128)(2,1)}, u32[]{:S(2)}, u32[]{:S(2)}) collective-permute-start(bf16[1000,512]{1,0:T(8,128)(2,1)} %collective-permute-done.22), channel_id=1, source_target_pairs={{0,4},{4,0},{8,12},{12,8},{16,20},{20,16},{24,28},{28,24},{1,5},{5... | collective-permute-start | bytes 3072008 | tf_op jit(solution)/shard_map/ppermute | solution.py:22
  286.5 28.4 %collective-permute-start.19 = (f32[512,512]{0,1:T(8,128)}, f32[512,512]{0,1:T(8,128)}, u32[]{:S(2)}, u32[]{:S(2)}) collective-permute-start(f32[512,512]{0,1:T(8,128)} %convert_add_fusion.1), channel_id=1, source_target_pairs={{0,1},{1,0},{2,3},{3,2},{4,5},{5,4},{6,7},{7,6},{8,9},{9,8},{10,11... | collective-permute-start | bytes 3145736 | tf_op jit(solution)/shard_map/ppermute | solution.py:22
  418.0 73.0 %collective-permute-start.60 = (bf16[1000,512]{1,0:T(8,128)(2,1)}, bf16[1000,512]{1,0:T(8,128)(2,1)}, u32[]{:S(2)}, u32[]{:S(2)}) collective-permute-start(bf16[1000,512]{1,0:T(8,128)(2,1)} %slice.517), channel_id=1, source_target_pairs={{0,4},{4,0},{8,12},{12,8},{16,20},{20,16},{24,28},{28,24},{1,5},{5... | collective-permute-start | bytes 3072008 | tf_op jit(solution)/shard_map/ppermute | solution.py:22
  425.4 63.2 %collective-permute-start.34 = (bf16[512,512]{0,1:T(8,128)(2,1)}, bf16[512,512]{0,1:T(8,128)(2,1)}, u32[]{:S(2)}, u32[]{:S(2)}) collective-permute-start(bf16[512,512]{0,1:T(8,128)(2,1)} %select_convert_fusion), channel_id=1, source_target_pairs={{0,1},{1,0},{2,3},{3,2},{4,5},{5,4},{6,7},{7,6},{8,9},{9,8},{10,11... | collective-permute-start | bytes 1572872 | tf_op jit(solution)/shard_map/ppermute | solution.py:22
  429.9 64.3 %collective-permute-start.56 = (bf16[1000,512]{1,0:T(8,128)(2,1)S(1)}, bf16[1000,512]{1,0:T(8,128)(2,1)S(1)}, u32[]{:S(2)}, u32[]{:S(2)}) collective-permute-start(bf16[1000,512]{1,0:T(8,128)(2,1)S(1)} %slice.513), channel_id=1, source_target_pairs={{0,4},{4,0},{8,12},{12,8},{16,20},{20,16},{24,28},{28,24},{1,5},{5... | collective-permute-start | bytes 3072008 | tf_op jit(solution)/shard_map/ppermute | solution.py:22
  431.3 65.3 %collective-permute-start.58 = (bf16[1000,512]{1,0:T(8,128)(2,1)S(1)}, bf16[1000,512]{1,0:T(8,128)(2,1)S(1)}, u32[]{:S(2)}, u32[]{:S(2)}) collective-permute-start(bf16[1000,512]{1,0:T(8,128)(2,1)S(1)} %slice.515), channel_id=1, source_target_pairs={{0,4},{4,0},{8,12},{12,8},{16,20},{20,16},{24,28},{28,24},{1,5},{5... | collective-permute-start | bytes 3072008 | tf_op jit(solution)/shard_map/ppermute | solution.py:22
  433.9 53.0 %collective-permute-start.31 = (f32[8,128]{1,0:T(8,128)S(1)}, f32[8,128]{1,0:T(8,128)S(1)}, u32[]{:S(2)}, u32[]{:S(2)}) collective-permute-start(f32[8,128]{1,0:T(8,128)S(1)} %fusion.118), channel_id=1, source_target_pairs={{0,4},{4,0},{8,12},{12,8},{16,20},{20,16},{24,28},{28,24},{1,5},{5... | collective-permute-start | bytes 12296 | tf_op jit(solution)/shard_map/ppermute | solution.py:22
  486.9 107.7 %collective-permute-start.62 = (bf16[1000,512]{1,0:T(8,128)(2,1)}, bf16[1000,512]{1,0:T(8,128)(2,1)}, u32[]{:S(2)}, u32[]{:S(2)}) collective-permute-start(bf16[1000,512]{1,0:T(8,128)(2,1)} %slice.519), channel_id=1, source_target_pairs={{0,4},{4,0},{8,12},{12,8},{16,20},{20,16},{24,28},{28,24},{1,5},{5... | collective-permute-start | bytes 3072008 | tf_op jit(solution)/shard_map/ppermute | solution.py:22
  488.7 12.2 %collective-permute-start.32 = (f32[8,128]{1,0:T(8,128)S(1)}, f32[8,128]{1,0:T(8,128)S(1)}, u32[]{:S(2)}, u32[]{:S(2)}) collective-permute-start(f32[8,128]{1,0:T(8,128)S(1)} %add.380), channel_id=1, source_target_pairs={{0,8},{4,12},{8,0},{12,4},{16,24},{20,28},{24,16},{28,20},{1,9},{5... | collective-permute-start | bytes 12296 | tf_op jit(solution)/shard_map/ppermute | solution.py:22
  491.0 12.7 %collective-permute-start.35 = (bf16[512,512]{0,1:T(8,128)(2,1)S(1)}, bf16[512,512]{0,1:T(8,128)(2,1)S(1)}, u32[]{:S(2)}, u32[]{:S(2)}) collective-permute-start(bf16[512,512]{0,1:T(8,128)(2,1)S(1)} %add_convert_fusion.6), channel_id=1, source_target_pairs={{0,2},{2,0},{1,3},{3,1},{4,6},{6,4},{5,7},{7,5},{8,10},{10,8},{9,1... | collective-permute-start | bytes 1572872 | tf_op jit(solution)/shard_map/ppermute | solution.py:22
  494.2 100.4 %collective-permute-start.61 = (bf16[1000,512]{1,0:T(8,128)(2,1)}, bf16[1000,512]{1,0:T(8,128)(2,1)}, u32[]{:S(2)}, u32[]{:S(2)}) collective-permute-start(bf16[1000,512]{1,0:T(8,128)(2,1)} %add_convert_fusion), channel_id=1, source_target_pairs={{0,8},{4,12},{8,0},{12,4},{16,24},{20,28},{24,16},{28,20},{1,9},{5... | collective-permute-start | bytes 3072008 | tf_op jit(solution)/shard_map/ppermute | solution.py:22
  496.6 98.0 %collective-permute-start.57 = (bf16[1000,512]{1,0:T(8,128)(2,1)}, bf16[1000,512]{1,0:T(8,128)(2,1)}, u32[]{:S(2)}, u32[]{:S(2)}) collective-permute-start(bf16[1000,512]{1,0:T(8,128)(2,1)} %add_convert_fusion.2), channel_id=1, source_target_pairs={{0,16},{4,20},{8,24},{12,28},{16,0},{20,4},{24,8},{28,12},{1,17},{... | collective-permute-start | bytes 3072008 | tf_op jit(solution)/shard_map/ppermute | solution.py:22
  500.9 93.8 %collective-permute-start.59 = (bf16[1000,512]{1,0:T(8,128)(2,1)}, bf16[1000,512]{1,0:T(8,128)(2,1)}, u32[]{:S(2)}, u32[]{:S(2)}) collective-permute-start(bf16[1000,512]{1,0:T(8,128)(2,1)} %add_convert_fusion.1), channel_id=1, source_target_pairs={{0,24},{4,28},{8,16},{12,20},{16,8},{20,12},{24,0},{28,4},{1,25},{... | collective-permute-start | bytes 3072008 | tf_op jit(solution)/shard_map/ppermute | solution.py:22
  503.7 83.5 %collective-permute-start.33 = (f32[8,128]{1,0:T(8,128)S(1)}, f32[8,128]{1,0:T(8,128)S(1)}, u32[]{:S(2)}, u32[]{:S(2)}) collective-permute-start(f32[8,128]{1,0:T(8,128)S(1)} %add.381), channel_id=1, source_target_pairs={{0,16},{4,20},{8,24},{12,28},{16,0},{20,4},{24,8},{28,12},{1,17},{... | collective-permute-start | bytes 12296 | tf_op jit(solution)/shard_map/ppermute | solution.py:22
  587.3 12.0 %collective-permute-start.36 = (f32[512,512]{0,1:T(8,128)}, f32[512,512]{0,1:T(8,128)}, u32[]{:S(2)}, u32[]{:S(2)}) collective-permute-start(f32[512,512]{0,1:T(8,128)} %convert_add_fusion), channel_id=1, source_target_pairs={{0,1},{1,0},{2,3},{3,2},{4,5},{5,4},{6,7},{7,6},{8,9},{9,8},{10,11... | collective-permute-start | bytes 3145736 | tf_op jit(solution)/shard_map/ppermute | solution.py:22
  628.7 28.7 %collective-permute-start.48 = (bf16[2,2,128,512]{2,3,1,0:T(8,128)(2,1)}, bf16[2,2,128,512]{2,3,1,0:T(8,128)(2,1)}, u32[]{:S(2)}, u32[]{:S(2)}) collective-permute-start(bf16[2,2,128,512]{2,3,1,0:T(8,128)(2,1)} %pad_maximum_fusion.13), channel_id=1, source_target_pairs={{0,4},{4,0},{8,12},{12,8},{16,20},{20,16},{24,28},{28,24},{1,5},{5... | collective-permute-start | bytes 1572872 | tf_op jit(solution)/shard_map/ppermute | solution.py:22
  630.2 26.1 %collective-permute-start.38 = (bf16[512,256]{0,1:T(8,128)(2,1)S(1)}, bf16[512,256]{0,1:T(8,128)(2,1)}, u32[]{:S(2)}, u32[]{:S(2)}) collective-permute-start(bf16[512,256]{0,1:T(8,128)(2,1)S(1)} %add_convert_fusion.12), channel_id=1, source_target_pairs={{0,2},{2,0},{1,3},{3,1},{4,6},{6,4},{5,7},{7,5},{8,10},{10,8},{9,1... | collective-permute-start | bytes 786440 | tf_op jit(solution)/shard_map/ppermute | solution.py:22
  649.5 15.1 %collective-permute-start.50 = (bf16[2,2,128,512]{2,3,1,0:T(8,128)(2,1)}, bf16[2,2,128,512]{2,3,1,0:T(8,128)(2,1)S(1)}, u32[]{:S(2)}, u32[]{:S(2)}) collective-permute-start(bf16[2,2,128,512]{2,3,1,0:T(8,128)(2,1)} %pad_maximum_fusion.14), channel_id=1, source_target_pairs={{0,4},{4,0},{8,12},{12,8},{16,20},{20,16},{24,28},{28,24},{1,5},{5... | collective-permute-start | bytes 1572872 | tf_op jit(solution)/shard_map/ppermute | solution.py:22
  652.3 23.5 %collective-permute-start.52 = (bf16[2,2,128,512]{2,3,1,0:T(8,128)(2,1)S(1)}, bf16[2,2,128,512]{2,3,1,0:T(8,128)(2,1)S(1)}, u32[]{:S(2)}, u32[]{:S(2)}) collective-permute-start(bf16[2,2,128,512]{2,3,1,0:T(8,128)(2,1)S(1)} %pad_maximum_fusion.15), channel_id=1, source_target_pairs={{0,4},{4,0},{8,12},{12,8},{16,20},{20,16},{24,28},{28,24},{1,5},{5... | collective-permute-start | bytes 1572872 | tf_op jit(solution)/shard_map/ppermute | solution.py:22
  654.6 109.7 %collective-permute-start.54 = (bf16[2,2,128,512]{2,3,1,0:T(8,128)(2,1)}, bf16[2,2,128,512]{2,3,1,0:T(8,128)(2,1)}, u32[]{:S(2)}, u32[]{:S(2)}) collective-permute-start(bf16[2,2,128,512]{2,3,1,0:T(8,128)(2,1)} %pad_maximum_fusion.16), channel_id=1, source_target_pairs={{0,4},{4,0},{8,12},{12,8},{16,20},{20,16},{24,28},{28,24},{1,5},{5... | collective-permute-start | bytes 1572872 | tf_op jit(solution)/shard_map/ppermute | solution.py:22
  657.3 19.9 %collective-permute-start.39 = (f32[512,256]{0,1:T(8,128)S(1)}, f32[512,256]{0,1:T(8,128)S(1)}, u32[]{:S(2)}, u32[]{:S(2)}) collective-permute-start(f32[512,256]{0,1:T(8,128)S(1)} %convert_add_fusion.2), channel_id=1, source_target_pairs={{0,1},{1,0},{2,3},{3,2},{4,5},{5,4},{6,7},{7,6},{8,9},{9,8},{10,11... | collective-permute-start | bytes 1572872 | tf_op jit(solution)/shard_map/ppermute | solution.py:22
  659.4 105.3 %collective-permute-start.49 = (bf16[2,2,128,512]{2,3,1,0:T(8,128)(2,1)}, bf16[2,2,128,512]{2,3,1,0:T(8,128)(2,1)}, u32[]{:S(2)}, u32[]{:S(2)}) collective-permute-start(bf16[2,2,128,512]{2,3,1,0:T(8,128)(2,1)} %add_convert_fusion.5), channel_id=1, source_target_pairs={{0,16},{4,20},{8,24},{12,28},{16,0},{20,4},{24,8},{28,12},{1,17},{... | collective-permute-start | bytes 1572872 | tf_op jit(solution)/shard_map/ppermute | solution.py:22
  665.5 100.8 %collective-permute-start.51 = (bf16[2,2,128,512]{2,3,1,0:T(8,128)(2,1)}, bf16[2,2,128,512]{2,3,1,0:T(8,128)(2,1)}, u32[]{:S(2)}, u32[]{:S(2)}) collective-permute-start(bf16[2,2,128,512]{2,3,1,0:T(8,128)(2,1)} %add_convert_fusion.4), channel_id=1, source_target_pairs={{0,24},{4,28},{8,16},{12,20},{16,8},{20,12},{24,0},{28,4},{1,25},{... | collective-permute-start | bytes 1572872 | tf_op jit(solution)/shard_map/ppermute | solution.py:22
  676.8 89.9 %collective-permute-start.53 = (bf16[2,2,128,512]{2,3,1,0:T(8,128)(2,1)}, bf16[2,2,128,512]{2,3,1,0:T(8,128)(2,1)}, u32[]{:S(2)}, u32[]{:S(2)}) collective-permute-start(bf16[2,2,128,512]{2,3,1,0:T(8,128)(2,1)} %add_convert_fusion.3), channel_id=1, source_target_pairs={{0,8},{4,12},{8,0},{12,4},{16,24},{20,28},{24,16},{28,20},{1,9},{5... | collective-permute-start | bytes 1572872 | tf_op jit(solution)/shard_map/ppermute | solution.py:22
  764.3 15.0 %collective-permute-start.46 = (bf16[144,512]{1,0:T(8,128)(2,1)S(1)}, bf16[144,512]{1,0:T(8,128)(2,1)S(1)}, u32[]{:S(2)}, u32[]{:S(2)}) collective-permute-start(bf16[144,512]{1,0:T(8,128)(2,1)S(1)} %get-tuple-element.171), channel_id=1, source_target_pairs={{0,4},{4,0},{8,12},{12,8},{16,20},{20,16},{24,28},{28,24},{1,5},{5... | collective-permute-start | bytes 442376 | tf_op jit(solution)/shard_map/ppermute | solution.py:22
  769.5 23.2 %collective-permute-start.55 = (f32[2,2,128,512]{2,3,1,0:T(8,128)}, f32[2,2,128,512]{2,3,1,0:T(8,128)}, u32[]{:S(2)}, u32[]{:S(2)}) collective-permute-start(f32[2,2,128,512]{2,3,1,0:T(8,128)} %add_add_fusion.1), channel_id=1, source_target_pairs={{0,1},{1,0},{2,3},{3,2},{4,5},{5,4},{6,7},{7,6},{8,9},{9,8},{10,11... | collective-permute-start | bytes 3145736 | tf_op jit(solution)/shard_map/ppermute | solution.py:22
  774.5 12.4 %collective-permute-start.41 = (bf16[144,512]{1,0:T(8,128)(2,1)S(1)}, bf16[144,512]{1,0:T(8,128)(2,1)S(1)}, u32[]{:S(2)}, u32[]{:S(2)}) collective-permute-start(bf16[144,512]{1,0:T(8,128)(2,1)S(1)} %get-tuple-element.167), channel_id=1, source_target_pairs={{0,16},{4,20},{8,24},{12,28},{16,0},{20,4},{24,8},{28,12},{1,17},{... | collective-permute-start | bytes 442376 | tf_op jit(solution)/shard_map/ppermute | solution.py:22
  (103 other events, 1020.1 us)

commit v2 on v1

v2 whole, which is shorter than its diff:
```python
import functools

import jax
import jax.numpy as jnp
from jax import lax
from jax.experimental import pallas as pl
from jax.experimental.pallas import tpu as pltpu
from jax.sharding import PartitionSpec as P

HEADS = 8
VOCAB = 32000
GROUPS = 4
EPSILON = 1e-05
SMOOTH = 0.1
F32 = jnp.float32
BF16 = jnp.bfloat16
PARAMS = pltpu.CompilerParams(vmem_limit_bytes=56 * 1024 * 1024)
COST = pl.CostEstimate(flops=1000, bytes_accessed=1000, transcendentals=0)


def swap(block, axis, mask):
    count = lax.axis_size(axis)
    return lax.ppermute(block, axis, [(i, i ^ mask) for i in range(count)])


def after(value, mark):
    return value if mark is None else lax.optimization_barrier((value, mark))[0]


class Gather:
    def __init__(self, block, axis):
        self.block, self.axis, self.count = block, axis, lax.axis_size(axis)
        self.near, self.far = {}, {0: block}

    def send(self, steps, mark=None):
        if self.count == 8:
            block = after(self.block, mark)
            for g in steps:
                self.far[g] = swap(block, self.axis, 2 * g)

    def forward(self, steps, mark=None):
        if self.count == 8:
            for g in steps:
                self.near[g] = swap(after(self.far[g], mark), self.axis, 1)

    def forward_together(self, steps, mark=None):
        if self.count == 8:
            sent = swap(jnp.stack([after(self.far[g], mark) for g in steps]), self.axis, 1)
            for n, g in enumerate(steps):
                self.near[g] = sent[n]

    def arrived(self, far=(), near=()):
        return [self.far[g] for g in far] + [self.near[g] for g in near] if self.count == 8 else None

    def mark(self, g):
        return self.far[g] if self.count == 8 else None

    def result(self):
        if self.count == 8:
            return [part for g in range(4) for part in (self.far[g], self.near[g])]
        blocks, step = [self.block], 1
        while step < self.count:
            blocks = blocks + [swap(part, self.axis, step) for part in blocks]
            step *= 2
        return blocks


class ScatterSum:
    def __init__(self, axis):
        self.axis = axis
        self.count = lax.axis_size(axis)
        self.blocks, self.near, self.far, self.kept = {}, {}, {}, None

    def give(self, groups, fars, nears, split=0, mark=None):
        per_half = self.count // (2 * GROUPS)
        if self.count == 8:
            sent = swap(after(nears, mark), self.axis, 1)
        for n, g in enumerate(groups):
            if self.count == 8:
                self.blocks[2 * g], self.near[g] = fars[n], (sent, n)
                continue
            for half, array in enumerate((fars[n], nears[n])):
                for k, piece in enumerate(jnp.split(array, per_half, axis=split)):
                    self.blocks[(2 * g + half) * per_half + k] = piece

    def forward(self, groups, mark=None):
        if self.count == 8:
            for g in groups:
                sent, n = self.near[g]
                part = self.blocks[2 * g].astype(F32) + after(sent, mark)[n].astype(F32)
                if g:
                    self.far[g] = swap(part.astype(BF16), self.axis, 2 * g)
                else:
                    self.kept = part

    def arrived(self, far=(), near=()):
        return [self.far[g] for g in far] + [self.near[g][0] for g in near] if self.count == 8 else None

    def result(self, mark=None):
        if self.count == 8:
            total = self.kept
            for g in (1, 2, 3):
                total = total + after(self.far[g], mark).astype(F32)
            return total
        blocks = [self.blocks[k] for k in range(self.count)]
        step = self.count // 2
        while step >= 1:
            blocks = [
                blocks[k].astype(F32) + swap(blocks[k + step].astype(BF16), self.axis, step).astype(F32)
                for k in range(step)
            ]
            step //= 2
        return blocks[0]


def dot(left, right):
    return jnp.dot(left, right, preferred_element_type=F32)


def dot_nt(left, right):
    return lax.dot_general(left, right, (((1,), (1,)), ((), ())), preferred_element_type=F32)


def dot_tn(left, right):
    return lax.dot_general(left, right, (((0,), (0,)), ((), ())), preferred_element_type=F32)


def call(kernel, outs, *args, scalars=None, scratch=()):
    specs = [pl.BlockSpec(memory_space=pltpu.VMEM)] * len(args)
    if scalars is not None:
        specs = [pl.BlockSpec(memory_space=pltpu.SMEM)] + specs
        args = (scalars,) + args
    return pl.pallas_call(
        kernel,
        in_specs=specs,
        out_specs=[pl.BlockSpec(memory_space=pltpu.VMEM)] * len(outs),
        out_shape=[jax.ShapeDtypeStruct(shape, dtype) for shape, dtype in outs],
        scratch_shapes=[pltpu.VMEM(shape, dtype) for shape, dtype in scratch],
        compiler_params=PARAMS,
        cost_estimate=COST,
    )(*args)


def by_core(flag_ref, low_ref, high_ref, mine, other):
    @pl.when(flag_ref[0] == 0)
    def _():
        low_ref[...], high_ref[...] = mine, other

    @pl.when(flag_ref[0] != 0)
    def _():
        low_ref[...], high_ref[...] = other, mine


def pair_parts(value, h):
    head = value.shape[0] // 2
    rows = value[h * head : (h + 1) * head]
    zeros = jnp.zeros_like(rows)
    return rows, jnp.concatenate([zeros, rows] if h else [rows, zeros], axis=0)


def pair_rows(j, size, start=0):
    return pl.ds(pl.multiple_of(start + j * size, size), size)


def norm_forward(values, gain, bias):
    average = jnp.mean(values, axis=0, keepdims=True)
    centered = values - average
    scale = lax.rsqrt(jnp.mean(centered * centered, axis=0, keepdims=True) + EPSILON)
    return centered * scale * gain + bias


def norm_backward(values, gain, upstream):
    average = jnp.mean(values, axis=0, keepdims=True)
    centered = values - average
    scale = lax.rsqrt(jnp.mean(centered * centered, axis=0, keepdims=True) + EPSILON)
    unit = centered * scale
    grad = upstream * gain
    result = scale * (
        grad - jnp.mean(grad, axis=0, keepdims=True) - unit * jnp.mean(grad * unit, axis=0, keepdims=True)
    )
    return result, jnp.sum(upstream * unit, axis=1, keepdims=True), jnp.sum(upstream, axis=1, keepdims=True)


def norm_columns(j, gain_grad, bias_grad, width):
    lanes = lax.broadcasted_iota(jnp.int32, (gain_grad.shape[0], width), 1)
    return jnp.where(lanes == j, gain_grad, 0.0) + jnp.where(lanes == 4 + j, bias_grad, 0.0)


def column(norms_ref, j):
    return norms_ref[:, j : j + 1].astype(F32)


def causal_mask(tokens):
    shape = (tokens, tokens)
    return lax.broadcasted_iota(jnp.int32, shape, 0) <= lax.broadcasted_iota(jnp.int32, shape, 1)


def heads_forward(query, keys_n, value_t, masked, out_ref, lse_ref, j):
    head = query.shape[0] // 2
    for h in range(2):
        s = masked(dot(keys_n, pair_parts(query, h)[1]))
        m = jnp.max(s, axis=0, keepdims=True)
        e = jnp.exp(s - m)
        total = jnp.sum(e, axis=0, keepdims=True)
        p = (e * (1.0 / total)).astype(BF16)
        out_ref[pair_rows(2 * j + h, head), :] = dot(value_t[h * head : (h + 1) * head], p).astype(BF16)
        lse_ref[j, h : h + 1, :] = m + jnp.log(total)


def heads_backward(query, key_t, keys_n, values_n, upstream, lse, masked):
    head = query.shape[0] // 2
    dq, dk, dv = [], 0.0, 0.0
    for h in range(2):
        q_pad = pair_parts(query, h)[1]
        do_pad = pair_parts(upstream, h)[1]
        p = jnp.exp(masked(dot(keys_n, q_pad)) - lse[h : h + 1, :])
        pdp = p * dot(values_n, do_pad)
        total = jnp.sum(pdp, axis=0, keepdims=True)
        ds = (pdp - p * total).astype(BF16)
        dq.append(dot(pair_parts(key_t, h)[0], ds) * head**-0.5)
        dk = dk + dot(ds, q_pad.T)
        dv = dv + dot(p.astype(BF16), do_pad.T)
    return jnp.concatenate(dq, axis=0).astype(BF16), dk.astype(BF16), dv.astype(BF16)


def self_forward_kernel(
    x_ref, norms_ref, project_ref, output_ref, query_ref, a1_ref, qkv_ref, att_ref, lse_ref, h1_ref, a2_ref, cross_ref
):
    tokens, width = x_ref.shape
    pair = 2 * width // HEADS
    scale = jnp.asarray((pair // 2) ** -0.5, BF16)
    a1_ref[...] = norm_forward(x_ref[...].T.astype(F32), column(norms_ref, 0), column(norms_ref, 4)).astype(BF16)
    qkv_ref[...] = dot(project_ref[...], a1_ref[...]).astype(BF16)

    def step(j, carry):
        allowed = causal_mask(tokens)
        heads_forward(
            qkv_ref[pair_rows(j, pair), :] * scale,
            qkv_ref[pair_rows(j, pair, width), :].T,
            qkv_ref[pair_rows(j, pair, 2 * width), :],
            lambda s: jnp.where(allowed, s, -1e30),
            att_ref,
            lse_ref,
            j,
        )
        return carry

    lax.fori_loop(0, HEADS // 2, step, 0)
    h1_ref[...] = x_ref[...].T.astype(F32) + dot(output_ref[...], att_ref[...])
    a2_ref[...] = norm_forward(h1_ref[...], column(norms_ref, 1), column(norms_ref, 5)).astype(BF16)
    cross_ref[...] = dot(query_ref[...], a2_ref[...]).astype(BF16) * scale


def self_forward(x, norms, project, output, query):
    tokens, width = x.shape
    bf = ((width, tokens), BF16)
    return call(
        self_forward_kernel,
        [bf, ((3 * width, tokens), BF16), bf, ((HEADS // 2, 2, tokens), F32), ((width, tokens), F32), bf, bf],
        *(x, norms, project, output, query),
    )


def memory_keys_kernel(memory_ref, weight_ref, out_ref):
    out_ref[...] = dot_nt(memory_ref[...], weight_ref[...]).astype(BF16)


def cross_forward_kernel(
    cross_ref, kv_ref, bias_ref, h1_ref, norms_ref, output_ref, att_ref, lse_ref, h2_ref, a3_ref, an_ref
):
    width = cross_ref.shape[0]
    pair = 2 * width // HEADS

    def step(j, carry):
        heads_forward(
            cross_ref[pair_rows(j, pair), :],
            kv_ref[:, pair_rows(j, pair)],
            kv_ref[:, pair_rows(j, pair, width)].T,
            lambda s: s + bias_ref[...],
            att_ref,
            lse_ref,
            j,
        )
        return carry

    lax.fori_loop(0, HEADS // 2, step, 0)
    h2_ref[...] = h1_ref[...] + dot(output_ref[...], att_ref[...])
    a3_ref[...] = norm_forward(h2_ref[...], column(norms_ref, 2), column(norms_ref, 6)).astype(BF16)
    an_ref[...] = a3_ref[...].T


def cross_forward(cross, kv, bias, h1, norms, output):
    width, tokens = cross.shape
    bf = ((width, tokens), BF16)
    return call(
        cross_forward_kernel,
        [bf, ((HEADS // 2, 2, tokens), F32), ((width, tokens), F32), bf, ((tokens, width), BF16)],
        *(cross, kv, bias, h1, norms, output),
    )


def final_norm_kernel(
    flags_ref, h2_ref, part_ref, other_ref, last_ref, norms_ref, weight_ref, b0_ref, b1_ref, ft_ref, fn_ref, out_ref, flat_ref
):
    tokens = h2_ref.shape[1]
    other = jnp.concatenate([other_ref[...], last_ref[...]], axis=0)
    by_core(flags_ref, b0_ref, b1_ref, h2_ref[...] + part_ref[...], h2_ref[...] + other)
    for p, ref in enumerate((b0_ref, b1_ref)):
        final = norm_forward(ref[...], column(norms_ref, 3), column(norms_ref, 7)).astype(BF16)
        ft_ref[:, p * tokens : (p + 1) * tokens] = final
        fn_ref[p * tokens : (p + 1) * tokens, :] = final.T

        @pl.when(flags_ref[1] == p)
        def _():
            out_ref[...] = ref[...].T

    flat_ref[...] = dot(weight_ref[...], fn_ref[...]) * (-SMOOTH / VOCAB)


def final_norm(flags, h2, part, other, norms, weight):
    width, tokens = h2.shape
    full = ((width, tokens), F32)
    return call(
        final_norm_kernel,
        [full, full, ((width, 2 * tokens), BF16), ((2 * tokens, width), BF16), ((tokens, width), F32), ((8, width), F32)],
        *(h2, part, *other, norms, weight),
        scalars=flags,
    )


def final_back_kernel(
    flags_ref, b0_ref, b1_ref, part_ref, other_ref, last_ref, norms_ref, db_ref, dy_ref, dn_ref, cols_ref, d0_ref, d1_ref
):
    tokens = b0_ref.shape[1]
    other = jnp.concatenate([other_ref[...], last_ref[...]], axis=0)
    by_core(flags_ref, d0_ref, d1_ref, part_ref[...], other)
    total, cols = 0.0, 0.0
    for p, (block_ref, d_ref) in enumerate(((b0_ref, d0_ref), (b1_ref, d1_ref))):
        grad, *norm_grads = norm_backward(block_ref[...], column(norms_ref, 3), d_ref[...])
        low = grad.astype(BF16)
        dy_ref[:, p * tokens : (p + 1) * tokens] = low
        dn_ref[p * tokens : (p + 1) * tokens, :] = low.T
        total, cols = total + grad, cols + norm_columns(3, *norm_grads, cols_ref.shape[1])
    db_ref[...], cols_ref[...] = total, cols


def final_back(flags, b0, b1, part, other, norms):
    width, tokens = b0.shape
    full = ((width, tokens), F32)
    return call(
        final_back_kernel,
        [full, ((width, 2 * tokens), BF16), ((2 * tokens, width), BF16), ((width, norms.shape[1]), F32)],
        *(b0, b1, part, *other, norms),
        scalars=flags,
        scratch=[full, full],
    )


def cross_back_kernel(
    flags_ref,
    db_ref,
    mine_ref,
    other_ref,
    last_ref,
    h2_ref,
    norms_ref,
    cols_in_ref,
    output_ref,
    att_ref,
    cross_ref,
    kv_ref,
    lse_ref,
    bias_ref,
    a2_ref,
    query_ref,
    h1_ref,
    dh1_ref,
    out_grad_ref,
    query_grad_ref,
    dkv_ref,
    cols_ref,
    d_ref,
    do_ref,
    dq_ref,
):
    width, tokens = h2_ref.shape
    pair, half = 2 * width // HEADS, tokens // 2
    other = jnp.concatenate([other_ref[...], last_ref[...]], axis=0)
    by_core(flags_ref, d_ref.at[:, :half], d_ref.at[:, half:], mine_ref[...], other)
    grad, *two = norm_backward(h2_ref[...], column(norms_ref, 2), d_ref[...])
    d_ref[...] = db_ref[...] + grad
    low = d_ref[...].astype(BF16)
    out_grad_ref[...] = dot_nt(low, att_ref[...]).astype(BF16)
    do_ref[...] = dot_tn(output_ref[...], low).astype(BF16)

    def step(j, carry):
        rows, keys, values = pair_rows(j, pair), pair_rows(j, pair), pair_rows(j, pair, width)
        dq, dk, dv = heads_backward(
            cross_ref[rows, :],
            kv_ref[:, keys].T,
            kv_ref[:, keys],
            kv_ref[:, values],
            do_ref[rows, :],
            lse_ref[j],
            lambda s: s + bias_ref[...],
        )
        dq_ref[rows, :], dkv_ref[:, keys], dkv_ref[:, values] = dq, dk, dv
        return carry

    lax.fori_loop(0, HEADS // 2, step, 0)
    query_grad_ref[...] = dot_nt(dq_ref[...], a2_ref[...]).astype(BF16)
    grad, *one = norm_backward(h1_ref[...], column(norms_ref, 1), dot_tn(query_ref[...], dq_ref[...]))
    dh1_ref[...] = d_ref[...] + grad
    columns = cols_ref.shape[1]
    cols_ref[...] = cols_in_ref[...] + norm_columns(2, *two, columns) + norm_columns(1, *one, columns)


def cross_back(flags, *args):
    h2, norms, kv = args[4], args[5], args[10]
    width, tokens = h2.shape
    full, bf = ((width, tokens), F32), ((width, tokens), BF16)
    square = ((width, width), BF16)
    return call(
        cross_back_kernel,
        [full, square, square, (kv.shape, BF16), (norms.shape, F32)],
        *args,
        scalars=flags,
        scratch=[full, bf, bf],
    )


def memory_back_kernel(dkv_ref, memory_ref, weight_ref, weight_grad_ref, memory_grad_ref):
    weight_grad_ref[...] = dot_tn(dkv_ref[...], memory_ref[...]).astype(BF16)
    memory_grad_ref[...] = dot(dkv_ref[...], weight_ref[...])


def self_back_kernel(
    dh1_ref, output_ref, att_ref, qkv_ref, lse_ref, a1_ref, x_ref, project_ref, norms_ref, cols_ref,
    out_grad_ref, project_grad_ref, inputs_grad_ref, norm_grad_ref, do_ref, dqkv_ref
):
    width, tokens = dh1_ref.shape
    pair = 2 * width // HEADS
    scale = jnp.asarray((pair // 2) ** -0.5, BF16)
    low = dh1_ref[...].astype(BF16)
    out_grad_ref[...] = dot_nt(low, att_ref[...]).astype(BF16)
    do_ref[...] = dot_tn(output_ref[...], low).astype(BF16)

    def step(j, carry):
        allowed = causal_mask(tokens)
        rows, keys, values = pair_rows(j, pair), pair_rows(j, pair, width), pair_rows(j, pair, 2 * width)
        key_t = qkv_ref[keys, :]
        dq, dk, dv = heads_backward(
            qkv_ref[rows, :] * scale,
            key_t,
            key_t.T,
            qkv_ref[values, :].T,
            do_ref[rows, :],
            lse_ref[j],
            lambda s: jnp.where(allowed, s, -1e30),
        )
        dqkv_ref[rows, :], dqkv_ref[keys, :], dqkv_ref[values, :] = dq, dk.T, dv.T
        return carry

    lax.fori_loop(0, HEADS // 2, step, 0)
    project_grad_ref[...] = dot_nt(dqkv_ref[...], a1_ref[...]).astype(BF16)
    grad, *zero = norm_backward(
        x_ref[...].T.astype(F32), column(norms_ref, 0), dot_tn(project_ref[...], dqkv_ref[...])
    )
    inputs_grad_ref[...] = (dh1_ref[...] + grad).T
    columns = cols_ref.shape[1]
    norm_grad_ref[...] = jnp.zeros(norm_grad_ref.shape, BF16)
    norm_grad_ref[:, :columns] = (cols_ref[...] + norm_columns(0, *zero, columns)).astype(BF16)


def self_back(*args):
    width, tokens = args[0].shape
    square = ((width, width), BF16)
    return call(
        self_back_kernel,
        [square, ((3 * width, width), BF16), ((tokens, width), F32), square],
        *args,
        scratch=[((width, tokens), BF16), ((3 * width, tokens), BF16)],
    )


def row_blocks(rows):
    parts = -(-rows // 512)
    size = -(-rows // (16 * parts)) * 16
    return [(start, min(start + size, rows)) for start in range(0, rows, size)]


def first_sweep_kernel(base, count, *refs):
    words, rest = refs[:count], refs[count:]
    ht_ref, target_ref, stat_in_ref, sum_in_ref, stat_ref, sum_ref = rest
    half = ht_ref.shape[1] // 2
    top, mass, drift = stat_in_ref[0:1, :], stat_in_ref[1:2, :], stat_in_ref[2:3, :]
    hits = stat_in_ref[3:4, :half]
    sums = sum_in_ref[...]
    for word_ref in words:
        for start, end in row_blocks(word_ref.shape[0]):
            rows = word_ref[start:end, :]
            z = dot(rows, ht_ref[...])
            old, top = top, jnp.maximum(top, jnp.max(z, axis=0, keepdims=True))
            e = jnp.exp(z - top)
            z0, z1 = z[:, :half], z[:, half:]
            gap = z0 - z1
            moved = jnp.concatenate(
                [
                    jnp.sum(e[:, :half] * gap, axis=0, keepdims=True),
                    -jnp.sum(e[:, half:] * gap, axis=0, keepdims=True),
                ],
                axis=1,
            )
            spot = lax.broadcasted_iota(jnp.int32, (end - start, half), 0)
            hit = spot == target_ref[0:1, :] - (base + start)
            hits = hits + jnp.sum(jnp.where(hit, z0 + z1, 0.0), axis=0, keepdims=True)
            factor = jnp.exp(old - top)
            mass = mass * factor + jnp.sum(e, axis=0, keepdims=True)
            drift = drift * factor + moved
            sums = sums + dot(jnp.ones((8, end - start), BF16), rows)
        base += word_ref.shape[0]
    hits = jnp.concatenate([hits, jnp.zeros_like(hits)], axis=1)
    stat_ref[...] = jnp.concatenate([top, mass, drift, hits, jnp.zeros((4, 2 * half), F32)], axis=0)
    sum_ref[...] = sums


def first_sweep(base, words, ht, target, stats, sums):
    return call(
        functools.partial(first_sweep_kernel, base, len(words)),
        [(stats.shape, F32), (sums.shape, F32)],
        *(*words, ht, target, stats, sums),
    )


def second_sweep_kernel(bases, last, flags_ref, *refs):
    count = len(bases)
    words, rest = refs[: 2 * count], refs[2 * count :]
    ht_ref, hn_ref, row_ref, target_ref, flat_ref, acc_in_refs = *rest[:5], rest[5:7]
    fars, near_ref, outs = rest[7 : 7 + count], rest[7 + count], rest[8 + count : 10 + count]
    acc_refs = rest[10 + count :] if last else outs
    half = ht_ref.shape[1] // 2
    sources = acc_in_refs
    for n, word_ref in enumerate(words):
        base = bases[n // 2] + (n % 2) * word_ref.shape[0]
        for start, end in row_blocks(word_ref.shape[0]):
            rows = word_ref[start:end, :]
            z = dot(rows, ht_ref[...])
            z0, z1 = z[:, :half], z[:, half:]
            p0 = jnp.exp(z0 - row_ref[0:1, :half])
            p1 = jnp.exp(z1 - row_ref[0:1, half:])
            gap = z0 - z1
            spot = lax.broadcasted_iota(jnp.int32, (end - start, half), 0)
            hit = spot == target_ref[0:1, :] - (base + start)
            picked = jnp.where(hit, row_ref[2:3, :half], 0.0)
            g0 = p0 * (row_ref[1:2, :half] + gap) - p1 - picked
            g1 = p1 * (row_ref[1:2, half:] - gap) - p0 - picked
            dz = jnp.concatenate([g0.astype(BF16), g1.astype(BF16)], axis=1)
            grad = (dot(dz, hn_ref[...]) + flat_ref[0:1, :]).astype(BF16)
            if n % 2:
                near_ref[n // 2, start:end, :] = grad
            else:
                fars[n // 2][start:end, :] = grad
            part = lax.dot_general(rows, dz, (((0,), (0,)), ((), ())), preferred_element_type=F32)
            acc_refs[0][...] = sources[0][...] + part[:, :half]
            acc_refs[1][...] = sources[1][...] + part[:, half:]
            sources = acc_refs
    if last:
        give_parts(flags_ref, [ref[...] for ref in acc_refs], *outs)


def second_sweep(flags, bases, words, ht, hn, row_stats, target, flat, accs, last):
    count = len(bases)
    far_shape = words[0].shape
    full = (accs[0].shape, F32)
    outs = call(
        functools.partial(second_sweep_kernel, bases, last),
        [(far_shape, BF16)] * count + [((count,) + far_shape, BF16), full, (accs[0].shape, BF16) if last else full],
        *(*words, ht, hn, row_stats, target, flat, *accs),
        scalars=flags,
        scratch=[full, full] if last else [],
    )
    return outs[:count], outs[count], outs[count + 1 :]


def gelu_parts(u):
    scale, cubic = 0.7978845608028654, 0.044715
    t = jnp.tanh(scale * (u + cubic * (u * u * u)))
    value = 0.5 * u * (1.0 + t)
    slope = 0.5 * (1.0 + t) + (0.5 * scale) * u * (1.0 - t * t) * (1.0 + (3.0 * cubic) * (u * u))
    return value, slope


def expert_rows(block_ref, which):
    return jnp.concatenate([block_ref[which, e] for e in range(block_ref.shape[1])], axis=0)


def expert_masks(route_ref, experts, hidden, tokens):
    names = lax.broadcasted_iota(jnp.int32, (experts * hidden, tokens), 0) // hidden
    return [names == route_ref[p : p + 1, :] for p in range(2)]


def give_parts(flags_ref, parts, mine_ref, theirs_ref):
    @pl.when(flags_ref[0] == 0)
    def _():
        mine_ref[...], theirs_ref[...] = parts[0], parts[1].astype(BF16)

    @pl.when(flags_ref[0] != 0)
    def _():
        mine_ref[...], theirs_ref[...] = parts[1], parts[0].astype(BF16)


def expert_forward_kernel(count, first, last, *refs):
    flags_ref, blocks, (a3_ref, route_ref) = refs[0], refs[1 : count + 1], refs[count + 1 : count + 3]
    ins, outs = refs[count + 3 : -2], refs[-2:]
    tokens = a3_ref.shape[1]
    accs = [0.0, 0.0] if first else [ref[...] for ref in ins]
    for block_ref in blocks:
        masks = expert_masks(route_ref, block_ref.shape[1], block_ref.shape[2], tokens)
        u = dot(expert_rows(block_ref, 0), a3_ref[...])
        g = gelu_parts(u)[0]
        w_out = expert_rows(block_ref, 1).T
        accs = [acc + dot(w_out, jnp.where(mask, g, 0.0).astype(BF16)) for acc, mask in zip(accs, masks)]
    if last:
        give_parts(flags_ref, accs, *outs)
    else:
        outs[0][...], outs[1][...] = accs


def expert_forward(flags, blocks, a3, route, accs, last):
    full = (a3.shape, F32)
    return call(
        functools.partial(expert_forward_kernel, len(blocks), not accs, last),
        [full, (a3.shape, BF16) if last else full],
        *(*blocks, a3, route, *accs),
        scalars=flags,
    )


def expert_backward_kernel(groups, flags_ref, *refs):
    blocks, rest = refs[: 2 * groups], refs[2 * groups :]
    a3_ref, an_ref, dy_ref, dn_ref, route_ref = rest[:5]
    fars, near_ref, mine_ref, theirs_ref, acc_ref = rest[5 : 5 + groups], *rest[5 + groups :]
    tokens = a3_ref.shape[1]
    for n, block_ref in enumerate(blocks):
        experts, hidden = block_ref.shape[1:3]
        masks = expert_masks(route_ref, experts, hidden, tokens)
        w_in = expert_rows(block_ref, 0)
        u = dot(w_in, a3_ref[...])
        g, slope = gelu_parts(u)
        d_act = dot(expert_rows(block_ref, 1), dy_ref[...])
        active = jnp.concatenate([jnp.where(mask, g, 0.0) for mask in masks], axis=1).astype(BF16)
        routed = jnp.where(masks[0], d_act[:, :tokens], 0.0) + jnp.where(masks[1], d_act[:, tokens:], 0.0)
        du = (routed * slope).astype(BF16)
        for matrix, grad in enumerate((dot(du, an_ref[...]), dot(active, dn_ref[...]))):
            grad = grad.astype(BF16)
            for e in range(experts):
                piece = grad[e * hidden : (e + 1) * hidden]
                if n % 2:
                    near_ref[n // 2, matrix, e] = piece
                else:
                    fars[n // 2][matrix, e] = piece
        part = dot(w_in.T, du)
        acc_ref[...] = part if n == 0 else acc_ref[...] + part
    half = tokens // 2
    give_parts(flags_ref, (acc_ref[:, :half], acc_ref[:, half:]), mine_ref, theirs_ref)


def expert_backward(flags, blocks, a3, a3_n, dy, dy_n, route):
    groups = len(blocks) // 2
    shape = blocks[0].shape
    half = (a3.shape[0], a3.shape[1] // 2)
    outs = call(
        functools.partial(expert_backward_kernel, groups),
        [(shape, BF16)] * groups + [((groups,) + shape, BF16), (half, F32), (half, BF16)],
        *(*blocks, a3, a3_n, dy, dy_n, route),
        scalars=flags,
        scratch=[(a3.shape, F32)],
    )
    return outs[:groups], outs[groups], outs[groups + 1 :]


def unpack_kernel(sizes, order_ref, mine_ref, twin_ref, *outs):
    count, half = mine_ref.shape[0], mine_ref.shape[1]

    def write(low_ref, high_ref):
        for j in range(count):
            source = order_ref[j]
            full = jnp.concatenate([low_ref[source], high_ref[source]], axis=0)
            start = 0
            for size, out in zip(sizes, outs):
                out[j * size : (j + 1) * size, :] = full[start : start + size]
                start += size

    pl.when(order_ref[count] == 0)(lambda: write(mine_ref, twin_ref))
    pl.when(order_ref[count] != 0)(lambda: write(twin_ref, mine_ref))


def unpack(mine, twin, order, core, sizes):
    count, half, width = mine.shape
    if any(size % 16 for size in sizes):
        low, high = jnp.where(core == 0, mine, twin), jnp.where(core == 0, twin, mine)
        full = jnp.concatenate([low, high], axis=1)[order]
        ends = [sum(sizes[: n + 1]) for n in range(len(sizes))]
        return [full[:, end - size : end].reshape(-1, width) for size, end in zip(sizes, ends)]
    return pl.pallas_call(
        functools.partial(unpack_kernel, sizes),
        in_specs=[pl.BlockSpec(memory_space=pltpu.SMEM)] + 2 * [pl.BlockSpec(memory_space=pltpu.VMEM)],
        out_specs=[pl.BlockSpec(memory_space=pltpu.VMEM)] * len(sizes),
        out_shape=[jax.ShapeDtypeStruct((count * size, width), mine.dtype) for size in sizes],
        compiler_params=PARAMS,
        cost_estimate=COST,
    )(jnp.concatenate([order, core[None]]).astype(jnp.int32), mine, twin)


def pack_kernel(sizes, order_ref, *refs):
    out_ref = refs[-1]
    count, half, width = out_ref.shape

    def write(core):
        for k in range(count):
            source = order_ref[k]
            start = -core * half
            for size, ref in zip(sizes, refs[:-1]):
                low, high = max(start, 0), min(start + size, half)
                if low < high:
                    rows = pl.ds(pl.multiple_of(source * size, 16) + (low - start), high - low)
                    out_ref[k, low:high, :] = ref[rows, :].astype(BF16)
                start += size
            low = max(start, 0)
            if low < half:
                out_ref[k, low:, :] = jnp.zeros((half - low, width), BF16)

    pl.when(order_ref[count] == 0)(lambda: write(0))
    pl.when(order_ref[count] != 0)(lambda: write(1))


def pack(grads, order, core, sizes, half):
    width = grads[0].shape[1]
    shards = grads[0].shape[0] // sizes[0]
    if any(size % 16 for size in sizes):
        full = jnp.concatenate([grad.reshape(shards, -1, width) for grad in grads], axis=1)
        full = jnp.pad(full, ((0, 0), (0, 2 * half - full.shape[1]), (0, 0)))[order].astype(BF16)
        return jnp.where(core == 0, full[:, :half], full[:, half:])
    return pl.pallas_call(
        functools.partial(pack_kernel, sizes),
        in_specs=[pl.BlockSpec(memory_space=pltpu.SMEM)]
        + len(grads) * [pl.BlockSpec(memory_space=pltpu.VMEM)],
        out_specs=pl.BlockSpec(memory_space=pltpu.VMEM),
        out_shape=jax.ShapeDtypeStruct((order.shape[0], half, width), BF16),
        compiler_params=PARAMS,
        cost_estimate=COST,
    )(jnp.concatenate([order, core[None]]).astype(jnp.int32), *grads)


def group_sum(mine, theirs):
    chip = (mine + swap(theirs, "vocab", 1).astype(F32)).astype(BF16)
    part = chip.astype(F32) + swap(chip, "pass", 1).astype(F32)
    half = part.shape[0] // 2
    return part, (swap(part[:half], "vocab", 1), swap(part[half:], "vocab", 1)), chip


def local(
    inputs,
    memory,
    expert_ids,
    targets,
    lengths,
    memory_mask,
    norm_gain,
    norm_bias,
    self_project,
    self_output,
    cross_query,
    memory_project,
    cross_output,
    expert_in,
    expert_out,
    embedding,
):
    seq_len, width = inputs.shape
    rows_axis = lax.axis_size("dp")
    here = lax.axis_index("dp")
    which = lax.axis_index("pass")
    core = lax.axis_index("vocab")
    shards = 2 * rows_axis

    sizes = [matrix.shape[1] for matrix in (self_project, self_output, cross_query, memory_project, cross_output)]
    norm_width = norm_gain.shape[1]
    norms = jnp.pad(jnp.concatenate([norm_gain, norm_bias], axis=0).T, ((0, 0), (0, width - 8)))
    sizes = (*sizes, norm_width)
    order = 2 * (jnp.arange(shards) // 2 ^ here) + (jnp.arange(shards) % 2 ^ which)

    def core_rows(matrices):
        rows = jnp.concatenate(matrices, axis=0)
        half = -(-rows.shape[0] // 32) * 16
        rows = jnp.pad(rows, ((0, 2 * half - rows.shape[0]), (0, 0)))
        return jnp.where(core == 0, rows[:half], rows[half:])

    mine = core_rows(
        [jnp.concatenate([self_project, self_output, cross_query, memory_project, cross_output], axis=1).T, norms]
    )
    pack_half = mine.shape[0]
    layer_gather = Gather(jnp.stack([mine, swap(mine, "pass", 1)]), "dp")
    layer_gather.send((1, 2, 3))
    layer_gather.forward((0, 1, 2, 3))
    mine = jnp.concatenate(layer_gather.result())
    project_t, self_output_t, cross_query_t, memory_project_t, cross_output_t, norms = unpack(
        mine, swap(mine, "vocab", 1), order, core, sizes
    )
    norms = norms[:, : min(width, 128)]
    flags = jnp.stack([core, which]).astype(jnp.int32)

    experts = expert_in.shape[0] // 2
    hidden = expert_in.shape[2]

    def core_half(weights):
        halves = weights.reshape(2, experts, width, hidden)
        return jnp.where(core == 0, halves[0], halves[1]).transpose(0, 2, 1)

    expert_block = jnp.stack([core_half(expert_in), core_half(expert_out)])
    expert_gather = Gather(expert_block, "dp")
    expert_gather.send((2, 1, 3), layer_gather.mark(3))
    expert_gather.forward((0,), project_t)
    word_gather = Gather(embedding, "dp")

    a1, qkv_t, attended_t, self_lse, h1, a2, cross_t = self_forward(
        inputs, norms, project_t, self_output_t, cross_query_t
    )
    cross_t = after(cross_t, expert_gather.arrived(near=(0,)))
    (memory_kv,) = call(
        memory_keys_kernel, [((memory.shape[0], 2 * width), BF16)], memory, memory_project_t
    )
    mem_bias = jnp.where(memory_mask[0][:, None] == 1, 0.0, -1e30).astype(F32)
    cross_att_t, cross_lse, h2, a3, a3_n = cross_forward(cross_t, memory_kv, mem_bias, h1, norms, cross_output_t)

    expert_gather.forward_together((2, 1, 3), a3)
    word_gather.send((2, 1, 3), (expert_gather.mark(3), a3))
    word_gather.forward((0,), expert_gather.arrived(near=(2,)))
    my_route = expert_ids[0, :, 0].astype(F32)[None, :]
    other_route = swap(my_route, "pass", 1)
    routes = jnp.concatenate([my_route, other_route] + [my_route] * 6, axis=0)
    routes = jnp.where(which == 0, routes, jnp.roll(routes, -1, axis=0).at[1].set(my_route[0]))
    route = (routes - (core * experts).astype(F32)).astype(jnp.int32)
    per_half = rows_axis // (2 * GROUPS)

    def halves(parts, axis):
        parts = [parts[n * per_half : (n + 1) * per_half] for n in range(2 * GROUPS)]
        return [part[0] if per_half == 1 else jnp.concatenate(part, axis=axis) for part in parts]

    expert_parts = halves(expert_gather.result(), 2)
    parts = ()
    for blocks in (expert_parts[:2], expert_parts[2:]):
        parts = expert_forward(flags, blocks, a3, route, parts, len(blocks) > 2)
    parts = after(parts, word_gather.arrived(far=(2, 1)))
    word_gather.forward((2, 1))
    y_part, y_other, mark = group_sum(*parts)
    word_gather.forward((3,), y_part)
    words = halves(word_gather.result(), 0)
    half_words = words[0].shape[0]

    valid = (jnp.arange(seq_len) < lengths[here]).astype(F32)
    half_weight = 0.5 * valid
    weight2 = jnp.concatenate([half_weight, half_weight])[None, :]
    block0, block1, final_t, final_n, block_out, flat_grad = final_norm(
        flags, h2, y_part, y_other, norms, jnp.broadcast_to(weight2, (8, 2 * seq_len)).astype(BF16)
    )
    shard_rows = embedding.shape[0]
    owner = targets // shard_rows
    in_quarter = (owner % 2 == core) & (owner // 2 % 2 == which)
    place = ((owner // 4) ^ here) * shard_rows + targets % shard_rows
    target = jnp.broadcast_to(jnp.where(in_quarter, place, -1)[None, :], (8, seq_len)).astype(jnp.int32)
    stats = jnp.concatenate(
        [jnp.full((1, 2 * seq_len), -1e30, F32), jnp.zeros((7, 2 * seq_len), F32)], axis=0
    )
    sums = jnp.zeros((8, width), F32)
    for g in (0, 2, 1, 3):
        stats, sums = first_sweep(
            2 * g * half_words, words[2 * g : 2 * g + 2], final_t, target, stats, sums
        )
    hits = stats[3, :seq_len]

    def merge(left, axis):
        right = swap(left, axis, 1)
        top = jnp.maximum(left[0:1], right[0:1])
        total = left[1:] * jnp.exp(left[0:1] - top) + right[1:] * jnp.exp(right[0:1] - top)
        return jnp.concatenate([top, total], axis=0)

    merged = merge(merge(stats, "vocab"), "pass")
    lse = merged[0:1] + jnp.log(merged[1:2])
    drift = merged[2:3] / merged[1:2]
    row_stats = jnp.concatenate(
        [
            jnp.where(weight2 > 0, lse + jnp.log(2.0), 1e30),
            2.0 - drift,
            (1.0 - SMOOTH) * weight2,
            jnp.zeros((5, 2 * seq_len), F32),
        ],
        axis=0,
    )
    accs = [(-SMOOTH / VOCAB) * sums[0][:, None] * half_weight[None, :]] * 2
    word_sum = ScatterSum("dp")
    loss = (
        0.25 * jnp.sum(weight2 * (lse + drift))
        - (1.0 - SMOOTH) * jnp.sum(half_weight * hits)
        + jnp.sum(flat_grad[0] * sums[0])
    )
    loss = jnp.broadcast_to(loss, (8, 128))
    first_loss = loss = loss + swap(loss, "dp", 1)
    step = 2
    while step < rows_axis:
        loss = loss + swap(loss, "dp", step)
        step *= 2
    for axis in ("vocab", "pass"):
        loss = loss + swap(loss, axis, 1)
    mean_loss = loss[0, 0] / jnp.sum(lengths).astype(F32)
    for groups in ((2,), (3, 1), (0,)):
        fars, nears, accs = second_sweep(
            flags,
            [2 * g * half_words for g in groups],
            [words[2 * g + n] for g in groups for n in range(2)],
            *(final_t, final_n, row_stats, target, flat_grad, accs, groups[0] == 0),
        )
        if groups[0]:
            word_sum.give(groups, fars, nears, mark=first_loss if groups[0] == 2 else None)
        if groups[0] == 3:
            accs = (after(accs[0], loss), accs[1])
    accs = after(accs, word_sum.arrived(near=(2,)))
    word_sum.forward((2,))

    dh_part, dh_other, mark = group_sum(*accs)
    db, dy, dy_n, cols = final_back(flags, block0, block1, dh_part, dh_other, norms)
    expert_sum = ScatterSum("dp")
    last_words = fars, nears
    *expert_grads, parts = expert_backward(flags, expert_parts, a3, a3_n, dy, dy_n, route)
    parts = after(parts, word_sum.arrived(far=(2,), near=(3, 1)))
    word_sum.forward((3, 1))
    expert_sum.give((0, 1, 2, 3), *expert_grads, 2)
    word_sum.give((0,), *last_words, mark=expert_sum.arrived(near=(0,)))
    da_part, da_other, mark = group_sum(*parts)

    dh1, cross_output_grad, cross_query_grad, pair_grad, cols = cross_back(
        flags,
        *(db, da_part, *da_other, h2, norms, cols, cross_output_t, cross_att_t, cross_t, memory_kv),
        *(cross_lse, mem_bias, a2, cross_query_t, h1),
    )
    dh1 = after(dh1, expert_sum.arrived(near=(0,)))
    expert_sum.forward((2, 3, 1, 0))
    memory_project_grad, memory_grad = call(
        memory_back_kernel,
        [((2 * width, width), BF16), (memory.shape, F32)],
        *(pair_grad, memory, memory_project_t),
    )
    self_output_grad, self_project_grad, inputs_grad, norm_grads = self_back(
        dh1, self_output_t, attended_t, qkv_t, self_lse, a1, inputs, project_t, norms, cols
    )
    self_project_grad = after(self_project_grad, word_sum.arrived(far=(3, 1)))
    evens = jnp.concatenate([jnp.arange(0, rows_axis, 2), jnp.arange(1, rows_axis, 2)])
    pack_order = 2 * ((evens if rows_axis == 8 else jnp.arange(rows_axis)) ^ here) + which
    blocks = pack(
        [self_project_grad, self_output_grad, cross_query_grad, memory_project_grad, cross_output_grad, norm_grads],
        pack_order,
        core,
        sizes,
        pack_half,
    )
    layer_sum = ScatterSum("dp")
    if rows_axis == 8:
        layer_sum.give((0, 1), [blocks[g] for g in range(2)], blocks[4:6])
        layer_sum.give((2, 3), [blocks[g] for g in range(2, 4)], blocks[6:])
        layer_sum.forward((2, 3, 1, 0), expert_sum.arrived(far=(2, 3, 1)))
        word_sum.forward((0,), expert_sum.arrived(far=(2, 3, 1)))
    else:
        layer_sum.blocks = {k: blocks[k] for k in range(rows_axis)}
    embedding_grad = word_sum.result()
    expert_grad = expert_sum.result()
    expert_twin = swap(expert_grad, "vocab", 1)
    expert_grad = jnp.concatenate(
        [
            jnp.where(core == 0, expert_grad, expert_twin),
            jnp.where(core == 0, expert_twin, expert_grad),
        ],
        axis=1,
    ).transpose(0, 1, 3, 2)
    layer_grad = layer_sum.result()
    twin = swap(layer_grad, "vocab", 1)
    layer_grad = jnp.concatenate(
        [jnp.where(core == 0, layer_grad, twin), jnp.where(core == 0, twin, layer_grad)], axis=0
    ).T
    ends = [sum(sizes[: n + 1]) for n in range(len(sizes))]
    layer_grads = [layer_grad[:, end - size : end] for size, end in zip(sizes, ends)]
    norm_out = layer_grads[5][:8]
    return (
        block_out[None],
        mean_loss,
        inputs_grad,
        memory_grad,
        norm_out[:4],
        norm_out[4:],
        *layer_grads[:5],
        expert_grad[0],
        expert_grad[1],
        embedding_grad,
    )


def solution(mesh):
    shared = P(None, ("dp", "pass"))
    placed = (
        P("dp", None),
        P("dp", None),
        P("pass", "dp", None),
        P("dp"),
        P(),
        P("dp", None),
        shared,
        shared,
        shared,
        shared,
        shared,
        shared,
        shared,
        P(None, None, ("dp", "pass")),
        P(None, None, ("dp", "pass")),
        P(("dp", "pass", "vocab"), None),
    )
    return jax.shard_map(
        local,
        mesh=mesh,
        in_specs=placed,
        out_specs=(
            P("pass", "dp", None),
            P(),
            P("dp", None),
            P("dp", None),
            shared,
            shared,
            shared,
            shared,
            shared,
            shared,
            shared,
            P(None, None, ("dp", "pass")),
            P(None, None, ("dp", "pass")),
            P(("dp", "pass", "vocab"), None),
        ),
        check_vma=False,
    )
```

time: 804 us -> 555 us (0.69)
  local copies, waits for them, and re-layouts: 123 us -> 31.8 us
  waiting for transfers between devices: 318 us -> 227 us
  other arithmetic: 87.7 us -> 29.9 us
  Pallas kernels: 153 us -> 194 us
  matrix products: 39.7 us -> 0 us
  starting transfers between devices: 68.4 us -> 57.4 us
    ppermute x63 -> x58, waiting for transfers between devices: 318 us -> 227 us  [swap(): return lax.ppermute(block, axis, [(i, i ^ mask) for i in range(count)])]
    pallas_call x15 -> x20, Pallas kernels: 153 us -> 194 us  [the longest x18 186 us: call(): pl.pallas_call(kernel, in_specs=specs, out_specs=[pl.BlockSpec(memory_spa...]
    dot_general x21 -> x0, matrix products: 39.7 us -> none  [the longest x14 24 us: ein(): return jnp.einsum(spec, left, right, preferred_element_type=F32)]
    slice x45 -> x9, local copies, waits for them, and re-layouts: 44 us -> 6.54 us  [the longest x3 2.03 us: local(): layer_grad[:, end - size:end]]
    concatenate x4, other arithmetic: 16.6 us -> 2.56 us  [the longest x1 0.71 us: local(): jnp.concatenate([norm_gain, norm_bias], axis=0)]
    unnamed x209 -> x79, local copies, waits for them, and re-layouts: 29.5 us -> 16.4 us
    reduce_sum x15 -> x1, other arithmetic: 13.2 us -> 1.23 us  [local(): jnp.sum(half_weight * hits)]
    ppermute x63 -> x58, starting transfers between devices: 68.4 us -> 57.4 us  [swap(): return lax.ppermute(block, axis, [(i, i ^ mask) for i in range(count)])]
  transfers between devices with their start and end apart: 63 -> 58, of which waited for: 20 -> 38; matrix products, arithmetic and copies ran while one was open for 21% -> 8% of each run, Pallas kernels for 4% -> 33%
where the time goes in v2:
time: 555 us; the launch traced here: 547 us
  waiting for transfers between devices  227 us (41%)
  Pallas kernels  194 us (35%)
  starting transfers between devices  57.4 us (10%)
  local copies, waits for them, and re-layouts  31.8 us (6%)
  other arithmetic  29.9 us (5%)
  between operations  6 us (1%)
    ppermute x58, waiting for transfers between devices, swap(): return lax.ppermute(block, axis, [(i, i ^ mask) for i in range(count)])  227 us
    pallas_call x18, Pallas kernels, call(): pl.pallas_call(kernel, in_specs=specs, out_specs=[pl.BlockSpec(memory_spa...  186 us
    ppermute x58, starting transfers between devices, swap(): return lax.ppermute(block, axis, [(i, i ^ mask) for i in range(count)])  57.4 us
    unnamed x79, local copies, waits for them, and re-layouts  16.4 us
  transfers between devices with their start and end apart: 58, of which 38 were waited for; matrix products, arithmetic and copies ran while one was open for 8% of the time, Pallas kernels for 33%

profile of v2, /device:TPU:0, one launch (start us, length us, event | category | flops | bytes accessed | tf_op | source)
XLA Modules:
  0.0 546.6 jit_solution(6363653458410246002)
XLA Ops:
  6.2 2.9 collective-permute-start
  9.1 3.8 collective-permute-done
  14.9 2.5 collective-permute-start.6
  19.0 3.4 collective-permute-done.2
  24.5 7.2 %collective-permute-done.6 = bf16[2,144,512]{2,1,0:T(8,128)(2,1)S(1)} collective-permute-done((bf16[2,144,512]{2,1,0:T(8,128)(2,1)S(1)}, bf16[2,144,512]{2,1,0:T(8,128)(2,1)S(1)}, u32[]{:S(2)}, u32[]{:S(2)}) %collective-permute-start.6) | collective-permute-done | bytes 294944 | tf_op jit(solution)/shard_map/ppermute | solution.py:23
  33.2 9.1 %collective-permute-done.4 = bf16[2,144,512]{2,1,0:T(8,128)(2,1)S(1)} collective-permute-done((bf16[2,144,512]{2,1,0:T(8,128)(2,1)S(1)}, bf16[2,144,512]{2,1,0:T(8,128)(2,1)S(1)}, u32[]{:S(2)}, u32[]{:S(2)}) %collective-permute-start.4) | collective-permute-done | bytes 294944 | tf_op jit(solution)/shard_map/ppermute | solution.py:23
  46.8 2.4 collective-permute-done.5
  52.9 3.4 collective-permute-done.8.twin_ref
  56.3 4.9 shard_map.263
  68.2 4.1 shard_map.265.kv_ref
  73.9 9.8 %shard_map.264 = (bf16[512,512]{1,0:T(8,128)(2,1)}, bf16[1536,512]{1,0:T(8,128)(2,1)}, bf16[512,512]{1,0:T(8,128)(2,1)}, f32[4,2,512]{2,1,0:T(2,128)}, f32[512,5...) custom-call(bf16[512,512]{1,0:T(8,128)(2,1)} %x_ref.3, bf16[512,128]{1,0:T(8,128)(2,1)} %slice.196.norms_ref, ...), custom_call_target="tpu_custom_call" | custom-call | flops 1000 | bytes 1000 | tf_op jit(solution)/shard_map/pallas_call | solution.py:133
  83.7 12.7 %shard_map.266 = (bf16[512,512]{1,0:T(8,128)(2,1)}, f32[4,2,512]{2,1,0:T(2,128)}, f32[512,512]{1,0:T(8,128)}, bf16[512,512]{1,0:T(8,128)(2,1)}, bf16[512,512]{1,0:T(8,128)(2,1)}) custom-call(bf16[512,512]{1,0:T(8,128)(2,1)} %get-tuple-element.126.cross_ref, bf16[1024,1024]{1,0:T(8,128)(2,1)} %shard_map.265.kv_ref, f32[1024,1]{1,0:T(8,128)} %copy.57.bias_ref, ...), custom_call_target="tpu_custom_call" | custom-call | flops 1000 | bytes 1000 | tf_op jit(solution)/shard_map/pallas_call | solution.py:133
  96.4 15.6 %collective-permute-done.11.refs_3_.refs_4_ = bf16[2,2,128,512]{3,2,1,0:T(8,128)(2,1)S(1)} collective-permute-done((bf16[2,2,128,512]{3,2,1,0:T(8,128)(2,1)S(1)}, bf16[2,2,128,512]{3,2,1,0:T(8,128)(2,1)S(1)}, u32[]{:S(2)}, u32[]{:S(2)}) %collective-permute-start.11) | collective-permute-done | bytes 524320 | tf_op jit(solution)/shard_map/ppermute | solution.py:23
  120.7 3.7 shard_map.267
  124.4 25.5 %collective-permute-done.13 = bf16[3,2,2,128,512]{4,3,2,1,0:T(8,128)(2,1)} collective-permute-done((bf16[3,2,2,128,512]{4,3,2,1,0:T(8,128)(2,1)}, bf16[3,2,2,128,512]{4,3,2,1,0:T(8,128)(2,1)}, u32[]{:S(2)}, u32[]{:S(2)}) %collective-permute-start.13) | collective-permute-done | bytes 1572896 | tf_op jit(solution)/shard_map/ppermute | solution.py:23
  149.9 2.5 slice_bitcast_fusion.8
  152.4 8.1 %shard_map.268 = (f32[512,512]{1,0:T(8,128)}, bf16[512,512]{1,0:T(8,128)(2,1)}) custom-call(s32[2]{0:T(128)} %pad_add_fusion.refs_0_.flags_ref, bf16[2,2,128,512]{3,2,1,0:T(8,128)(2,1)} %copy-done.5, bf16[2,2,128,512]{3,2,1,0:T(8,128)(2,1)} %get-tuple-element.273.refs_2_.refs_3_, bf16[2,2,128,512]{3,2,1,0:T(8,128)(2,1)} %copy-done.6, ...), custom_call_target="tpu_custom_call" | custom-call | flops 1000 | bytes 1000 | tf_op jit(solution)/shard_map/pallas_call | solution.py:133
  167.8 11.0 %collective-permute-done.18 = bf16[512,512]{1,0:T(8,128)(2,1)S(1)} collective-permute-done((bf16[512,512]{1,0:T(8,128)(2,1)S(1)}, bf16[512,512]{1,0:T(8,128)(2,1)S(1)}, u32[]{:S(2)}, u32[]{:S(2)}) %collective-permute-start.18) | collective-permute-done | bytes 524320 | tf_op jit(solution)/shard_map/ppermute | solution.py:23
  183.6 9.3 %collective-permute-done.21.refs_0_ = bf16[1000,512]{1,0:T(8,128)(2,1)S(1)} collective-permute-done((bf16[1000,512]{1,0:T(8,128)(2,1)}, bf16[1000,512]{1,0:T(8,128)(2,1)S(1)}, u32[]{:S(2)}, u32[]{:S(2)}) %collective-permute-start.21) | collective-permute-done | bytes 1024032 | tf_op jit(solution)/shard_map/ppermute | solution.py:23
  198.0 6.4 %shard_map.269 = (f32[512,512]{1,0:T(8,128)}, f32[512,512]{1,0:T(8,128)}, bf16[512,1024]{1,0:T(8,128)(2,1)}, bf16[1024,512]{1,0:T(8,128)(2,1)}, f32[512,512]{1,0:T(8,128)}, /*index=5*/f32[8,512]{1,0:T(8,128)}) custom-call(s32[2]{0:T(128)} %pad_add_fusion.refs_0_.flags_ref, f32[512,512]{1,0:T(8,128)} %get-tuple-element.130.h2_ref, f32[512,512]{1,0:T(8,128)} %copy-done.1, ...), custom_call_target="tpu_custom_call" | custom-call | flops 1000 | bytes 1000 | tf_op jit(solution)/shard_map/pallas_call | solution.py:133
  207.0 7.8 %shard_map.270 = (f32[8,1024]{1,0:T(8,128)}, f32[8,512]{1,0:T(8,128)}) custom-call(bf16[1000,512]{1,0:T(8,128)(2,1)} %refs_0_.3, bf16[1000,512]{1,0:T(8,128)(2,1)} %collective-permute-done.25.refs_1_, bf16[512,1024]{1,0:T(8,128)(2,1)} %get-tuple-element.145.refs_2_.refs_4_, s32[8,512]{1,0:T(8,128)} %broadcast_in_dim.49.refs_3_.refs_5_.refs_7_, ...), custom_call_target="tpu_custom_call" | custom-call | flops 1000 | bytes 1000 | tf_op jit(solution)/shard_map/pallas_call | solution.py:133
  214.7 13.0 %collective-permute-done.24.refs_1_ = bf16[1000,512]{1,0:T(8,128)(2,1)} collective-permute-done((bf16[1000,512]{1,0:T(8,128)(2,1)}, bf16[1000,512]{1,0:T(8,128)(2,1)}, u32[]{:S(2)}, u32[]{:S(2)}) %collective-permute-start.24) | collective-permute-done | bytes 1024032 | tf_op jit(solution)/shard_map/ppermute | solution.py:23
  227.7 7.8 %shard_map.271 = (f32[8,1024]{1,0:T(8,128)}, f32[8,512]{1,0:T(8,128)}) custom-call(bf16[1000,512]{1,0:T(8,128)(2,1)} %collective-permute-done.15.refs_0_, bf16[1000,512]{1,0:T(8,128)(2,1)} %collective-permute-done.24.refs_1_, bf16[512,1024]{1,0:T(8,128)(2,1)} %get-tuple-element.145.refs_2_.refs_4_, s32[8,512]{1,0:T(8,128)} %broadcast_in_dim.49.refs_3_.refs_5_.refs_7_, ...), custom_call_target="tpu_custom_call" | custom-call | flops 1000 | bytes 1000 | tf_op jit(solution)/shard_map/pallas_call | solution.py:133
  235.5 14.2 %collective-permute-done.23.refs_1_.refs_3_ = bf16[1000,512]{1,0:T(8,128)(2,1)} collective-permute-done((bf16[1000,512]{1,0:T(8,128)(2,1)S(1)}, bf16[1000,512]{1,0:T(8,128)(2,1)}, u32[]{:S(2)}, u32[]{:S(2)}) %collective-permute-start.23) | collective-permute-done | bytes 1024032 | tf_op jit(solution)/shard_map/ppermute | solution.py:23
  249.7 7.9 %shard_map.272 = (f32[8,1024]{1,0:T(8,128)}, f32[8,512]{1,0:T(8,128)}) custom-call(bf16[1000,512]{1,0:T(8,128)(2,1)} %copy-done.7, bf16[1000,512]{1,0:T(8,128)(2,1)} %collective-permute-done.23.refs_1_.refs_3_, bf16[512,1024]{1,0:T(8,128)(2,1)} %get-tuple-element.145.refs_2_.refs_4_, s32[8,512]{1,0:T(8,128)} %broadcast_in_dim.49.refs_3_.refs_5_.refs_7_, ...), custom_call_target="tpu_custom_call" | custom-call | flops 1000 | bytes 1000 | tf_op jit(solution)/shard_map/pallas_call | solution.py:133
  257.6 13.6 %collective-permute-done.22.refs_1_ = bf16[1000,512]{1,0:T(8,128)(2,1)} collective-permute-done((bf16[1000,512]{1,0:T(8,128)(2,1)S(1)}, bf16[1000,512]{1,0:T(8,128)(2,1)}, u32[]{:S(2)}, u32[]{:S(2)}) %collective-permute-start.22) | collective-permute-done | bytes 1024032 | tf_op jit(solution)/shard_map/ppermute | solution.py:23
  271.2 7.8 %shard_map.273 = (f32[8,1024]{1,0:T(8,128)}, f32[8,512]{1,0:T(8,128)}) custom-call(bf16[1000,512]{1,0:T(8,128)(2,1)} %copy-done.9, bf16[1000,512]{1,0:T(8,128)(2,1)} %collective-permute-done.22.refs_1_, bf16[512,1024]{1,0:T(8,128)(2,1)} %get-tuple-element.145.refs_2_.refs_4_, s32[8,512]{1,0:T(8,128)} %broadcast_in_dim.49.refs_3_.refs_5_.refs_7_, ...), custom_call_target="tpu_custom_call" | custom-call | flops 1000 | bytes 1000 | tf_op jit(solution)/shard_map/pallas_call | solution.py:133
  291.9 11.9 %shard_map.274 = (bf16[1000,512]{1,0:T(8,128)(2,1)}, bf16[1,1000,512]{2,1,0:T(8,128)(2,1)}, f32[512,512]{1,0:T(8,128)}, f32[512,512]{1,0:T(8,128)}) custom-call(s32[2]{0:T(128)} %pad_add_fusion.refs_0_.flags_ref, bf16[1000,512]{1,0:T(8,128)(2,1)} %collective-permute-done.15.refs_0_, bf16[1000,512]{1,0:T(8,128)(2,1)} %collective-permute-done.24.refs_1_, ...), custom_call_target="tpu_custom_call" | custom-call | flops 1000 | bytes 1000 | tf_op jit(solution)/shard_map/pallas_call | solution.py:133
  304.4 3.6 collective-permute-done.29
  308.4 4.2 collective-permute-done.30
  315.2 20.4 %shard_map.275 = (bf16[1000,512]{1,0:T(8,128)(2,1)}, bf16[1000,512]{1,0:T(8,128)(2,1)}, bf16[2,1000,512]{2,1,0:T(8,128)(2,1)}, f32[512,512]{1,0:T(8,128)}, f32[512,512]{1,0:T(8,128)}) custom-call(s32[2]{0:T(128)} %pad_add_fusion.refs_0_.flags_ref, bf16[1000,512]{1,0:T(8,128)(2,1)} %copy-done.9, bf16[1000,512]{1,0:T(8,128)(2,1)} %collective-permute-done.22.refs_1_, ...), custom_call_target="tpu_custom_call" | custom-call | flops 1000 | bytes 1000 | tf_op jit(solution)/shard_map/pallas_call | solution.py:133
  335.6 12.8 %shard_map.276 = (bf16[1000,512]{1,0:T(8,128)(2,1)}, bf16[1,1000,512]{2,1,0:T(8,128)(2,1)}, f32[512,512]{1,0:T(8,128)}, bf16[512,512]{1,0:T(8,128)(2,1)}) custom-call(s32[2]{0:T(128)} %pad_add_fusion.refs_0_.flags_ref, bf16[1000,512]{1,0:T(8,128)(2,1)} %refs_0_.3, bf16[1000,512]{1,0:T(8,128)(2,1)} %collective-permute-done.25.refs_1_, ...), custom_call_target="tpu_custom_call" | custom-call | flops 1000 | bytes 1000 | tf_op jit(solution)/shard_map/pallas_call | solution.py:133
  353.3 12.7 %collective-permute-done.35 = bf16[512,512]{1,0:T(8,128)(2,1)S(1)} collective-permute-done((bf16[512,512]{1,0:T(8,128)(2,1)S(1)}, bf16[512,512]{1,0:T(8,128)(2,1)S(1)}, u32[]{:S(2)}, u32[]{:S(2)}) %collective-permute-start.35) | collective-permute-done | bytes 524320 | tf_op jit(solution)/shard_map/ppermute | solution.py:23
  369.8 5.9 %shard_map.277 = (f32[512,512]{1,0:T(8,128)}, bf16[512,1024]{1,0:T(8,128)(2,1)}, bf16[1024,512]{1,0:T(8,128)(2,1)}, f32[512,128]{1,0:T(8,128)}) custom-call(s32[2]{0:T(128)} %pad_add_fusion.refs_0_.flags_ref, f32[512,512]{1,0:T(8,128)} %get-tuple-element.156.b0_ref, f32[512,512]{1,0:T(8,128)} %get-tuple-element.157.b1_ref, f32[512,512]{1,0:T(8,128)} %copy-done, ...), custom_call_target="tpu_custom_call" | custom-call | flops 1000 | bytes 1000 | tf_op jit(solution)/shard_map/pallas_call | solution.py:133
  375.7 15.5 %shard_map.278 = (bf16[2,2,128,512]{3,2,1,0:T(8,128)(2,1)}, bf16[2,2,128,512]{3,2,1,0:T(8,128)(2,1)}, bf16[2,2,128,512]{3,2,1,0:T(8,128)(2,1)}, bf16[2,2,128,512...) custom-call(s32[2]{0:T(128)} %pad_add_fusion.refs_0_.flags_ref, ...), custom_call_target="tpu_custom_call" | custom-call | flops 1000 | bytes 1000 | tf_op jit(solution)/shard_map/pallas_call | solution.py:133
  392.8 3.4 collective-permute-done.39
  396.2 3.5 collective-permute-done.38
  404.1 2.8 fusion.3
  413.7 22.2 %shard_map.279 = (f32[512,512]{1,0:T(8,128)}, bf16[512,512]{1,0:T(8,128)(2,1)}, bf16[512,512]{1,0:T(8,128)(2,1)}, bf16[1024,1024]{1,0:T(8,128)(2,1)}, f32[512,128]{1,0:T(8,128)}) custom-call(s32[2]{0:T(128)} %pad_add_fusion.refs_0_.flags_ref, f32[512,512]{1,0:T(8,128)} %get-tuple-element.170.db_ref, f32[512,256]{1,0:T(8,128)} %copy-done.2, ...), custom_call_target="tpu_custom_call" | custom-call | flops 1000 | bytes 1000 | tf_op jit(solution)/shard_map/pallas_call | solution.py:133
  435.9 5.9 %shard_map.281 = (bf16[1024,512]{1,0:T(8,128)(2,1)}, f32[1024,512]{1,0:T(8,128)}) custom-call(bf16[1024,1024]{1,0:T(8,128)(2,1)} %get-tuple-element.193.dkv_ref, bf16[1024,512]{1,0:T(8,128)(2,1)} %memory_ref.3, bf16[1024,512]{1,0:T(8,128)(2,1)} %get-tuple-element.127.weight_ref), custom_call_target="tpu_custom_call" | custom-call | flops 1000 | bytes 1000 | tf_op jit(solution)/shard_map/pallas_call | solution.py:133
  441.8 15.1 %shard_map.280 = (bf16[512,512]{1,0:T(8,128)(2,1)}, bf16[1536,512]{1,0:T(8,128)(2,1)}, f32[512,512]{1,0:T(8,128)}, bf16[512,512]{1,0:T(8,128)(2,1)}) custom-call(f32[512,512]{1,0:T(8,128)} %get-tuple-element.186.dh1_ref, bf16[512,512]{1,0:T(8,128)(2,1)} %get-tuple-element.122.output_ref, bf16[512,512]{1,0:T(8,128)(2,1)} %get-tuple-element.187.att_ref, ...), custom_call_target="tpu_custom_call" | custom-call | flops 1000 | bytes 1000 | tf_op jit(solution)/shard_map/pallas_call | solution.py:133
  461.7 3.7 shard_map.282
  468.6 7.9 %collective-permute-done.47 = bf16[2,144,512]{2,1,0:T(8,128)(2,1)S(1)} collective-permute-done((bf16[2,144,512]{2,1,0:T(8,128)(2,1)S(1)}, bf16[2,144,512]{2,1,0:T(8,128)(2,1)S(1)}, u32[]{:S(2)}, u32[]{:S(2)}) %collective-permute-start.47) | collective-permute-done | bytes 294944 | tf_op jit(solution)/shard_map/ppermute | solution.py:23
  476.5 7.6 %collective-permute-done.49 = bf16[2,2,128,512]{3,2,1,0:T(8,128)(2,1)} collective-permute-done((bf16[2,2,128,512]{3,2,1,0:T(8,128)(2,1)S(1)}, bf16[2,2,128,512]{3,2,1,0:T(8,128)(2,1)}, u32[]{:S(2)}, u32[]{:S(2)}) %collective-permute-start.49) | collective-permute-done | bytes 524320 | tf_op jit(solution)/shard_map/ppermute | solution.py:23
  484.1 23.0 %collective-permute-done.48 = bf16[2,2,128,512]{3,2,1,0:T(8,128)(2,1)} collective-permute-done((bf16[2,2,128,512]{3,2,1,0:T(8,128)(2,1)S(1)}, bf16[2,2,128,512]{3,2,1,0:T(8,128)(2,1)}, u32[]{:S(2)}, u32[]{:S(2)}) %collective-permute-start.48) | collective-permute-done | bytes 524320 | tf_op jit(solution)/shard_map/ppermute | solution.py:23
  515.9 3.7 collective-permute-done.53
  528.0 9.4 %collective-permute-done.57 = bf16[1,1000,512]{2,1,0:T(8,128)(2,1)} collective-permute-done((bf16[1,1000,512]{2,1,0:T(8,128)(2,1)}, bf16[1,1000,512]{2,1,0:T(8,128)(2,1)}, u32[]{:S(2)}, u32[]{:S(2)}) %collective-permute-start.57) | collective-permute-done | bytes 1024032 | tf_op jit(solution)/shard_map/ppermute | solution.py:23
  537.4 4.4 fusion.2
  (250 shorter events, 120.6 us)
Async XLA Ops:
  6.2 6.8 %collective-permute-start = (bf16[144,512]{1,0:T(8,128)(2,1)S(1)}, bf16[144,512]{1,0:T(8,128)(2,1)S(1)}, u32[]{:S(2)}, u32[]{:S(2)}) collective-permute-start(bf16[144,512]{1,0:T(8,128)(2,1)S(1)} %get-tuple-element.261), channel_id=1, source_target_pairs={{0,2},{2,0},{1,3},{3,1},{4,6},{6,4},{5,7},{7,5},{8,10},{10,8},{9,1... | collective-permute-start | bytes 442376 | tf_op jit(solution)/shard_map/ppermute | solution.py:23
  13.0 9.4 %collective-permute-start.2 = (bf16[2,144,512]{2,1,0:T(8,128)(2,1)S(1)}, bf16[2,144,512]{2,1,0:T(8,128)(2,1)S(1)}, u32[]{:S(2)}, u32[]{:S(2)}) collective-permute-start(bf16[2,144,512]{2,1,0:T(8,128)(2,1)S(1)} %pad_maximum_fusion.2), channel_id=1, source_target_pairs={{0,8},{4,12},{8,0},{12,4},{16,24},{20,28},{24,16},{28,20},{1,9},{5... | collective-permute-start | bytes 884744 | tf_op jit(solution)/shard_map/ppermute | solution.py:23
  14.9 16.8 %collective-permute-start.6 = (bf16[2,144,512]{2,1,0:T(8,128)(2,1)S(1)}, bf16[2,144,512]{2,1,0:T(8,128)(2,1)S(1)}, u32[]{:S(2)}, u32[]{:S(2)}) collective-permute-start(bf16[2,144,512]{2,1,0:T(8,128)(2,1)S(1)} %pad_maximum_fusion.2), channel_id=1, source_target_pairs={{0,24},{4,28},{8,16},{12,20},{16,8},{20,12},{24,0},{28,4},{1,25},{... | collective-permute-start | bytes 884744 | tf_op jit(solution)/shard_map/ppermute | solution.py:23
  17.3 24.9 %collective-permute-start.4 = (bf16[2,144,512]{2,1,0:T(8,128)(2,1)S(1)}, bf16[2,144,512]{2,1,0:T(8,128)(2,1)S(1)}, u32[]{:S(2)}, u32[]{:S(2)}) collective-permute-start(bf16[2,144,512]{2,1,0:T(8,128)(2,1)S(1)} %pad_maximum_fusion.2), channel_id=1, source_target_pairs={{0,16},{4,20},{8,24},{12,28},{16,0},{20,4},{24,8},{28,12},{1,17},{... | collective-permute-start | bytes 884744 | tf_op jit(solution)/shard_map/ppermute | solution.py:23
  17.5 26.3 %collective-permute-start.1 = (bf16[2,144,512]{2,1,0:T(8,128)(2,1)S(1)}, bf16[2,144,512]{2,1,0:T(8,128)(2,1)S(1)}, u32[]{:S(2)}, u32[]{:S(2)}) collective-permute-start(bf16[2,144,512]{2,1,0:T(8,128)(2,1)S(1)} %pad_maximum_fusion.2), channel_id=1, source_target_pairs={{0,4},{4,0},{8,12},{12,8},{16,20},{20,16},{24,28},{28,24},{1,5},{5... | collective-permute-start | bytes 884744 | tf_op jit(solution)/shard_map/ppermute | solution.py:23
  22.3 23.0 %collective-permute-start.3 = (bf16[2,144,512]{2,1,0:T(8,128)(2,1)S(1)}, bf16[2,144,512]{2,1,0:T(8,128)(2,1)S(1)}, u32[]{:S(2)}, u32[]{:S(2)}) collective-permute-start(bf16[2,144,512]{2,1,0:T(8,128)(2,1)S(1)} %collective-permute-done.2), channel_id=1, source_target_pairs={{0,4},{4,0},{8,12},{12,8},{16,20},{20,16},{24,28},{28,24},{1,5},{5... | collective-permute-start | bytes 884744 | tf_op jit(solution)/shard_map/ppermute | solution.py:23
  31.7 19.0 %collective-permute-start.7 = (bf16[2,144,512]{2,1,0:T(8,128)(2,1)S(1)}, bf16[2,144,512]{2,1,0:T(8,128)(2,1)S(1)}, u32[]{:S(2)}, u32[]{:S(2)}) collective-permute-start(bf16[2,144,512]{2,1,0:T(8,128)(2,1)S(1)} %collective-permute-done.6), channel_id=1, source_target_pairs={{0,4},{4,0},{8,12},{12,8},{16,20},{20,16},{24,28},{28,24},{1,5},{5... | collective-permute-start | bytes 884744 | tf_op jit(solution)/shard_map/ppermute | solution.py:23
  42.3 7.0 %collective-permute-start.5 = (bf16[2,144,512]{2,1,0:T(8,128)(2,1)S(1)}, bf16[2,144,512]{2,1,0:T(8,128)(2,1)S(1)}, u32[]{:S(2)}, u32[]{:S(2)}) collective-permute-start(bf16[2,144,512]{2,1,0:T(8,128)(2,1)S(1)} %collective-permute-done.4), channel_id=1, source_target_pairs={{0,4},{4,0},{8,12},{12,8},{16,20},{20,16},{24,28},{28,24},{1,5},{5... | collective-permute-start | bytes 884744 | tf_op jit(solution)/shard_map/ppermute | solution.py:23
  51.5 4.9 collective-permute-start.8
  61.2 22.4 %collective-permute-start.9 = (bf16[2,2,128,512]{3,2,1,0:T(8,128)(2,1)S(1)}, bf16[2,2,128,512]{3,2,1,0:T(8,128)(2,1)S(1)}, u32[]{:S(2)}, u32[]{:S(2)}) collective-permute-start(bf16[2,2,128,512]{3,2,1,0:T(8,128)(2,1)S(1)} %pad_maximum_fusion.1.refs_1_.refs_0_), channel_id=1, source_target_pairs={{0,4},{4,0},{8,12},{12,8},{16,20},{20,16},{24,28},{28,24},{1,5},{5... | collective-permute-start | bytes 1572872 | tf_op jit(solution)/shard_map/ppermute | solution.py:23
  62.7 33.6 %collective-permute-start.12 = (bf16[2,2,128,512]{3,2,1,0:T(8,128)(2,1)S(1)}, bf16[2,2,128,512]{3,2,1,0:T(8,128)(2,1)S(1)}, u32[]{:S(2)}, u32[]{:S(2)}) collective-permute-start(bf16[2,2,128,512]{3,2,1,0:T(8,128)(2,1)S(1)} %pad_maximum_fusion.1.refs_1_.refs_0_), channel_id=1, source_target_pairs={{0,24},{4,28},{8,16},{12,20},{16,8},{20,12},{24,0},{28,4},{1,25},{... | collective-permute-start | bytes 1572872 | tf_op jit(solution)/shard_map/ppermute | solution.py:23
  65.2 31.2 %collective-permute-start.10 = (bf16[2,2,128,512]{3,2,1,0:T(8,128)(2,1)S(1)}, bf16[2,2,128,512]{3,2,1,0:T(8,128)(2,1)S(1)}, u32[]{:S(2)}, u32[]{:S(2)}) collective-permute-start(bf16[2,2,128,512]{3,2,1,0:T(8,128)(2,1)S(1)} %pad_maximum_fusion.1.refs_1_.refs_0_), channel_id=1, source_target_pairs={{0,8},{4,12},{8,0},{12,4},{16,24},{20,28},{24,16},{28,20},{1,9},{5... | collective-permute-start | bytes 1572872 | tf_op jit(solution)/shard_map/ppermute | solution.py:23
  66.0 45.9 %collective-permute-start.11 = (bf16[2,2,128,512]{3,2,1,0:T(8,128)(2,1)S(1)}, bf16[2,2,128,512]{3,2,1,0:T(8,128)(2,1)S(1)}, u32[]{:S(2)}, u32[]{:S(2)}) collective-permute-start(bf16[2,2,128,512]{3,2,1,0:T(8,128)(2,1)S(1)} %pad_maximum_fusion.1.refs_1_.refs_0_), channel_id=1, source_target_pairs={{0,16},{4,20},{8,24},{12,28},{16,0},{20,4},{24,8},{28,12},{1,17},{... | collective-permute-start | bytes 1572872 | tf_op jit(solution)/shard_map/ppermute | solution.py:23
  113.3 36.6 %collective-permute-start.13 = (bf16[3,2,2,128,512]{4,3,2,1,0:T(8,128)(2,1)}, bf16[3,2,2,128,512]{4,3,2,1,0:T(8,128)(2,1)}, u32[]{:S(2)}, u32[]{:S(2)}) collective-permute-start(bf16[3,2,2,128,512]{4,3,2,1,0:T(8,128)(2,1)} %pad_maximum_fusion), channel_id=1, source_target_pairs={{0,4},{4,0},{8,12},{12,8},{16,20},{20,16},{24,28},{28,24},{1,5},{5... | collective-permute-start | bytes 4718600 | tf_op jit(solution)/shard_map/ppermute | solution.py:23
  113.8 46.7 %collective-permute-start.16 = (bf16[1000,512]{1,0:T(8,128)(2,1)}, bf16[1000,512]{1,0:T(8,128)(2,1)S(1)}, u32[]{:S(2)}, u32[]{:S(2)}) collective-permute-start(bf16[1000,512]{1,0:T(8,128)(2,1)} %refs_0_.3), channel_id=1, source_target_pairs={{0,8},{4,12},{8,0},{12,4},{16,24},{20,28},{24,16},{28,20},{1,9},{5... | collective-permute-start | bytes 3072008 | tf_op jit(solution)/shard_map/ppermute | solution.py:23
  113.8 47.5 %collective-permute-start.15 = (bf16[1000,512]{1,0:T(8,128)(2,1)}, bf16[1000,512]{1,0:T(8,128)(2,1)}, u32[]{:S(2)}, u32[]{:S(2)}) collective-permute-start(bf16[1000,512]{1,0:T(8,128)(2,1)} %refs_0_.3), channel_id=1, source_target_pairs={{0,16},{4,20},{8,24},{12,28},{16,0},{20,4},{24,8},{28,12},{1,17},{... | collective-permute-start | bytes 3072008 | tf_op jit(solution)/shard_map/ppermute | solution.py:23
  116.2 3.6 collective-permute-start.14
  164.8 14.0 %collective-permute-start.18 = (bf16[512,512]{1,0:T(8,128)(2,1)S(1)}, bf16[512,512]{1,0:T(8,128)(2,1)S(1)}, u32[]{:S(2)}, u32[]{:S(2)}) collective-permute-start(bf16[512,512]{1,0:T(8,128)(2,1)S(1)} %add_convert_fusion.1), channel_id=1, source_target_pairs={{0,2},{2,0},{1,3},{3,1},{4,6},{6,4},{5,7},{7,5},{8,10},{10,8},{9,1... | collective-permute-start | bytes 1572872 | tf_op jit(solution)/shard_map/ppermute | solution.py:23
  166.3 26.5 %collective-permute-start.21 = (bf16[1000,512]{1,0:T(8,128)(2,1)}, bf16[1000,512]{1,0:T(8,128)(2,1)S(1)}, u32[]{:S(2)}, u32[]{:S(2)}) collective-permute-start(bf16[1000,512]{1,0:T(8,128)(2,1)} %refs_0_.3), channel_id=1, source_target_pairs={{0,24},{4,28},{8,16},{12,20},{16,8},{20,12},{24,0},{28,4},{1,25},{... | collective-permute-start | bytes 3072008 | tf_op jit(solution)/shard_map/ppermute | solution.py:23
  180.0 15.1 %collective-permute-start.20 = (f32[256,512]{1,0:T(8,128)}, f32[256,512]{1,0:T(8,128)}, u32[]{:S(2)}, u32[]{:S(2)}) collective-permute-start(f32[256,512]{1,0:T(8,128)} %get-tuple-element.281), channel_id=1, source_target_pairs={{0,1},{1,0},{2,3},{3,2},{4,5},{5,4},{6,7},{7,6},{8,9},{9,8},{10,11... | collective-permute-start | bytes 1572872 | tf_op jit(solution)/shard_map/ppermute | solution.py:23
  180.0 25.7 %collective-permute-start.25 = (bf16[1000,512]{1,0:T(8,128)(2,1)}, bf16[1000,512]{1,0:T(8,128)(2,1)}, u32[]{:S(2)}, u32[]{:S(2)}) collective-permute-start(bf16[1000,512]{1,0:T(8,128)(2,1)} %refs_0_.3), channel_id=1, source_target_pairs={{0,4},{4,0},{8,12},{12,8},{16,20},{20,16},{24,28},{28,24},{1,5},{5... | collective-permute-start | bytes 3072008 | tf_op jit(solution)/shard_map/ppermute | solution.py:23
  181.5 46.2 %collective-permute-start.24 = (bf16[1000,512]{1,0:T(8,128)(2,1)}, bf16[1000,512]{1,0:T(8,128)(2,1)}, u32[]{:S(2)}, u32[]{:S(2)}) collective-permute-start(bf16[1000,512]{1,0:T(8,128)(2,1)} %collective-permute-done.15.refs_0_), channel_id=1, source_target_pairs={{0,4},{4,0},{8,12},{12,8},{16,20},{20,16},{24,28},{28,24},{1,5},{5... | collective-permute-start | bytes 3072008 | tf_op jit(solution)/shard_map/ppermute | solution.py:23
  182.0 67.6 %collective-permute-start.23 = (bf16[1000,512]{1,0:T(8,128)(2,1)S(1)}, bf16[1000,512]{1,0:T(8,128)(2,1)}, u32[]{:S(2)}, u32[]{:S(2)}) collective-permute-start(bf16[1000,512]{1,0:T(8,128)(2,1)S(1)} %copy-done.8), channel_id=1, source_target_pairs={{0,4},{4,0},{8,12},{12,8},{16,20},{20,16},{24,28},{28,24},{1,5},{5... | collective-permute-start | bytes 3072008 | tf_op jit(solution)/shard_map/ppermute | solution.py:23
  192.9 78.4 %collective-permute-start.22 = (bf16[1000,512]{1,0:T(8,128)(2,1)S(1)}, bf16[1000,512]{1,0:T(8,128)(2,1)}, u32[]{:S(2)}, u32[]{:S(2)}) collective-permute-start(bf16[1000,512]{1,0:T(8,128)(2,1)S(1)} %collective-permute-done.21.refs_0_), channel_id=1, source_target_pairs={{0,4},{4,0},{8,12},{12,8},{16,20},{20,16},{24,28},{28,24},{1,5},{5... | collective-permute-start | bytes 3072008 | tf_op jit(solution)/shard_map/ppermute | solution.py:23
  279.0 3.1 collective-permute-start.26
  283.7 4.0 collective-permute-start.27
  289.6 14.2 %collective-permute-start.28 = (f32[8,128]{1,0:T(8,128)S(1)}, f32[8,128]{1,0:T(8,128)S(1)}, u32[]{:S(2)}, u32[]{:S(2)}) collective-permute-start(f32[8,128]{1,0:T(8,128)S(1)} %broadcast_in_dim.51), channel_id=1, source_target_pairs={{0,4},{4,0},{8,12},{12,8},{16,20},{20,16},{24,28},{28,24},{1,5},{5... | collective-permute-start | bytes 12296 | tf_op jit(solution)/shard_map/ppermute | solution.py:23
  303.8 44.6 %collective-permute-start.33 = (bf16[1,1000,512]{2,1,0:T(8,128)(2,1)}, bf16[1,1000,512]{2,1,0:T(8,128)(2,1)S(1)}, u32[]{:S(2)}, u32[]{:S(2)}) collective-permute-start(bf16[1,1000,512]{2,1,0:T(8,128)(2,1)} %get-tuple-element.167), channel_id=1, source_target_pairs={{0,4},{4,0},{8,12},{12,8},{16,20},{20,16},{24,28},{28,24},{1,5},{5... | collective-permute-start | bytes 3072008 | tf_op jit(solution)/shard_map/ppermute | solution.py:23
  304.4 3.6 collective-permute-start.29
  308.0 4.5 collective-permute-start.30
  313.7 21.9 %collective-permute-start.32 = (f32[8,128]{1,0:T(8,128)S(1)}, f32[8,128]{1,0:T(8,128)S(1)}, u32[]{:S(2)}, u32[]{:S(2)}) collective-permute-start(f32[8,128]{1,0:T(8,128)S(1)} %add.186), channel_id=1, source_target_pairs={{0,2},{2,0},{1,3},{3,1},{4,6},{6,4},{5,7},{7,5},{8,10},{10,8},{9,1... | collective-permute-start | bytes 12296 | tf_op jit(solution)/shard_map/ppermute | solution.py:23
  348.5 47.7 %collective-permute-start.39 = (bf16[2,1000,512]{2,1,0:T(8,128)(2,1)}, bf16[2,1000,512]{2,1,0:T(8,128)(2,1)S(1)}, u32[]{:S(2)}, u32[]{:S(2)}) collective-permute-start(bf16[2,1000,512]{2,1,0:T(8,128)(2,1)} %get-tuple-element.177), channel_id=1, source_target_pairs={{0,4},{4,0},{8,12},{12,8},{16,20},{20,16},{24,28},{28,24},{1,5},{5... | collective-permute-start | bytes 6144008 | tf_op jit(solution)/shard_map/ppermute | solution.py:23
  352.0 14.0 %collective-permute-start.35 = (bf16[512,512]{1,0:T(8,128)(2,1)S(1)}, bf16[512,512]{1,0:T(8,128)(2,1)S(1)}, u32[]{:S(2)}, u32[]{:S(2)}) collective-permute-start(bf16[512,512]{1,0:T(8,128)(2,1)S(1)} %add_convert_fusion), channel_id=1, source_target_pairs={{0,2},{2,0},{1,3},{3,1},{4,6},{6,4},{5,7},{7,5},{8,10},{10,8},{9,1... | collective-permute-start | bytes 1572872 | tf_op jit(solution)/shard_map/ppermute | solution.py:23
  352.9 46.7 %collective-permute-start.38 = (bf16[1000,512]{1,0:T(8,128)(2,1)S(1)}, bf16[1000,512]{1,0:T(8,128)(2,1)S(1)}, u32[]{:S(2)}, u32[]{:S(2)}) collective-permute-start(bf16[1000,512]{1,0:T(8,128)(2,1)S(1)} %fusion.5), channel_id=1, source_target_pairs={{0,16},{4,20},{8,24},{12,28},{16,0},{20,4},{24,8},{28,12},{1,17},{... | collective-permute-start | bytes 3072008 | tf_op jit(solution)/shard_map/ppermute | solution.py:23
  391.3 50.5 %collective-permute-start.44 = (bf16[4,2,2,128,512]{4,3,2,1,0:T(8,128)(2,1)}, bf16[4,2,2,128,512]{4,3,2,1,0:T(8,128)(2,1)S(1)}, u32[]{:S(2)}, u32[]{:S(2)}) collective-permute-start(bf16[4,2,2,128,512]{4,3,2,1,0:T(8,128)(2,1)} %get-tuple-element.185), channel_id=1, source_target_pairs={{0,4},{4,0},{8,12},{12,8},{16,20},{20,16},{24,28},{28,24},{1,5},{5... | collective-permute-start | bytes 6291464 | tf_op jit(solution)/shard_map/ppermute | solution.py:23
  402.5 8.4 %collective-permute-start.41 = (bf16[512,256]{1,0:T(8,128)(2,1)S(1)}, bf16[512,256]{1,0:T(8,128)(2,1)S(1)}, u32[]{:S(2)}, u32[]{:S(2)}) collective-permute-start(bf16[512,256]{1,0:T(8,128)(2,1)S(1)} %add_convert_fusion.2), channel_id=1, source_target_pairs={{0,2},{2,0},{1,3},{3,1},{4,6},{6,4},{5,7},{7,5},{8,10},{10,8},{9,1... | collective-permute-start | bytes 786440 | tf_op jit(solution)/shard_map/ppermute | solution.py:23
  406.9 50.0 %collective-permute-start.46 = (bf16[1000,512]{1,0:T(8,128)(2,1)}, bf16[1000,512]{1,0:T(8,128)(2,1)S(1)}, u32[]{:S(2)}, u32[]{:S(2)}) collective-permute-start(bf16[1000,512]{1,0:T(8,128)(2,1)} %get-tuple-element.269), channel_id=1, source_target_pairs={{0,8},{4,12},{8,0},{12,4},{16,24},{20,28},{24,16},{28,20},{1,9},{5... | collective-permute-start | bytes 3072008 | tf_op jit(solution)/shard_map/ppermute | solution.py:23
  406.9 50.0 %collective-permute-start.45 = (bf16[1000,512]{1,0:T(8,128)(2,1)S(1)}, bf16[1000,512]{1,0:T(8,128)(2,1)S(1)}, u32[]{:S(2)}, u32[]{:S(2)}) collective-permute-start(bf16[1000,512]{1,0:T(8,128)(2,1)S(1)} %get-tuple-element.270), channel_id=1, source_target_pairs={{0,24},{4,28},{8,16},{12,20},{16,8},{20,12},{24,0},{28,4},{1,25},{... | collective-permute-start | bytes 3072008 | tf_op jit(solution)/shard_map/ppermute | solution.py:23
  458.2 18.3 %collective-permute-start.50 = (bf16[2,2,128,512]{3,2,1,0:T(8,128)(2,1)S(1)}, bf16[2,2,128,512]{3,2,1,0:T(8,128)(2,1)}, u32[]{:S(2)}, u32[]{:S(2)}) collective-permute-start(bf16[2,2,128,512]{3,2,1,0:T(8,128)(2,1)S(1)} %get-tuple-element.266), channel_id=1, source_target_pairs={{0,8},{4,12},{8,0},{12,4},{16,24},{20,28},{24,16},{28,20},{1,9},{5... | collective-permute-start | bytes 1572872 | tf_op jit(solution)/shard_map/ppermute | solution.py:23
  458.2 25.9 %collective-permute-start.49 = (bf16[2,2,128,512]{3,2,1,0:T(8,128)(2,1)S(1)}, bf16[2,2,128,512]{3,2,1,0:T(8,128)(2,1)}, u32[]{:S(2)}, u32[]{:S(2)}) collective-permute-start(bf16[2,2,128,512]{3,2,1,0:T(8,128)(2,1)S(1)} %get-tuple-element.267), channel_id=1, source_target_pairs={{0,24},{4,28},{8,16},{12,20},{16,8},{20,12},{24,0},{28,4},{1,25},{... | collective-permute-start | bytes 1572872 | tf_op jit(solution)/shard_map/ppermute | solution.py:23
  460.0 47.2 %collective-permute-start.48 = (bf16[2,2,128,512]{3,2,1,0:T(8,128)(2,1)S(1)}, bf16[2,2,128,512]{3,2,1,0:T(8,128)(2,1)}, u32[]{:S(2)}, u32[]{:S(2)}) collective-permute-start(bf16[2,2,128,512]{3,2,1,0:T(8,128)(2,1)S(1)} %get-tuple-element.268), channel_id=1, source_target_pairs={{0,16},{4,20},{8,24},{12,28},{16,0},{20,4},{24,8},{28,12},{1,17},{... | collective-permute-start | bytes 1572872 | tf_op jit(solution)/shard_map/ppermute | solution.py:23
  466.5 10.0 %collective-permute-start.47 = (bf16[2,144,512]{2,1,0:T(8,128)(2,1)S(1)}, bf16[2,144,512]{2,1,0:T(8,128)(2,1)S(1)}, u32[]{:S(2)}, u32[]{:S(2)}) collective-permute-start(bf16[2,144,512]{2,1,0:T(8,128)(2,1)S(1)} %get-tuple-element.277), channel_id=1, source_target_pairs={{0,4},{4,0},{8,12},{12,8},{16,20},{20,16},{24,28},{28,24},{1,5},{5... | collective-permute-start | bytes 884744 | tf_op jit(solution)/shard_map/ppermute | solution.py:23
  468.1 39.1 %collective-permute-start.52 = (bf16[2,144,512]{2,1,0:T(8,128)(2,1)S(1)}, bf16[2,144,512]{2,1,0:T(8,128)(2,1)S(1)}, u32[]{:S(2)}, u32[]{:S(2)}) collective-permute-start(bf16[2,144,512]{2,1,0:T(8,128)(2,1)S(1)} %get-tuple-element.278), channel_id=1, source_target_pairs={{0,4},{4,0},{8,12},{12,8},{16,20},{20,16},{24,28},{28,24},{1,5},{5... | collective-permute-start | bytes 884744 | tf_op jit(solution)/shard_map/ppermute | solution.py:23
  508.3 11.3 %collective-permute-start.53 = (bf16[144,512]{1,0:T(8,128)(2,1)S(1)}, bf16[144,512]{1,0:T(8,128)(2,1)S(1)}, u32[]{:S(2)}, u32[]{:S(2)}) collective-permute-start(bf16[144,512]{1,0:T(8,128)(2,1)S(1)} %get-tuple-element.274), channel_id=1, source_target_pairs={{0,16},{4,20},{8,24},{12,28},{16,0},{20,4},{24,8},{28,12},{1,17},{... | collective-permute-start | bytes 442376 | tf_op jit(solution)/shard_map/ppermute | solution.py:23
  508.4 11.2 %collective-permute-start.54 = (bf16[144,512]{1,0:T(8,128)(2,1)S(1)}, bf16[144,512]{1,0:T(8,128)(2,1)S(1)}, u32[]{:S(2)}, u32[]{:S(2)}) collective-permute-start(bf16[144,512]{1,0:T(8,128)(2,1)S(1)} %get-tuple-element.275), channel_id=1, source_target_pairs={{0,24},{4,28},{8,16},{12,20},{16,8},{20,12},{24,0},{28,4},{1,25},{... | collective-permute-start | bytes 442376 | tf_op jit(solution)/shard_map/ppermute | solution.py:23
  510.3 10.7 %collective-permute-start.51 = (bf16[144,512]{1,0:T(8,128)(2,1)S(1)}, bf16[144,512]{1,0:T(8,128)(2,1)S(1)}, u32[]{:S(2)}, u32[]{:S(2)}) collective-permute-start(bf16[144,512]{1,0:T(8,128)(2,1)S(1)} %get-tuple-element.276), channel_id=1, source_target_pairs={{0,8},{4,12},{8,0},{12,4},{16,24},{20,28},{24,16},{28,20},{1,9},{5... | collective-permute-start | bytes 442376 | tf_op jit(solution)/shard_map/ppermute | solution.py:23
  514.3 23.1 %collective-permute-start.57 = (bf16[1,1000,512]{2,1,0:T(8,128)(2,1)}, bf16[1,1000,512]{2,1,0:T(8,128)(2,1)}, u32[]{:S(2)}, u32[]{:S(2)}) collective-permute-start(bf16[1,1000,512]{2,1,0:T(8,128)(2,1)} %get-tuple-element.212), channel_id=1, source_target_pairs={{0,4},{4,0},{8,12},{12,8},{16,20},{20,16},{24,28},{28,24},{1,5},{5... | collective-permute-start | bytes 3072008 | tf_op jit(solution)/shard_map/ppermute | solution.py:23
  523.9 17.9 %collective-permute-start.56 = (f32[2,2,128,512]{3,2,1,0:T(8,128)S(1)}, f32[2,2,128,512]{3,2,1,0:T(8,128)S(1)}, u32[]{:S(2)}, u32[]{:S(2)}) collective-permute-start(f32[2,2,128,512]{3,2,1,0:T(8,128)S(1)} %fusion.8), channel_id=1, source_target_pairs={{0,1},{1,0},{2,3},{3,2},{4,5},{5,4},{6,7},{7,6},{8,9},{9,8},{10,11... | collective-permute-start | bytes 3145736 | tf_op jit(solution)/shard_map/ppermute | solution.py:23
  (40 other events, 383.1 us)

commit v3 on v2

--- a/solution.py
+++ b/solution.py
@@ -57,7 +57,7 @@
 
     def result(self):
         if self.count == 8:
-            return [part for g in range(4) for part in (self.far[g], self.near[g])]
+            return [part for g in range(4) for part in (self.far.get(g), self.near.get(g))]
         blocks, step = [self.block], 1
         while step < self.count:
             blocks = blocks + [swap(part, self.axis, step) for part in blocks]
@@ -69,39 +69,50 @@
     def __init__(self, axis):
         self.axis = axis
         self.count = lax.axis_size(axis)
-        self.blocks, self.near, self.far, self.kept = {}, {}, {}, None
+        self.blocks, self.fars, self.near, self.step, self.sent, self.last = {}, {}, {}, None, None, None
 
     def give(self, groups, fars, nears, split=0, mark=None):
         per_half = self.count // (2 * GROUPS)
         if self.count == 8:
-            sent = swap(after(nears, mark), self.axis, 1)
+            if isinstance(nears, (list, tuple)):
+                nears = [swap(after(near, mark), self.axis, 1) for near in nears]
+                self.near.update({g: (near, None) for g, near in zip(groups, nears)})
+            else:
+                sent = swap(after(nears, mark), self.axis, 1)
+                self.near.update({g: (sent, n) for n, g in enumerate(groups)})
+            self.fars.update(dict(zip(groups, fars)))
+            return
         for n, g in enumerate(groups):
-            if self.count == 8:
-                self.blocks[2 * g], self.near[g] = fars[n], (sent, n)
-                continue
             for half, array in enumerate((fars[n], nears[n])):
                 for k, piece in enumerate(jnp.split(array, per_half, axis=split)):
                     self.blocks[(2 * g + half) * per_half + k] = piece
 
-    def forward(self, groups, mark=None):
+    def joined(self, g, mark=None):
+        sent, n = self.near[g]
+        sent = after(sent, mark)
+        return self.fars[g].astype(F32) + (sent if n is None else sent[n]).astype(F32)
+
+    def second(self, groups=None, mark=None):
         if self.count == 8:
-            for g in groups:
-                sent, n = self.near[g]
-                part = self.blocks[2 * g].astype(F32) + after(sent, mark)[n].astype(F32)
-                if g:
-                    self.far[g] = swap(part.astype(BF16), self.axis, 2 * g)
-                else:
-                    self.kept = part
-
-    def arrived(self, far=(), near=()):
-        return [self.far[g] for g in far] + [self.near[g][0] for g in near] if self.count == 8 else None
+            parts = [self.joined(g, mark).astype(BF16) for g in groups or (1, 3)]
+            if groups:
+                self.step = {**(self.step or {}), **{g: swap(part, self.axis, 2) for g, part in zip(groups, parts)}}
+            else:
+                self.sent = sent = swap(jnp.stack(parts), self.axis, 2)
+                self.step = {1: sent[0], 3: sent[1]}
+
+    def third(self, mark=None):
+        if self.count == 8:
+            step = after(self.step[3], mark)
+            self.last = swap((self.joined(2) + step.astype(F32)).astype(BF16), self.axis, 4)
+
+    def arrived(self, near=()):
+        return [self.near[g][0] for g in near] if self.count == 8 else None
 
     def result(self, mark=None):
         if self.count == 8:
-            total = self.kept
-            for g in (1, 2, 3):
-                total = total + after(self.far[g], mark).astype(F32)
-            return total
+            last = after(self.last, mark)
+            return self.joined(0) + self.step[1].astype(F32) + last.astype(F32)
         blocks = [self.blocks[k] for k in range(self.count)]
         step = self.count // 2
         while step >= 1:
@@ -532,12 +543,26 @@
     )
 
 
+def merge_stats(left, right):
+    top = jnp.maximum(left[0:1], right[0:1])
+    total = left[1:] * jnp.exp(left[0:1] - top) + right[1:] * jnp.exp(right[0:1] - top)
+    return jnp.concatenate([top, total], axis=0)
+
+
+def stats_result(stats):
+    return stats[0:1] + jnp.log(stats[1:2]), stats[2:3] / stats[1:2]
+
+
 def second_sweep_kernel(bases, last, flags_ref, *refs):
     count = len(bases)
     words, rest = refs[: 2 * count], refs[2 * count :]
-    ht_ref, hn_ref, row_ref, target_ref, flat_ref, acc_in_refs = *rest[:5], rest[5:7]
-    fars, near_ref, outs = rest[7 : 7 + count], rest[7 + count], rest[8 + count : 10 + count]
-    acc_refs = rest[10 + count :] if last else outs
+    ht_ref, hn_ref, left_ref, right_ref, weight_ref, target_ref, flat_ref, acc_in_refs = *rest[:7], rest[7:9]
+    fars, nears, outs = rest[9 : 9 + count], rest[9 + count : 9 + 2 * count], rest[9 + 2 * count : 11 + 2 * count]
+    acc_refs = rest[11 + 2 * count :] if last else outs
+    lse, drift = stats_result(merge_stats(left_ref[...], right_ref[...]))
+    weight = weight_ref[0:1, :]
+    offset, slant = jnp.where(weight > 0, lse + 0.6931471805599453, 1e30), 2.0 - drift
+    target_weight = (1.0 - SMOOTH) * weight[:, : weight.shape[1] // 2]
     half = ht_ref.shape[1] // 2
     sources = acc_in_refs
     for n, word_ref in enumerate(words):
@@ -546,20 +571,17 @@
             rows = word_ref[start:end, :]
             z = dot(rows, ht_ref[...])
             z0, z1 = z[:, :half], z[:, half:]
-            p0 = jnp.exp(z0 - row_ref[0:1, :half])
-            p1 = jnp.exp(z1 - row_ref[0:1, half:])
+            p0 = jnp.exp(z0 - offset[:, :half])
+            p1 = jnp.exp(z1 - offset[:, half:])
             gap = z0 - z1
             spot = lax.broadcasted_iota(jnp.int32, (end - start, half), 0)
             hit = spot == target_ref[0:1, :] - (base + start)
-            picked = jnp.where(hit, row_ref[2:3, :half], 0.0)
-            g0 = p0 * (row_ref[1:2, :half] + gap) - p1 - picked
-            g1 = p1 * (row_ref[1:2, half:] - gap) - p0 - picked
+            picked = jnp.where(hit, target_weight, 0.0)
+            g0 = p0 * (slant[:, :half] + gap) - p1 - picked
+            g1 = p1 * (slant[:, half:] - gap) - p0 - picked
             dz = jnp.concatenate([g0.astype(BF16), g1.astype(BF16)], axis=1)
             grad = (dot(dz, hn_ref[...]) + flat_ref[0:1, :]).astype(BF16)
-            if n % 2:
-                near_ref[n // 2, start:end, :] = grad
-            else:
-                fars[n // 2][start:end, :] = grad
+            (nears if n % 2 else fars)[n // 2][start:end, :] = grad
             part = lax.dot_general(rows, dz, (((0,), (0,)), ((), ())), preferred_element_type=F32)
             acc_refs[0][...] = sources[0][...] + part[:, :half]
             acc_refs[1][...] = sources[1][...] + part[:, half:]
@@ -568,18 +590,18 @@
         give_parts(flags_ref, [ref[...] for ref in acc_refs], *outs)
 
 
-def second_sweep(flags, bases, words, ht, hn, row_stats, target, flat, accs, last):
+def second_sweep(flags, bases, words, ht, hn, stats, weight, target, flat, accs, last):
     count = len(bases)
     far_shape = words[0].shape
     full = (accs[0].shape, F32)
     outs = call(
         functools.partial(second_sweep_kernel, bases, last),
-        [(far_shape, BF16)] * count + [((count,) + far_shape, BF16), full, (accs[0].shape, BF16) if last else full],
-        *(*words, ht, hn, row_stats, target, flat, *accs),
+        [(far_shape, BF16)] * (2 * count) + [full, (accs[0].shape, BF16) if last else full],
+        *(*words, ht, hn, *stats, weight, target, flat, *accs),
         scalars=flags,
         scratch=[full, full] if last else [],
     )
-    return outs[:count], outs[count], outs[count + 1 :]
+    return outs[:count], outs[count : 2 * count], outs[2 * count :]
 
 
 def gelu_parts(u):
@@ -639,7 +661,7 @@
 def expert_backward_kernel(groups, flags_ref, *refs):
     blocks, rest = refs[: 2 * groups], refs[2 * groups :]
     a3_ref, an_ref, dy_ref, dn_ref, route_ref = rest[:5]
-    fars, near_ref, mine_ref, theirs_ref, acc_ref = rest[5 : 5 + groups], *rest[5 + groups :]
+    fars, nears, (mine_ref, theirs_ref, acc_ref) = rest[5 : 5 + groups], rest[5 + groups : 7 + groups], rest[7 + groups :]
     tokens = a3_ref.shape[1]
     for n, block_ref in enumerate(blocks):
         experts, hidden = block_ref.shape[1:3]
@@ -656,7 +678,7 @@
             for e in range(experts):
                 piece = grad[e * hidden : (e + 1) * hidden]
                 if n % 2:
-                    near_ref[n // 2, matrix, e] = piece
+                    nears[n // 2 % 2][n // 4, matrix, e] = piece
                 else:
                     fars[n // 2][matrix, e] = piece
         part = dot(w_in.T, du)
@@ -671,12 +693,12 @@
     half = (a3.shape[0], a3.shape[1] // 2)
     outs = call(
         functools.partial(expert_backward_kernel, groups),
-        [(shape, BF16)] * groups + [((groups,) + shape, BF16), (half, F32), (half, BF16)],
+        [(shape, BF16)] * groups + [((groups // 2,) + shape, BF16)] * 2 + [(half, F32), (half, BF16)],
         *(*blocks, a3, a3_n, dy, dy_n, route),
         scalars=flags,
         scratch=[(a3.shape, F32)],
     )
-    return outs[:groups], outs[groups], outs[groups + 1 :]
+    return outs[:groups], outs[groups : groups + 2], outs[groups + 2 :]
 
 
 def unpack_kernel(sizes, order_ref, mine_ref, twin_ref, *outs):
@@ -788,7 +810,6 @@
     norm_width = norm_gain.shape[1]
     norms = jnp.pad(jnp.concatenate([norm_gain, norm_bias], axis=0).T, ((0, 0), (0, width - 8)))
     sizes = (*sizes, norm_width)
-    order = 2 * (jnp.arange(shards) // 2 ^ here) + (jnp.arange(shards) % 2 ^ which)
 
     def core_rows(matrices):
         rows = jnp.concatenate(matrices, axis=0)
@@ -800,16 +821,6 @@
         [jnp.concatenate([self_project, self_output, cross_query, memory_project, cross_output], axis=1).T, norms]
     )
     pack_half = mine.shape[0]
-    layer_gather = Gather(jnp.stack([mine, swap(mine, "pass", 1)]), "dp")
-    layer_gather.send((1, 2, 3))
-    layer_gather.forward((0, 1, 2, 3))
-    mine = jnp.concatenate(layer_gather.result())
-    project_t, self_output_t, cross_query_t, memory_project_t, cross_output_t, norms = unpack(
-        mine, swap(mine, "vocab", 1), order, core, sizes
-    )
-    norms = norms[:, : min(width, 128)]
-    flags = jnp.stack([core, which]).astype(jnp.int32)
-
     experts = expert_in.shape[0] // 2
     hidden = expert_in.shape[2]
 
@@ -819,23 +830,48 @@
 
     expert_block = jnp.stack([core_half(expert_in), core_half(expert_out)])
     expert_gather = Gather(expert_block, "dp")
+    layer_gather = Gather(mine, "dp")
+    layer_gather.send((2, 3, 1))
+    layer_gather.forward((0,))
+    layer_gather.forward_together((1, 2, 3))
+    expert_gather.forward((0,), layer_gather.arrived(far=(1, 2, 3)))
+    parts = layer_gather.result()
+    if rows_axis == 8:
+        parts = parts[0::2] + parts[1::2]
+        mine = [jnp.stack(parts[:4]), jnp.stack(parts[4:])]
+        block_order = (0, 2, 4, 6, 1, 3, 5, 7)
+    else:
+        mine, block_order = [jnp.stack(parts)], range(rows_axis)
+    mine = jnp.concatenate([array for part in mine for array in (part, swap(part, "pass", 1))])
+    mine = after(mine, expert_gather.arrived(near=(0,)))
+    position = {}
+    for n, k in enumerate(block_order):
+        part, place = divmod(n, 4) if rows_axis == 8 else (0, n)
+        size = 4 if rows_axis == 8 else rows_axis
+        position[k] = part * 2 * size + place, part * 2 * size + size + place
+    where = jnp.array([position[k] for k in range(rows_axis)], jnp.int32)
+    order = where[jnp.arange(shards) // 2 ^ here, jnp.arange(shards) % 2 ^ which]
+    project_t, self_output_t, cross_query_t, memory_project_t, cross_output_t, norms = unpack(
+        mine, swap(mine, "vocab", 1), order, core, sizes
+    )
+    norms = norms[:, : min(width, 128)]
+    flags = jnp.stack([core, which]).astype(jnp.int32)
+
     expert_gather.send((2, 1, 3), layer_gather.mark(3))
-    expert_gather.forward((0,), project_t)
     word_gather = Gather(embedding, "dp")
+    word_gather.forward((0,), expert_gather.arrived(near=(0,)))
 
     a1, qkv_t, attended_t, self_lse, h1, a2, cross_t = self_forward(
         inputs, norms, project_t, self_output_t, cross_query_t
     )
-    cross_t = after(cross_t, expert_gather.arrived(near=(0,)))
     (memory_kv,) = call(
         memory_keys_kernel, [((memory.shape[0], 2 * width), BF16)], memory, memory_project_t
     )
     mem_bias = jnp.where(memory_mask[0][:, None] == 1, 0.0, -1e30).astype(F32)
     cross_att_t, cross_lse, h2, a3, a3_n = cross_forward(cross_t, memory_kv, mem_bias, h1, norms, cross_output_t)
-
-    expert_gather.forward_together((2, 1, 3), a3)
-    word_gather.send((2, 1, 3), (expert_gather.mark(3), a3))
-    word_gather.forward((0,), expert_gather.arrived(near=(2,)))
+    expert_gather.forward_together((2, 1, 3), (a3, word_gather.arrived(near=(0,))))
+    word_gather.send((2, 1), (expert_gather.arrived(far=(1, 2, 3)), a3))
+
     my_route = expert_ids[0, :, 0].astype(F32)[None, :]
     other_route = swap(my_route, "pass", 1)
     routes = jnp.concatenate([my_route, other_route] + [my_route] * 6, axis=0)
@@ -849,14 +885,13 @@
 
     expert_parts = halves(expert_gather.result(), 2)
     parts = ()
-    for blocks in (expert_parts[:2], expert_parts[2:]):
-        parts = expert_forward(flags, blocks, a3, route, parts, len(blocks) > 2)
+    for place in (0, 1):
+        parts = expert_forward(flags, expert_parts[place::2], a3, route, parts, place == 1)
     parts = after(parts, word_gather.arrived(far=(2, 1)))
     word_gather.forward((2, 1))
     y_part, y_other, mark = group_sum(*parts)
-    word_gather.forward((3,), y_part)
-    words = halves(word_gather.result(), 0)
-    half_words = words[0].shape[0]
+    word_gather.send((3,), word_gather.arrived(far=(2, 1)))
+    half_words = embedding.shape[0] * per_half
 
     valid = (jnp.arange(seq_len) < lengths[here]).astype(F32)
     half_weight = 0.5 * valid
@@ -874,29 +909,18 @@
     )
     sums = jnp.zeros((8, width), F32)
     for g in (0, 2, 1, 3):
+        if g == 1:
+            word_gather.forward((3,), stats)
+        words = halves(word_gather.result(), 0)
         stats, sums = first_sweep(
             2 * g * half_words, words[2 * g : 2 * g + 2], final_t, target, stats, sums
         )
     hits = stats[3, :seq_len]
 
-    def merge(left, axis):
-        right = swap(left, axis, 1)
-        top = jnp.maximum(left[0:1], right[0:1])
-        total = left[1:] * jnp.exp(left[0:1] - top) + right[1:] * jnp.exp(right[0:1] - top)
-        return jnp.concatenate([top, total], axis=0)
-
-    merged = merge(merge(stats, "vocab"), "pass")
-    lse = merged[0:1] + jnp.log(merged[1:2])
-    drift = merged[2:3] / merged[1:2]
-    row_stats = jnp.concatenate(
-        [
-            jnp.where(weight2 > 0, lse + jnp.log(2.0), 1e30),
-            2.0 - drift,
-            (1.0 - SMOOTH) * weight2,
-            jnp.zeros((5, 2 * seq_len), F32),
-        ],
-        axis=0,
-    )
+    stats = merge_stats(stats, swap(stats, "vocab", 1))
+    stats = stats, swap(stats, "pass", 1)
+    lse, drift = stats_result(merge_stats(*stats))
+    weight8 = jnp.broadcast_to(weight2, (8, 2 * seq_len))
     accs = [(-SMOOTH / VOCAB) * sums[0][:, None] * half_weight[None, :]] * 2
     word_sum = ScatterSum("dp")
     loss = (
@@ -905,46 +929,50 @@
         + jnp.sum(flat_grad[0] * sums[0])
     )
     loss = jnp.broadcast_to(loss, (8, 128))
-    first_loss = loss = loss + swap(loss, "dp", 1)
-    step = 2
-    while step < rows_axis:
+    loss_mark = loss
+    if rows_axis == 8:
+        stack = jnp.stack([loss] + [swap(loss, "dp", 2 * g) for g in (1, 2, 3)])
+        loss = sum(lax.dynamic_index_in_dim(stack, here // 2 ^ z, 0, False) for z in range(4))
+        loss_mark = loss
+        loss = loss + swap(loss, "dp", 1)
+    step = 1
+    while rows_axis != 8 and step < rows_axis:
         loss = loss + swap(loss, "dp", step)
         step *= 2
+    loss_end = loss
     for axis in ("vocab", "pass"):
         loss = loss + swap(loss, axis, 1)
     mean_loss = loss[0, 0] / jnp.sum(lengths).astype(F32)
-    for groups in ((2,), (3, 1), (0,)):
+    for groups in ((3,), (1, 2, 0)):
         fars, nears, accs = second_sweep(
             flags,
             [2 * g * half_words for g in groups],
             [words[2 * g + n] for g in groups for n in range(2)],
-            *(final_t, final_n, row_stats, target, flat_grad, accs, groups[0] == 0),
+            *(final_t, final_n, stats, weight8, target, flat_grad, accs, groups[-1] == 0),
         )
-        if groups[0]:
-            word_sum.give(groups, fars, nears, mark=first_loss if groups[0] == 2 else None)
-        if groups[0] == 3:
-            accs = (after(accs[0], loss), accs[1])
-    accs = after(accs, word_sum.arrived(near=(2,)))
-    word_sum.forward((2,))
+        if groups[-1]:
+            word_sum.give(groups, fars, nears, mark=loss_mark)
+    word_sum.give((2, 1), fars[1::-1], nears[1::-1])
+    accs = after(accs, (word_sum.arrived(near=(3,)), loss_end))
+    word_sum.second((3,))
 
     dh_part, dh_other, mark = group_sum(*accs)
     db, dy, dy_n, cols = final_back(flags, block0, block1, dh_part, dh_other, norms)
     expert_sum = ScatterSum("dp")
     last_words = fars, nears
     *expert_grads, parts = expert_backward(flags, expert_parts, a3, a3_n, dy, dy_n, route)
-    parts = after(parts, word_sum.arrived(far=(2,), near=(3, 1)))
-    word_sum.forward((3, 1))
-    expert_sum.give((0, 1, 2, 3), *expert_grads, 2)
-    word_sum.give((0,), *last_words, mark=expert_sum.arrived(near=(0,)))
+    mark = (word_sum.arrived(near=(2,)), word_sum.step)
+    word_sum.second((1,), parts)
+    for start in (1, 0):
+        expert_sum.give((start, start + 2), expert_grads[0][start::2], expert_grads[1][start], 2, mark)
     da_part, da_other, mark = group_sum(*parts)
+    word_sum.third(parts)
 
     dh1, cross_output_grad, cross_query_grad, pair_grad, cols = cross_back(
         flags,
         *(db, da_part, *da_other, h2, norms, cols, cross_output_t, cross_att_t, cross_t, memory_kv),
         *(cross_lse, mem_bias, a2, cross_query_t, h1),
     )
-    dh1 = after(dh1, expert_sum.arrived(near=(0,)))
-    expert_sum.forward((2, 3, 1, 0))
     memory_project_grad, memory_grad = call(
         memory_back_kernel,
         [((2 * width, width), BF16), (memory.shape, F32)],
@@ -953,7 +981,8 @@
     self_output_grad, self_project_grad, inputs_grad, norm_grads = self_back(
         dh1, self_output_t, attended_t, qkv_t, self_lse, a1, inputs, project_t, norms, cols
     )
-    self_project_grad = after(self_project_grad, word_sum.arrived(far=(3, 1)))
+    expert_sum.second(None, (inputs_grad, word_sum.step, word_sum.last))
+    expert_sum.third()
     evens = jnp.concatenate([jnp.arange(0, rows_axis, 2), jnp.arange(1, rows_axis, 2)])
     pack_order = 2 * ((evens if rows_axis == 8 else jnp.arange(rows_axis)) ^ here) + which
     blocks = pack(
@@ -965,12 +994,14 @@
     )
     layer_sum = ScatterSum("dp")
     if rows_axis == 8:
-        layer_sum.give((0, 1), [blocks[g] for g in range(2)], blocks[4:6])
-        layer_sum.give((2, 3), [blocks[g] for g in range(2, 4)], blocks[6:])
-        layer_sum.forward((2, 3, 1, 0), expert_sum.arrived(far=(2, 3, 1)))
-        word_sum.forward((0,), expert_sum.arrived(far=(2, 3, 1)))
+        layer_sum.give((0, 1, 2, 3), [blocks[g] for g in range(4)], blocks[4:])
+        layer_sum.second()
+        word_sum.give((0,), last_words[0][2:], last_words[1][2:], mark=layer_sum.arrived(near=(0,)))
+        layer_sum.third((expert_sum.last, word_sum.arrived(near=(0,))))
     else:
         layer_sum.blocks = {k: blocks[k] for k in range(rows_axis)}
+    if rows_axis != 8:
+        word_sum.give((0,), last_words[0][2:], last_words[1][2:])
     embedding_grad = word_sum.result()
     expert_grad = expert_sum.result()
     expert_twin = swap(expert_grad, "vocab", 1)

time: 555 us -> 486 us (0.88)
  waiting for transfers between devices: 227 us -> 163 us
  starting transfers between devices: 57.4 us -> 51.8 us
    ppermute x58 -> x57, waiting for transfers between devices: 227 us -> 163 us  [swap(): return lax.ppermute(block, axis, [(i, i ^ mask) for i in range(count)])]
    ppermute x58 -> x57, starting transfers between devices: 57.4 us -> 51.8 us  [swap(): return lax.ppermute(block, axis, [(i, i ^ mask) for i in range(count)])]
    pallas_call x18 -> x17, Pallas kernels: 186 us -> 183 us  [call(): pl.pallas_call(kernel, in_specs=specs, out_specs=[pl.BlockSpec(memory_spa...]
    unnamed x79 -> x96, local copies, waits for them, and re-layouts: 16.4 us -> 18.3 us
  transfers between devices with their start and end apart: 58 -> 57, of which waited for: 38 -> 30; matrix products, arithmetic and copies ran while one was open for 8% -> 9% of each run, Pallas kernels for 33% -> 39%
where the time goes in v3:
time: 486 us; the launch traced here: 477 us
  Pallas kernels  192 us (40%)
  waiting for transfers between devices  163 us (34%)
  starting transfers between devices  51.8 us (11%)
  local copies, waits for them, and re-layouts  36.2 us (7%)
  other arithmetic  27.6 us (6%)
  between operations  6.26 us (1%)
    pallas_call x17, Pallas kernels, call(): pl.pallas_call(kernel, in_specs=specs, out_specs=[pl.BlockSpec(memory_spa...  183 us
    ppermute x57, waiting for transfers between devices, swap(): return lax.ppermute(block, axis, [(i, i ^ mask) for i in range(count)])  163 us
    ppermute x57, starting transfers between devices, swap(): return lax.ppermute(block, axis, [(i, i ^ mask) for i in range(count)])  51.8 us
    unnamed x96, local copies, waits for them, and re-layouts  18.3 us
  transfers between devices with their start and end apart: 57, of which 30 were waited for; matrix products, arithmetic and copies ran while one was open for 9% of the time, Pallas kernels for 39%

profile of v3, /device:TPU:0, one launch (start us, length us, event | category | flops | bytes accessed | tf_op | source)
XLA Modules:
  0.0 476.9 jit_solution(17352653222133157276)
XLA Ops:
  6.2 3.0 collective-permute-start.4
  9.2 3.6 collective-permute-start.2
  15.4 2.4 collective-permute-done.2
  17.8 7.2 %collective-permute-done.1 = bf16[144,512]{1,0:T(8,128)(2,1)S(1)} collective-permute-done((bf16[144,512]{1,0:T(8,128)(2,1)S(1)}, bf16[144,512]{1,0:T(8,128)(2,1)S(1)}, u32[]{:S(2)}, u32[]{:S(2)}) %collective-permute-start.1) | collective-permute-done | bytes 147488 | tf_op jit(solution)/shard_map/ppermute | solution.py:23
  30.1 8.2 %collective-permute-done.5 = bf16[3,144,512]{2,1,0:T(8,128)(2,1)S(1)} collective-permute-done((bf16[3,144,512]{2,1,0:T(8,128)(2,1)S(1)}, bf16[3,144,512]{2,1,0:T(8,128)(2,1)S(1)}, u32[]{:S(2)}, u32[]{:S(2)}) %collective-permute-start.5) | collective-permute-done | bytes 442400 | tf_op jit(solution)/shard_map/ppermute | solution.py:23
  40.6 2.9 collective-permute-done.3
  45.9 7.8 %collective-permute-done.6 = bf16[4,144,512]{2,1,0:T(8,128)(2,1)S(1)} collective-permute-done((bf16[4,144,512]{2,1,0:T(8,128)(2,1)S(1)}, bf16[4,144,512]{2,1,0:T(8,128)(2,1)S(1)}, u32[]{:S(2)}, u32[]{:S(2)}) %collective-permute-start.6) | collective-permute-done | bytes 589856 | tf_op jit(solution)/shard_map/ppermute | solution.py:23
  57.9 2.4 collective-permute-start.9
  62.6 4.9 %shard_map.272 = (bf16[1536,512]{1,0:T(8,128)(2,1)}, bf16[512,512]{1,0:T(8,128)(2,1)}, bf16[512,512]{1,0:T(8,128)(2,1)}, bf16[1024,512]{1,0:T(8,128)(2,1)}, bf16...) custom-call(s32[17]{0:T(128)} %pad_add_fusion.1.order_ref, ...), custom_call_target="tpu_custom_call" | custom-call | flops 1000 | bytes 1000 | tf_op jit(solution)/shard_map/pallas_call | solution.py:727
  67.4 4.1 shard_map.274.kv_ref
  73.2 9.8 %shard_map.273 = (bf16[512,512]{1,0:T(8,128)(2,1)}, bf16[1536,512]{1,0:T(8,128)(2,1)}, bf16[512,512]{1,0:T(8,128)(2,1)}, f32[4,2,512]{2,1,0:T(2,128)}, f32[512,5...) custom-call(bf16[512,512]{1,0:T(8,128)(2,1)} %x_ref.3, bf16[512,128]{1,0:T(8,128)(2,1)} %slice.208.norms_ref, ...), custom_call_target="tpu_custom_call" | custom-call | flops 1000 | bytes 1000 | tf_op jit(solution)/shard_map/pallas_call | solution.py:144
  82.9 12.5 %shard_map.275 = (bf16[512,512]{1,0:T(8,128)(2,1)}, f32[4,2,512]{2,1,0:T(2,128)}, f32[512,512]{1,0:T(8,128)}, bf16[512,512]{1,0:T(8,128)(2,1)}, bf16[512,512]{1,0:T(8,128)(2,1)}) custom-call(bf16[512,512]{1,0:T(8,128)(2,1)} %get-tuple-element.125.cross_ref, bf16[1024,1024]{1,0:T(8,128)(2,1)} %shard_map.274.kv_ref, f32[1024,1]{1,0:T(8,128)} %copy.58.bias_ref, ...), custom_call_target="tpu_custom_call" | custom-call | flops 1000 | bytes 1000 | tf_op jit(solution)/shard_map/pallas_call | solution.py:144
  95.4 6.9 %collective-permute-done.9.refs_3_.refs_4_ = bf16[2,2,128,512]{3,2,1,0:T(8,128)(2,1)S(1)} collective-permute-done((bf16[2,2,128,512]{3,2,1,0:T(8,128)(2,1)S(1)}, bf16[2,2,128,512]{3,2,1,0:T(8,128)(2,1)S(1)}, u32[]{:S(2)}, u32[]{:S(2)}) %collective-permute-start.9) | collective-permute-done | bytes 524320 | tf_op jit(solution)/shard_map/ppermute | solution.py:23
  105.2 2.4 collective-permute-start.15
  112.1 5.4 %shard_map.276 = (f32[512,512]{1,0:T(8,128)}, f32[512,512]{1,0:T(8,128)}) custom-call(s32[2]{0:T(128)} %pad_add_fusion.refs_0_.flags_ref, bf16[2,2,128,512]{3,2,1,0:T(8,128)(2,1)} %copy-done.4, bf16[2,2,128,512]{3,2,1,0:T(8,128)(2,1)} %copy-done.6, bf16[2,2,128,512]{3,2,1,0:T(8,128)(2,1)} %copy-done.7, bf16[2,2,128,512]{3,2,1,0:T(8,128)(2,1)} %copy-done.5, ...), custom_call_target="tpu_custom_call" | custom-call | flops 1000 | bytes 1000 | tf_op jit(solution)/shard_map/pallas_call | solution.py:144
  117.6 22.1 %collective-permute-done.13 = bf16[3,2,2,128,512]{4,3,2,1,0:T(8,128)(2,1)} collective-permute-done((bf16[3,2,2,128,512]{4,3,2,1,0:T(8,128)(2,1)}, bf16[3,2,2,128,512]{4,3,2,1,0:T(8,128)(2,1)}, u32[]{:S(2)}, u32[]{:S(2)}) %collective-permute-start.13) | collective-permute-done | bytes 1572896 | tf_op jit(solution)/shard_map/ppermute | solution.py:23
  139.7 2.5 slice_bitcast_fusion.6
  142.2 6.4 %shard_map.277 = (f32[512,512]{1,0:T(8,128)}, bf16[512,512]{1,0:T(8,128)(2,1)}) custom-call(s32[2]{0:T(128)} %pad_add_fusion.refs_0_.flags_ref, bf16[2,2,128,512]{3,2,1,0:T(8,128)(2,1)} %copy-done.12, bf16[2,2,128,512]{3,2,1,0:T(8,128)(2,1)} %get-tuple-element.266.refs_2_.refs_3_, bf16[2,2,128,512]{3,2,1,0:T(8,128)(2,1)} %get-tuple-element.265.refs_3_.refs_5_, ...), custom_call_target="tpu_custom_call" | custom-call | flops 1000 | bytes 1000 | tf_op jit(solution)/shard_map/pallas_call | solution.py:144
  152.0 2.1 collective-permute-done.17
  159.5 10.2 %collective-permute-done.18 = bf16[512,512]{1,0:T(8,128)(2,1)S(1)} collective-permute-done((bf16[512,512]{1,0:T(8,128)(2,1)S(1)}, bf16[512,512]{1,0:T(8,128)(2,1)S(1)}, u32[]{:S(2)}, u32[]{:S(2)}) %collective-permute-start.18) | collective-permute-done | bytes 524320 | tf_op jit(solution)/shard_map/ppermute | solution.py:23
  174.5 6.4 %shard_map.278 = (f32[512,512]{1,0:T(8,128)}, f32[512,512]{1,0:T(8,128)}, bf16[512,1024]{1,0:T(8,128)(2,1)}, bf16[1024,512]{1,0:T(8,128)(2,1)}, f32[512,512]{1,0:T(8,128)}, /*index=5*/f32[8,512]{1,0:T(8,128)}) custom-call(s32[2]{0:T(128)} %pad_add_fusion.refs_0_.flags_ref, f32[512,512]{1,0:T(8,128)} %get-tuple-element.129.h2_ref, f32[512,512]{1,0:T(8,128)} %copy-done.2, ...), custom_call_target="tpu_custom_call" | custom-call | flops 1000 | bytes 1000 | tf_op jit(solution)/shard_map/pallas_call | solution.py:144
  182.1 7.8 %shard_map.279 = (f32[8,1024]{1,0:T(8,128)}, f32[8,512]{1,0:T(8,128)}) custom-call(bf16[1000,512]{1,0:T(8,128)(2,1)} %refs_4_.1, bf16[1000,512]{1,0:T(8,128)(2,1)} %copy-done.8, bf16[512,1024]{1,0:T(8,128)(2,1)} %get-tuple-element.145.refs_2_.refs_6_, s32[8,512]{1,0:T(8,128)} %broadcast_in_dim.49.refs_3_.refs_7_.refs_11_, ...), custom_call_target="tpu_custom_call" | custom-call | flops 1000 | bytes 1000 | tf_op jit(solution)/shard_map/pallas_call | solution.py:144
  190.9 7.8 %shard_map.280 = (f32[8,1024]{1,0:T(8,128)}, f32[8,512]{1,0:T(8,128)}) custom-call(bf16[1000,512]{1,0:T(8,128)(2,1)} %collective-permute-done.15.refs_0_.refs_2_, bf16[1000,512]{1,0:T(8,128)(2,1)} %copy-done.9, bf16[512,1024]{1,0:T(8,128)(2,1)} %get-tuple-element.145.refs_2_.refs_6_, s32[8,512]{1,0:T(8,128)} %broadcast_in_dim.49.refs_3_.refs_7_.refs_11_, ...), custom_call_target="tpu_custom_call" | custom-call | flops 1000 | bytes 1000 | tf_op jit(solution)/shard_map/pallas_call | solution.py:144
  199.6 7.0 %collective-permute-done.24.refs_1_ = bf16[1000,512]{1,0:T(8,128)(2,1)S(1)} collective-permute-done((bf16[1000,512]{1,0:T(8,128)(2,1)}, bf16[1000,512]{1,0:T(8,128)(2,1)S(1)}, u32[]{:S(2)}, u32[]{:S(2)}) %collective-permute-start.24) | collective-permute-done | bytes 1024032 | tf_op jit(solution)/shard_map/ppermute | solution.py:23
  207.6 7.9 %shard_map.281 = (f32[8,1024]{1,0:T(8,128)}, f32[8,512]{1,0:T(8,128)}) custom-call(bf16[1000,512]{1,0:T(8,128)(2,1)} %collective-permute-done.16.refs_0_, bf16[1000,512]{1,0:T(8,128)(2,1)} %copy-done.10, bf16[512,1024]{1,0:T(8,128)(2,1)} %get-tuple-element.145.refs_2_.refs_6_, s32[8,512]{1,0:T(8,128)} %broadcast_in_dim.49.refs_3_.refs_7_.refs_11_, ...), custom_call_target="tpu_custom_call" | custom-call | flops 1000 | bytes 1000 | tf_op jit(solution)/shard_map/pallas_call | solution.py:144
  215.6 11.6 %collective-permute-done.23.refs_1_ = bf16[1000,512]{1,0:T(8,128)(2,1)S(1)} collective-permute-done((bf16[1000,512]{1,0:T(8,128)(2,1)}, bf16[1000,512]{1,0:T(8,128)(2,1)S(1)}, u32[]{:S(2)}, u32[]{:S(2)}) %collective-permute-start.23) | collective-permute-done | bytes 1024032 | tf_op jit(solution)/shard_map/ppermute | solution.py:23
  228.1 7.8 %shard_map.282 = (f32[8,1024]{1,0:T(8,128)}, f32[8,512]{1,0:T(8,128)}) custom-call(bf16[1000,512]{1,0:T(8,128)(2,1)} %collective-permute-done.21.refs_0_, bf16[1000,512]{1,0:T(8,128)(2,1)} %copy-done.11, bf16[512,1024]{1,0:T(8,128)(2,1)} %get-tuple-element.145.refs_2_.refs_6_, s32[8,512]{1,0:T(8,128)} %broadcast_in_dim.49.refs_3_.refs_7_.refs_11_, ...), custom_call_target="tpu_custom_call" | custom-call | flops 1000 | bytes 1000 | tf_op jit(solution)/shard_map/pallas_call | solution.py:144
  245.5 2.1 collective-permute-start.29
  247.6 2.4 collective-permute-start.27
  251.7 11.8 %shard_map.283 = (bf16[1000,512]{1,0:T(8,128)(2,1)}, bf16[1000,512]{1,0:T(8,128)(2,1)}, f32[512,512]{1,0:T(8,128)}, f32[512,512]{1,0:T(8,128)}) custom-call(s32[2]{0:T(128)} %pad_add_fusion.refs_0_.flags_ref, bf16[1000,512]{1,0:T(8,128)(2,1)} %collective-permute-done.21.refs_0_, bf16[1000,512]{1,0:T(8,128)(2,1)} %copy-done.11, ...), custom_call_target="tpu_custom_call" | custom-call | flops 1000 | bytes 1000 | tf_op jit(solution)/shard_map/pallas_call | solution.py:144
  265.7 30.8 %shard_map.284 = (bf16[1000,512]{1,0:T(8,128)(2,1)}, bf16[1000,512]{1,0:T(8,128)(2,1)}, bf16[1000,512]{1,0:T(8,128)(2,1)}, bf16[1000,512]{1,0:T(8,128)(2,1)}, bf...) custom-call(s32[2]{0:T(128)} %pad_add_fusion.refs_0_.flags_ref, ...), custom_call_target="tpu_custom_call" | custom-call | flops 1000 | bytes 1000 | tf_op jit(solution)/shard_map/pallas_call | solution.py:144
  296.7 2.1 collective-permute-done.34
  303.2 11.0 %collective-permute-done.35 = bf16[512,512]{1,0:T(8,128)(2,1)S(1)} collective-permute-done((bf16[512,512]{1,0:T(8,128)(2,1)S(1)}, bf16[512,512]{1,0:T(8,128)(2,1)S(1)}, u32[]{:S(2)}, u32[]{:S(2)}) %collective-permute-start.35) | collective-permute-done | bytes 524320 | tf_op jit(solution)/shard_map/ppermute | solution.py:23
  318.0 5.9 %shard_map.285 = (f32[512,512]{1,0:T(8,128)}, bf16[512,1024]{1,0:T(8,128)(2,1)}, bf16[1024,512]{1,0:T(8,128)(2,1)}, f32[512,128]{1,0:T(8,128)}) custom-call(s32[2]{0:T(128)} %pad_add_fusion.refs_0_.flags_ref, f32[512,512]{1,0:T(8,128)} %get-tuple-element.156.b0_ref, f32[512,512]{1,0:T(8,128)} %get-tuple-element.157.b1_ref, f32[512,512]{1,0:T(8,128)} %copy-done.1, ...), custom_call_target="tpu_custom_call" | custom-call | flops 1000 | bytes 1000 | tf_op jit(solution)/shard_map/pallas_call | solution.py:144
  323.9 15.5 %shard_map.286 = (bf16[2,2,128,512]{3,2,1,0:T(8,128)(2,1)}, bf16[2,2,128,512]{3,2,1,0:T(8,128)(2,1)}, bf16[2,2,128,512]{3,2,1,0:T(8,128)(2,1)}, bf16[2,2,128,512...) custom-call(s32[2]{0:T(128)} %pad_add_fusion.refs_0_.flags_ref, ...), custom_call_target="tpu_custom_call" | custom-call | flops 1000 | bytes 1000 | tf_op jit(solution)/shard_map/pallas_call | solution.py:144
  339.7 7.7 %collective-permute-done.48 = bf16[1000,512]{1,0:T(8,128)(2,1)S(1)} collective-permute-done((bf16[1000,512]{1,0:T(8,128)(2,1)S(1)}, bf16[1000,512]{1,0:T(8,128)(2,1)S(1)}, u32[]{:S(2)}, u32[]{:S(2)}) %collective-permute-start.48) | collective-permute-done | bytes 1024032 | tf_op jit(solution)/shard_map/ppermute | solution.py:23
  348.1 2.6 collective-permute-start.50
  352.9 4.9 %collective-permute-done.39 = bf16[512,256]{1,0:T(8,128)(2,1)S(1)} collective-permute-done((bf16[512,256]{1,0:T(8,128)(2,1)S(1)}, bf16[512,256]{1,0:T(8,128)(2,1)S(1)}, u32[]{:S(2)}, u32[]{:S(2)}) %collective-permute-start.39) | collective-permute-done | bytes 262176 | tf_op jit(solution)/shard_map/ppermute | solution.py:23
  361.7 22.2 %shard_map.287 = (f32[512,512]{1,0:T(8,128)}, bf16[512,512]{1,0:T(8,128)(2,1)}, bf16[512,512]{1,0:T(8,128)(2,1)}, bf16[1024,1024]{1,0:T(8,128)(2,1)}, f32[512,128]{1,0:T(8,128)}) custom-call(s32[2]{0:T(128)} %pad_add_fusion.refs_0_.flags_ref, f32[512,512]{1,0:T(8,128)} %get-tuple-element.167.db_ref, f32[512,256]{1,0:T(8,128)} %copy-done.3, ...), custom_call_target="tpu_custom_call" | custom-call | flops 1000 | bytes 1000 | tf_op jit(solution)/shard_map/pallas_call | solution.py:144
  383.9 15.1 %shard_map.288 = (bf16[512,512]{1,0:T(8,128)(2,1)}, bf16[1536,512]{1,0:T(8,128)(2,1)}, f32[512,512]{1,0:T(8,128)}, bf16[512,512]{1,0:T(8,128)(2,1)}) custom-call(f32[512,512]{1,0:T(8,128)} %get-tuple-element.177.dh1_ref, bf16[512,512]{1,0:T(8,128)(2,1)} %get-tuple-element.123.output_ref, bf16[512,512]{1,0:T(8,128)(2,1)} %get-tuple-element.178.att_ref, ...), custom_call_target="tpu_custom_call" | custom-call | flops 1000 | bytes 1000 | tf_op jit(solution)/shard_map/pallas_call | solution.py:144
  401.1 5.9 %shard_map.289 = (bf16[1024,512]{1,0:T(8,128)(2,1)}, f32[1024,512]{1,0:T(8,128)}) custom-call(bf16[1024,1024]{1,0:T(8,128)(2,1)} %get-tuple-element.184.dkv_ref, bf16[1024,512]{1,0:T(8,128)(2,1)} %memory_ref.3, bf16[1024,512]{1,0:T(8,128)(2,1)} %get-tuple-element.126.weight_ref), custom_call_target="tpu_custom_call" | custom-call | flops 1000 | bytes 1000 | tf_op jit(solution)/shard_map/pallas_call | solution.py:144
  407.0 3.7 shard_map.290
  412.4 14.3 %collective-permute-done.42 = bf16[4,144,512]{2,1,0:T(8,128)(2,1)S(1)} collective-permute-done((bf16[4,144,512]{2,1,0:T(8,128)(2,1)S(1)}, bf16[4,144,512]{2,1,0:T(8,128)(2,1)S(1)}, u32[]{:S(2)}, u32[]{:S(2)}) %collective-permute-start.42) | collective-permute-done | bytes 589856 | tf_op jit(solution)/shard_map/ppermute | solution.py:23
  438.5 3.0 collective-permute-done.43
  441.5 8.7 %collective-permute-done.53 = bf16[1000,512]{1,0:T(8,128)(2,1)S(1)} collective-permute-done((bf16[1000,512]{1,0:T(8,128)(2,1)}, bf16[1000,512]{1,0:T(8,128)(2,1)S(1)}, u32[]{:S(2)}, u32[]{:S(2)}) %collective-permute-start.53) | collective-permute-done | bytes 1024032 | tf_op jit(solution)/shard_map/ppermute | solution.py:23
  450.2 6.3 %collective-permute-done.52 = bf16[2,2,128,512]{3,2,1,0:T(8,128)(2,1)} collective-permute-done((bf16[2,2,128,512]{3,2,1,0:T(8,128)(2,1)}, bf16[2,2,128,512]{3,2,1,0:T(8,128)(2,1)}, u32[]{:S(2)}, u32[]{:S(2)}) %collective-permute-start.52) | collective-permute-done | bytes 524320 | tf_op jit(solution)/shard_map/ppermute | solution.py:23
  459.3 5.1 %collective-permute-done.54 = bf16[144,512]{1,0:T(8,128)(2,1)S(1)} collective-permute-done((bf16[144,512]{1,0:T(8,128)(2,1)S(1)}, bf16[144,512]{1,0:T(8,128)(2,1)S(1)}, u32[]{:S(2)}, u32[]{:S(2)}) %collective-permute-start.54) | collective-permute-done | bytes 147488 | tf_op jit(solution)/shard_map/ppermute | solution.py:23
  465.6 3.1 convert_add_fusion
  (271 shorter events, 103.7 us)
Async XLA Ops:
  6.2 23.9 %collective-permute-start.4 = (bf16[144,512]{1,0:T(8,128)(2,1)S(1)}, bf16[144,512]{1,0:T(8,128)(2,1)S(1)}, u32[]{:S(2)}, u32[]{:S(2)}) collective-permute-start(bf16[144,512]{1,0:T(8,128)(2,1)S(1)} %get-tuple-element.257), channel_id=1, source_target_pairs={{0,4},{4,0},{8,12},{12,8},{16,20},{20,16},{24,28},{28,24},{1,5},{5... | collective-permute-start | bytes 442376 | tf_op jit(solution)/shard_map/ppermute | solution.py:23
  9.2 8.6 %collective-permute-start.2 = (bf16[144,512]{1,0:T(8,128)(2,1)S(1)}, bf16[144,512]{1,0:T(8,128)(2,1)S(1)}, u32[]{:S(2)}, u32[]{:S(2)}) collective-permute-start(bf16[144,512]{1,0:T(8,128)(2,1)S(1)} %get-tuple-element.257), channel_id=1, source_target_pairs={{0,24},{4,28},{8,16},{12,20},{16,8},{20,12},{24,0},{28,4},{1,25},{... | collective-permute-start | bytes 442376 | tf_op jit(solution)/shard_map/ppermute | solution.py:23
  12.8 12.2 %collective-permute-start.1 = (bf16[144,512]{1,0:T(8,128)(2,1)S(1)}, bf16[144,512]{1,0:T(8,128)(2,1)S(1)}, u32[]{:S(2)}, u32[]{:S(2)}) collective-permute-start(bf16[144,512]{1,0:T(8,128)(2,1)S(1)} %get-tuple-element.257), channel_id=1, source_target_pairs={{0,16},{4,20},{8,24},{12,28},{16,0},{20,4},{24,8},{28,12},{1,17},{... | collective-permute-start | bytes 442376 | tf_op jit(solution)/shard_map/ppermute | solution.py:23
  12.8 12.2 %collective-permute-start = (bf16[144,512]{1,0:T(8,128)(2,1)S(1)}, bf16[144,512]{1,0:T(8,128)(2,1)S(1)}, u32[]{:S(2)}, u32[]{:S(2)}) collective-permute-start(bf16[144,512]{1,0:T(8,128)(2,1)S(1)} %get-tuple-element.257), channel_id=1, source_target_pairs={{0,8},{4,12},{8,0},{12,4},{16,24},{20,28},{24,16},{28,20},{1,9},{5... | collective-permute-start | bytes 442376 | tf_op jit(solution)/shard_map/ppermute | solution.py:23
  25.1 13.2 %collective-permute-start.5 = (bf16[3,144,512]{2,1,0:T(8,128)(2,1)S(1)}, bf16[3,144,512]{2,1,0:T(8,128)(2,1)S(1)}, u32[]{:S(2)}, u32[]{:S(2)}) collective-permute-start(bf16[3,144,512]{2,1,0:T(8,128)(2,1)S(1)} %pad_maximum_fusion.5), channel_id=1, source_target_pairs={{0,4},{4,0},{8,12},{12,8},{16,20},{20,16},{24,28},{28,24},{1,5},{5... | collective-permute-start | bytes 1327112 | tf_op jit(solution)/shard_map/ppermute | solution.py:23
  25.7 28.8 %collective-permute-start.7 = (bf16[2,2,128,512]{3,2,1,0:T(8,128)(2,1)S(1)}, bf16[2,2,128,512]{3,2,1,0:T(8,128)(2,1)S(1)}, u32[]{:S(2)}, u32[]{:S(2)}) collective-permute-start(bf16[2,2,128,512]{3,2,1,0:T(8,128)(2,1)S(1)} %pad_maximum_fusion.4.refs_1_.refs_0_), channel_id=1, source_target_pairs={{0,4},{4,0},{8,12},{12,8},{16,20},{20,16},{24,28},{28,24},{1,5},{5... | collective-permute-start | bytes 1572872 | tf_op jit(solution)/shard_map/ppermute | solution.py:23
  27.2 16.3 %collective-permute-start.3 = (bf16[4,144,512]{2,1,0:T(8,128)(2,1)S(1)}, bf16[4,144,512]{2,1,0:T(8,128)(2,1)S(1)}, u32[]{:S(2)}, u32[]{:S(2)}) collective-permute-start(bf16[4,144,512]{2,1,0:T(8,128)(2,1)S(1)} %pad_maximum_fusion.2), channel_id=1, source_target_pairs={{0,2},{2,0},{1,3},{3,1},{4,6},{6,4},{5,7},{7,5},{8,10},{10,8},{9,1... | collective-permute-start | bytes 1769480 | tf_op jit(solution)/shard_map/ppermute | solution.py:23
  38.4 15.3 %collective-permute-start.6 = (bf16[4,144,512]{2,1,0:T(8,128)(2,1)S(1)}, bf16[4,144,512]{2,1,0:T(8,128)(2,1)S(1)}, u32[]{:S(2)}, u32[]{:S(2)}) collective-permute-start(bf16[4,144,512]{2,1,0:T(8,128)(2,1)S(1)} %pad_maximum_fusion.3), channel_id=1, source_target_pairs={{0,2},{2,0},{1,3},{3,1},{4,6},{6,4},{5,7},{7,5},{8,10},{10,8},{9,1... | collective-permute-start | bytes 1769480 | tf_op jit(solution)/shard_map/ppermute | solution.py:23
  55.3 7.2 %collective-permute-start.8 = (bf16[16,144,512]{2,1,0:T(8,128)(2,1)}, bf16[16,144,512]{2,1,0:T(8,128)(2,1)}, u32[]{:S(2)}, u32[]{:S(2)}) collective-permute-start(bf16[16,144,512]{2,1,0:T(8,128)(2,1)} %constant_dynamic-update-slice_fusion.5.mine_ref), channel_id=1, source_target_pairs={{0,1},{1,0},{2,3},{3,2},{4,5},{5,4},{6,7},{7,6},{8,9},{9,8},{10,11... | collective-permute-start | bytes 7077896 | tf_op jit(solution)/shard_map/ppermute | solution.py:23
  55.4 40.0 %collective-permute-start.10 = (bf16[1000,512]{1,0:T(8,128)(2,1)}, bf16[1000,512]{1,0:T(8,128)(2,1)S(1)}, u32[]{:S(2)}, u32[]{:S(2)}) collective-permute-start(bf16[1000,512]{1,0:T(8,128)(2,1)} %refs_4_.1), channel_id=1, source_target_pairs={{0,4},{4,0},{8,12},{12,8},{16,20},{20,16},{24,28},{28,24},{1,5},{5... | collective-permute-start | bytes 3072008 | tf_op jit(solution)/shard_map/ppermute | solution.py:23
  55.9 39.5 %collective-permute-start.12 = (bf16[2,2,128,512]{3,2,1,0:T(8,128)(2,1)S(1)}, bf16[2,2,128,512]{3,2,1,0:T(8,128)(2,1)S(1)}, u32[]{:S(2)}, u32[]{:S(2)}) collective-permute-start(bf16[2,2,128,512]{3,2,1,0:T(8,128)(2,1)S(1)} %pad_maximum_fusion.4.refs_1_.refs_0_), channel_id=1, source_target_pairs={{0,24},{4,28},{8,16},{12,20},{16,8},{20,12},{24,0},{28,4},{1,25},{... | collective-permute-start | bytes 1572872 | tf_op jit(solution)/shard_map/ppermute | solution.py:23
  57.9 37.5 %collective-permute-start.11 = (bf16[2,2,128,512]{3,2,1,0:T(8,128)(2,1)S(1)}, bf16[2,2,128,512]{3,2,1,0:T(8,128)(2,1)S(1)}, u32[]{:S(2)}, u32[]{:S(2)}) collective-permute-start(bf16[2,2,128,512]{3,2,1,0:T(8,128)(2,1)S(1)} %pad_maximum_fusion.4.refs_1_.refs_0_), channel_id=1, source_target_pairs={{0,8},{4,12},{8,0},{12,4},{16,24},{20,28},{24,16},{28,20},{1,9},{5... | collective-permute-start | bytes 1572872 | tf_op jit(solution)/shard_map/ppermute | solution.py:23
  57.9 44.4 %collective-permute-start.9 = (bf16[2,2,128,512]{3,2,1,0:T(8,128)(2,1)S(1)}, bf16[2,2,128,512]{3,2,1,0:T(8,128)(2,1)S(1)}, u32[]{:S(2)}, u32[]{:S(2)}) collective-permute-start(bf16[2,2,128,512]{3,2,1,0:T(8,128)(2,1)S(1)} %pad_maximum_fusion.4.refs_1_.refs_0_), channel_id=1, source_target_pairs={{0,16},{4,20},{8,24},{12,28},{16,0},{20,4},{24,8},{28,12},{1,17},{... | collective-permute-start | bytes 1572872 | tf_op jit(solution)/shard_map/ppermute | solution.py:23
  103.6 36.0 %collective-permute-start.13 = (bf16[3,2,2,128,512]{4,3,2,1,0:T(8,128)(2,1)}, bf16[3,2,2,128,512]{4,3,2,1,0:T(8,128)(2,1)}, u32[]{:S(2)}, u32[]{:S(2)}) collective-permute-start(bf16[3,2,2,128,512]{4,3,2,1,0:T(8,128)(2,1)} %pad_maximum_fusion), channel_id=1, source_target_pairs={{0,4},{4,0},{8,12},{12,8},{16,20},{20,16},{24,28},{28,24},{1,5},{5... | collective-permute-start | bytes 4718600 | tf_op jit(solution)/shard_map/ppermute | solution.py:23
  105.2 45.1 %collective-permute-start.16 = (bf16[1000,512]{1,0:T(8,128)(2,1)}, bf16[1000,512]{1,0:T(8,128)(2,1)}, u32[]{:S(2)}, u32[]{:S(2)}) collective-permute-start(bf16[1000,512]{1,0:T(8,128)(2,1)} %refs_4_.1), channel_id=1, source_target_pairs={{0,8},{4,12},{8,0},{12,4},{16,24},{20,28},{24,16},{28,20},{1,9},{5... | collective-permute-start | bytes 3072008 | tf_op jit(solution)/shard_map/ppermute | solution.py:23
  105.2 46.9 %collective-permute-start.15 = (bf16[1000,512]{1,0:T(8,128)(2,1)}, bf16[1000,512]{1,0:T(8,128)(2,1)}, u32[]{:S(2)}, u32[]{:S(2)}) collective-permute-start(bf16[1000,512]{1,0:T(8,128)(2,1)} %refs_4_.1), channel_id=1, source_target_pairs={{0,16},{4,20},{8,24},{12,28},{16,0},{20,4},{24,8},{28,12},{1,17},{... | collective-permute-start | bytes 3072008 | tf_op jit(solution)/shard_map/ppermute | solution.py:23
  107.6 3.6 collective-permute-start.14
  155.6 14.0 %collective-permute-start.18 = (bf16[512,512]{1,0:T(8,128)(2,1)S(1)}, bf16[512,512]{1,0:T(8,128)(2,1)S(1)}, u32[]{:S(2)}, u32[]{:S(2)}) collective-permute-start(bf16[512,512]{1,0:T(8,128)(2,1)S(1)} %add_convert_fusion.4), channel_id=1, source_target_pairs={{0,2},{2,0},{1,3},{3,1},{4,6},{6,4},{5,7},{7,5},{8,10},{10,8},{9,1... | collective-permute-start | bytes 1572872 | tf_op jit(solution)/shard_map/ppermute | solution.py:23
  157.1 41.5 %collective-permute-start.21 = (bf16[1000,512]{1,0:T(8,128)(2,1)}, bf16[1000,512]{1,0:T(8,128)(2,1)}, u32[]{:S(2)}, u32[]{:S(2)}) collective-permute-start(bf16[1000,512]{1,0:T(8,128)(2,1)} %refs_4_.1), channel_id=1, source_target_pairs={{0,24},{4,28},{8,16},{12,20},{16,8},{20,12},{24,0},{28,4},{1,25},{... | collective-permute-start | bytes 3072008 | tf_op jit(solution)/shard_map/ppermute | solution.py:23
  158.9 31.0 %collective-permute-start.22 = (bf16[1000,512]{1,0:T(8,128)(2,1)}, bf16[1000,512]{1,0:T(8,128)(2,1)S(1)}, u32[]{:S(2)}, u32[]{:S(2)}) collective-permute-start(bf16[1000,512]{1,0:T(8,128)(2,1)} %collective-permute-done.15.refs_0_.refs_2_), channel_id=1, source_target_pairs={{0,4},{4,0},{8,12},{12,8},{16,20},{20,16},{24,28},{28,24},{1,5},{5... | collective-permute-start | bytes 3072008 | tf_op jit(solution)/shard_map/ppermute | solution.py:23
  172.8 33.9 %collective-permute-start.24 = (bf16[1000,512]{1,0:T(8,128)(2,1)}, bf16[1000,512]{1,0:T(8,128)(2,1)S(1)}, u32[]{:S(2)}, u32[]{:S(2)}) collective-permute-start(bf16[1000,512]{1,0:T(8,128)(2,1)} %collective-permute-done.16.refs_0_), channel_id=1, source_target_pairs={{0,4},{4,0},{8,12},{12,8},{16,20},{20,16},{24,28},{28,24},{1,5},{5... | collective-permute-start | bytes 3072008 | tf_op jit(solution)/shard_map/ppermute | solution.py:23
  198.6 28.5 %collective-permute-start.23 = (bf16[1000,512]{1,0:T(8,128)(2,1)}, bf16[1000,512]{1,0:T(8,128)(2,1)S(1)}, u32[]{:S(2)}, u32[]{:S(2)}) collective-permute-start(bf16[1000,512]{1,0:T(8,128)(2,1)} %collective-permute-done.21.refs_0_), channel_id=1, source_target_pairs={{0,4},{4,0},{8,12},{12,8},{16,20},{20,16},{24,28},{28,24},{1,5},{5... | collective-permute-start | bytes 3072008 | tf_op jit(solution)/shard_map/ppermute | solution.py:23
  239.6 4.0 collective-permute-start.26
  245.5 18.0 %collective-permute-start.29 = (f32[8,128]{1,0:T(8,128)S(1)}, f32[8,128]{1,0:T(8,128)S(1)}, u32[]{:S(2)}, u32[]{:S(2)}) collective-permute-start(f32[8,128]{1,0:T(8,128)S(1)} %broadcast_in_dim.51), channel_id=1, source_target_pairs={{0,24},{4,28},{8,16},{12,20},{16,8},{20,12},{24,0},{28,4},{1,25},{... | collective-permute-start | bytes 12296 | tf_op jit(solution)/shard_map/ppermute | solution.py:23
  247.6 16.0 %collective-permute-start.28 = (f32[8,128]{1,0:T(8,128)S(1)}, f32[8,128]{1,0:T(8,128)S(1)}, u32[]{:S(2)}, u32[]{:S(2)}) collective-permute-start(f32[8,128]{1,0:T(8,128)S(1)} %broadcast_in_dim.51), channel_id=1, source_target_pairs={{0,16},{4,20},{8,24},{12,28},{16,0},{20,4},{24,8},{28,12},{1,17},{... | collective-permute-start | bytes 12296 | tf_op jit(solution)/shard_map/ppermute | solution.py:23
  247.6 16.0 %collective-permute-start.27 = (f32[8,128]{1,0:T(8,128)S(1)}, f32[8,128]{1,0:T(8,128)S(1)}, u32[]{:S(2)}, u32[]{:S(2)}) collective-permute-start(f32[8,128]{1,0:T(8,128)S(1)} %broadcast_in_dim.51), channel_id=1, source_target_pairs={{0,8},{4,12},{8,0},{12,4},{16,24},{20,28},{24,16},{28,20},{1,9},{5... | collective-permute-start | bytes 12296 | tf_op jit(solution)/shard_map/ppermute | solution.py:23
  263.7 32.9 %collective-permute-start.33 = (bf16[1000,512]{1,0:T(8,128)(2,1)}, bf16[1000,512]{1,0:T(8,128)(2,1)S(1)}, u32[]{:S(2)}, u32[]{:S(2)}) collective-permute-start(bf16[1000,512]{1,0:T(8,128)(2,1)} %get-tuple-element.164), channel_id=1, source_target_pairs={{0,4},{4,0},{8,12},{12,8},{16,20},{20,16},{24,28},{28,24},{1,5},{5... | collective-permute-start | bytes 3072008 | tf_op jit(solution)/shard_map/ppermute | solution.py:23
  264.2 32.3 %collective-permute-start.30 = (f32[8,128]{1,0:T(8,128)S(1)}, f32[8,128]{1,0:T(8,128)S(1)}, u32[]{:S(2)}, u32[]{:S(2)}) collective-permute-start(f32[8,128]{1,0:T(8,128)S(1)} %add_bitcast_fusion), channel_id=1, source_target_pairs={{0,4},{4,0},{8,12},{12,8},{16,20},{20,16},{24,28},{28,24},{1,5},{5... | collective-permute-start | bytes 12296 | tf_op jit(solution)/shard_map/ppermute | solution.py:23
  300.2 14.0 %collective-permute-start.35 = (bf16[512,512]{1,0:T(8,128)(2,1)S(1)}, bf16[512,512]{1,0:T(8,128)(2,1)S(1)}, u32[]{:S(2)}, u32[]{:S(2)}) collective-permute-start(bf16[512,512]{1,0:T(8,128)(2,1)S(1)} %add_convert_fusion.3), channel_id=1, source_target_pairs={{0,2},{2,0},{1,3},{3,1},{4,6},{6,4},{5,7},{7,5},{8,10},{10,8},{9,1... | collective-permute-start | bytes 1572872 | tf_op jit(solution)/shard_map/ppermute | solution.py:23
  300.8 38.7 %collective-permute-start.44 = (bf16[1000,512]{1,0:T(8,128)(2,1)}, bf16[1000,512]{1,0:T(8,128)(2,1)S(1)}, u32[]{:S(2)}, u32[]{:S(2)}) collective-permute-start(bf16[1000,512]{1,0:T(8,128)(2,1)} %get-tuple-element.194), channel_id=1, source_target_pairs={{0,4},{4,0},{8,12},{12,8},{16,20},{20,16},{24,28},{28,24},{1,5},{5... | collective-permute-start | bytes 3072008 | tf_op jit(solution)/shard_map/ppermute | solution.py:23
  301.3 46.0 %collective-permute-start.48 = (bf16[1000,512]{1,0:T(8,128)(2,1)S(1)}, bf16[1000,512]{1,0:T(8,128)(2,1)S(1)}, u32[]{:S(2)}, u32[]{:S(2)}) collective-permute-start(bf16[1000,512]{1,0:T(8,128)(2,1)S(1)} %copy-done.37), channel_id=1, source_target_pairs={{0,4},{4,0},{8,12},{12,8},{16,20},{20,16},{24,28},{28,24},{1,5},{5... | collective-permute-start | bytes 3072008 | tf_op jit(solution)/shard_map/ppermute | solution.py:23
  303.1 36.4 %collective-permute-start.45 = (bf16[1000,512]{1,0:T(8,128)(2,1)S(1)}, bf16[1000,512]{1,0:T(8,128)(2,1)S(1)}, u32[]{:S(2)}, u32[]{:S(2)}) collective-permute-start(bf16[1000,512]{1,0:T(8,128)(2,1)S(1)} %add_convert_fusion.2), channel_id=1, source_target_pairs={{0,8},{4,12},{8,0},{12,4},{16,24},{20,28},{24,16},{28,20},{1,9},{5... | collective-permute-start | bytes 3072008 | tf_op jit(solution)/shard_map/ppermute | solution.py:23
  339.5 11.8 %collective-permute-start.38 = (bf16[512,256]{1,0:T(8,128)(2,1)}, bf16[512,256]{1,0:T(8,128)(2,1)S(1)}, u32[]{:S(2)}, u32[]{:S(2)}) collective-permute-start(bf16[512,256]{1,0:T(8,128)(2,1)} %get-tuple-element.172), channel_id=1, source_target_pairs={{0,1},{1,0},{2,3},{3,2},{4,5},{5,4},{6,7},{7,6},{8,9},{9,8},{10,11... | collective-permute-start | bytes 786440 | tf_op jit(solution)/shard_map/ppermute | solution.py:23
  347.6 51.4 %collective-permute-start.49 = (bf16[1000,512]{1,0:T(8,128)(2,1)S(1)}, bf16[1000,512]{1,0:T(8,128)(2,1)S(1)}, u32[]{:S(2)}, u32[]{:S(2)}) collective-permute-start(bf16[1000,512]{1,0:T(8,128)(2,1)S(1)} %add_convert_fusion.1), channel_id=1, source_target_pairs={{0,8},{4,12},{8,0},{12,4},{16,24},{20,28},{24,16},{28,20},{1,9},{5... | collective-permute-start | bytes 3072008 | tf_op jit(solution)/shard_map/ppermute | solution.py:23
  348.1 50.9 %collective-permute-start.50 = (bf16[1000,512]{1,0:T(8,128)(2,1)S(1)}, bf16[1000,512]{1,0:T(8,128)(2,1)S(1)}, u32[]{:S(2)}, u32[]{:S(2)}) collective-permute-start(bf16[1000,512]{1,0:T(8,128)(2,1)S(1)} %add_convert_fusion), channel_id=1, source_target_pairs={{0,16},{4,20},{8,24},{12,28},{16,0},{20,4},{24,8},{28,12},{1,17},{... | collective-permute-start | bytes 3072008 | tf_op jit(solution)/shard_map/ppermute | solution.py:23
  350.7 48.3 %collective-permute-start.47 = (bf16[2,2,2,128,512]{4,3,2,1,0:T(8,128)(2,1)}, bf16[2,2,2,128,512]{4,3,2,1,0:T(8,128)(2,1)S(1)}, u32[]{:S(2)}, u32[]{:S(2)}) collective-permute-start(bf16[2,2,2,128,512]{4,3,2,1,0:T(8,128)(2,1)} %get-tuple-element.199), channel_id=1, source_target_pairs={{0,4},{4,0},{8,12},{12,8},{16,20},{20,16},{24,28},{28,24},{1,5},{5... | collective-permute-start | bytes 3145736 | tf_op jit(solution)/shard_map/ppermute | solution.py:23
  351.3 6.4 %collective-permute-start.39 = (bf16[512,256]{1,0:T(8,128)(2,1)S(1)}, bf16[512,256]{1,0:T(8,128)(2,1)S(1)}, u32[]{:S(2)}, u32[]{:S(2)}) collective-permute-start(bf16[512,256]{1,0:T(8,128)(2,1)S(1)} %add_convert_fusion.5), channel_id=1, source_target_pairs={{0,2},{2,0},{1,3},{3,1},{4,6},{6,4},{5,7},{7,5},{8,10},{10,8},{9,1... | collective-permute-start | bytes 786440 | tf_op jit(solution)/shard_map/ppermute | solution.py:23
  357.9 3.0 collective-permute-start.40
  359.5 71.4 %collective-permute-start.46 = (bf16[2,2,2,128,512]{4,3,2,1,0:T(8,128)(2,1)}, bf16[2,2,2,128,512]{4,3,2,1,0:T(8,128)(2,1)S(1)}, u32[]{:S(2)}, u32[]{:S(2)}) collective-permute-start(bf16[2,2,2,128,512]{4,3,2,1,0:T(8,128)(2,1)} %get-tuple-element.196), channel_id=1, source_target_pairs={{0,4},{4,0},{8,12},{12,8},{16,20},{20,16},{24,28},{28,24},{1,5},{5... | collective-permute-start | bytes 3145736 | tf_op jit(solution)/shard_map/ppermute | solution.py:23
  400.3 30.6 %collective-permute-start.51 = (bf16[2,2,2,128,512]{4,3,2,1,0:T(8,128)(2,1)S(1)}, bf16[2,2,2,128,512]{4,3,2,1,0:T(8,128)(2,1)S(1)}, u32[]{:S(2)}, u32[]{:S(2)}) collective-permute-start(bf16[2,2,2,128,512]{4,3,2,1,0:T(8,128)(2,1)S(1)} %pad_maximum_fusion.1), channel_id=1, source_target_pairs={{0,8},{4,12},{8,0},{12,4},{16,24},{20,28},{24,16},{28,20},{1,9},{5... | collective-permute-start | bytes 3145736 | tf_op jit(solution)/shard_map/ppermute | solution.py:23
  411.8 14.9 %collective-permute-start.42 = (bf16[4,144,512]{2,1,0:T(8,128)(2,1)S(1)}, bf16[4,144,512]{2,1,0:T(8,128)(2,1)S(1)}, u32[]{:S(2)}, u32[]{:S(2)}) collective-permute-start(bf16[4,144,512]{2,1,0:T(8,128)(2,1)S(1)} %slice.275), channel_id=1, source_target_pairs={{0,4},{4,0},{8,12},{12,8},{16,20},{20,16},{24,28},{28,24},{1,5},{5... | collective-permute-start | bytes 1769480 | tf_op jit(solution)/shard_map/ppermute | solution.py:23
  426.7 23.4 %collective-permute-start.53 = (bf16[1000,512]{1,0:T(8,128)(2,1)}, bf16[1000,512]{1,0:T(8,128)(2,1)S(1)}, u32[]{:S(2)}, u32[]{:S(2)}) collective-permute-start(bf16[1000,512]{1,0:T(8,128)(2,1)} %get-tuple-element.208), channel_id=1, source_target_pairs={{0,4},{4,0},{8,12},{12,8},{16,20},{20,16},{24,28},{28,24},{1,5},{5... | collective-permute-start | bytes 3072008 | tf_op jit(solution)/shard_map/ppermute | solution.py:23
  429.2 12.3 %collective-permute-start.43 = (bf16[2,144,512]{2,1,0:T(8,128)(2,1)}, bf16[2,144,512]{2,1,0:T(8,128)(2,1)S(1)}, u32[]{:S(2)}, u32[]{:S(2)}) collective-permute-start(bf16[2,144,512]{2,1,0:T(8,128)(2,1)} %pad_maximum_fusion.6), channel_id=1, source_target_pairs={{0,8},{4,12},{8,0},{12,4},{16,24},{20,28},{24,16},{28,20},{1,9},{5... | collective-permute-start | bytes 884744 | tf_op jit(solution)/shard_map/ppermute | solution.py:23
  431.9 24.6 %collective-permute-start.52 = (bf16[2,2,128,512]{3,2,1,0:T(8,128)(2,1)}, bf16[2,2,128,512]{3,2,1,0:T(8,128)(2,1)}, u32[]{:S(2)}, u32[]{:S(2)}) collective-permute-start(bf16[2,2,128,512]{3,2,1,0:T(8,128)(2,1)} %fusion.1), channel_id=1, source_target_pairs={{0,16},{4,20},{8,24},{12,28},{16,0},{20,4},{24,8},{28,12},{1,17},{... | collective-permute-start | bytes 1572872 | tf_op jit(solution)/shard_map/ppermute | solution.py:23
  433.7 3.6 collective-permute-start.32
  457.6 6.8 %collective-permute-start.54 = (bf16[144,512]{1,0:T(8,128)(2,1)S(1)}, bf16[144,512]{1,0:T(8,128)(2,1)S(1)}, u32[]{:S(2)}, u32[]{:S(2)}) collective-permute-start(bf16[144,512]{1,0:T(8,128)(2,1)S(1)} %fusion.6), channel_id=1, source_target_pairs={{0,16},{4,20},{8,24},{12,28},{16,0},{20,4},{24,8},{28,12},{1,17},{... | collective-permute-start | bytes 442376 | tf_op jit(solution)/shard_map/ppermute | solution.py:23
  459.3 12.9 %collective-permute-start.56 = (f32[2,2,128,512]{3,2,1,0:T(8,128)S(1)}, f32[2,2,128,512]{3,2,1,0:T(8,128)S(1)}, u32[]{:S(2)}, u32[]{:S(2)}) collective-permute-start(f32[2,2,128,512]{3,2,1,0:T(8,128)S(1)} %fusion), channel_id=1, source_target_pairs={{0,1},{1,0},{2,3},{3,2},{4,5},{5,4},{6,7},{7,6},{8,9},{9,8},{10,11... | collective-permute-start | bytes 3145736 | tf_op jit(solution)/shard_map/ppermute | solution.py:23
  465.5 3.2 collective-permute-start.55
  (48 other events, 402.5 us)
